TPU v7x, 32 devices: a whole 2x2x4 slice. The times are simulated.
32 devices in a mesh: pipe: 4 (over y, core), dp: 8 (over z, x).
Axes of the slice: x: 2, y: 2, z: 4, core: 2. Of those that a mesh axis runs over, the one named last changes fastest.
Arguments:
- inputs: bfloat16 [2560, 960], P('dp', 'pipe'), may hold values from -6 to 6
- cotangent: bfloat16 [2560, 960], P('dp', 'pipe'), may hold values from -6 to 6
- lengths: int32 [8, 4], P('dp'), may hold values from 16 to 128, as said below
- w_query: bfloat16 [4, 960, 960], P('pipe'), may hold values from -0.1875 to 0.1875
- w_key: bfloat16 [4, 960, 320], P('pipe'), may hold values from -0.1875 to 0.1875
- w_value: bfloat16 [4, 960, 320], P('pipe'), may hold values from -0.1875 to 0.1875
- w_proj: bfloat16 [4, 960, 960], P('pipe'), may hold values from -0.75 to 0.75
- w_gate: bfloat16 [4, 960, 2560], P('pipe'), may hold values from -0.1875 to 0.1875
- w_up: bfloat16 [4, 960, 2560], P('pipe'), may hold values from -0.1875 to 0.1875
- w_down: bfloat16 [4, 2560, 960], P('pipe'), may hold values from -0.125 to 0.125
- gain_attn: float32 [4, 960], P('pipe'), may hold values from 0.1 to 1.9
- gain_mlp: float32 [4, 960], P('pipe'), may hold values from 0.1 to 1.9
Outputs:
- layer_output: float32 [2560, 960], P('dp', 'pipe')
- grad_input: float32 [2560, 960], P('dp', 'pipe')
- grad_query: float32 [4, 960, 960], P('pipe', 'dp')
- grad_key: float32 [4, 960, 320], P('pipe', 'dp')
- grad_value: float32 [4, 960, 320], P('pipe', 'dp')
- grad_proj: float32 [4, 960, 960], P('pipe', 'dp')
- grad_gate: float32 [4, 960, 2560], P('pipe', 'dp')
- grad_up: float32 [4, 960, 2560], P('pipe', 'dp')
- grad_down: float32 [4, 2560, 960], P('pipe', 'dp')
- grad_gain_attn: float32 [4, 960], P('pipe', 'dp')
- grad_gain_mlp: float32 [4, 960], P('pipe', 'dp')
Inputs may be any that keep to these rules, and one draw needn't show every extreme that they name: lengths[g, m] is between a quarter of micro-batch m's slots and all of them (128 slots for m = 0, 64 for the others); in each data group one micro-batch, drawn from the seed, is full; in some data group the first micro-batch is full, and in some other data group a later micro-batch holds exactly a quarter of its slots.
All inputs are finite; a program needn't handle non-finite values.
Results may differ from a plain program's by a relative error of at most 0.035.
Values may be sent and summed in bfloat16 or wider, within the bound.
No kernel may reach another device: no remote copies, remote signals or barrier semaphores. Data moves between devices by JAX's collectives and lax.ppermute only.
A program may use at most 256 MiB of HBM per device.

v0:
```python
import jax
import jax.numpy as jnp
from jax import lax
from jax.sharding import PartitionSpec as P

HEAD_DIM = 64
MICRO = 4


epsilon = 1e-05
rope_base = 10000.0
masked_score = -1e30


def from_behind(block, axis, distance):
    devices = range(lax.axis_size(axis))
    route = [(i - distance, i) for i in devices if i - distance in devices]
    return lax.ppermute(block, axis, route)


def broadcast(value, axis, source):
    kept = jnp.where(lax.axis_index(axis) == source, value, 0).astype(value.dtype)
    return lax.psum(kept, axis)


def rms_normalize(hidden, gain_vector):
    return (
        hidden
        * lax.rsqrt(jnp.mean(hidden * hidden, axis=-1, keepdims=True) + epsilon)
        * gain_vector
    )


def rope_tables(row_count, head_dim):
    half_dim = head_dim // 2
    positions = jnp.arange(row_count, dtype=jnp.float32)[:, None]
    frequency = rope_base ** (-jnp.arange(half_dim, dtype=jnp.float32) / half_dim)
    angles = positions * frequency[None, :]
    return (jnp.cos(angles)[:, None, :], jnp.sin(angles)[:, None, :])


def rotate(tensor, cosine_table, sine_table):
    half_dim = tensor.shape[-1] // 2
    first_half = tensor[..., :half_dim]
    second_half = tensor[..., half_dim:]
    return jnp.concatenate(
        [
            first_half * cosine_table - second_half * sine_table,
            second_half * cosine_table + first_half * sine_table,
        ],
        axis=-1,
    )


def times_transposed(left_rows, right_rows):
    return lax.dot_general(
        left_rows, right_rows, (((1,), (1,)), ((), ())), preferred_element_type=jnp.float32
    )


def rows_product(left_rows, right_rows):
    return lax.dot_general(
        left_rows, right_rows, (((0,), (0,)), ((), ())), preferred_element_type=jnp.float32
    )


def attention_probs(query_rot, key_rot, length):
    row_count, head_count, head_dim = query_rot.shape
    kv_heads = key_rot.shape[1]
    grouped = query_rot.reshape(row_count, kv_heads, head_count // kv_heads, head_dim)
    scores = jnp.einsum(
        "qkgd,skd->kgqs", grouped, key_rot, preferred_element_type=jnp.float32
    ) * head_dim ** (-0.5)
    row_ids = jnp.arange(row_count)[:, None]
    col_ids = jnp.arange(row_count)[None, :]
    allowed = (col_ids <= row_ids) & (col_ids < length)
    return jax.nn.softmax(jnp.where(allowed, scores, masked_score), axis=-1)


def layer_forward(hidden, params, length, tables):
    w_query, w_key, w_value, w_proj, w_gate, w_up, w_down, gain_attn, gain_mlp = params
    cosine_table, sine_table = tables
    head_dim = cosine_table.shape[-1] * 2
    row_count = hidden.shape[0]
    head_count = w_query.shape[1] // head_dim
    kv_heads = w_key.shape[1] // head_dim
    normed_attn = rms_normalize(hidden, gain_attn).astype(jnp.bfloat16)
    queries = jnp.dot(normed_attn, w_query, preferred_element_type=jnp.float32).reshape(
        row_count, head_count, head_dim
    )
    key_rows = jnp.dot(normed_attn, w_key, preferred_element_type=jnp.float32).reshape(
        row_count, kv_heads, head_dim
    )
    value_rows = jnp.dot(normed_attn, w_value, preferred_element_type=jnp.float32).astype(
        jnp.bfloat16
    )
    value_rows = value_rows.reshape(row_count, kv_heads, head_dim)
    query_rot = rotate(queries, cosine_table, sine_table).astype(jnp.bfloat16)
    key_rot = rotate(key_rows, cosine_table, sine_table).astype(jnp.bfloat16)
    probabilities = attention_probs(query_rot, key_rot, length)
    mixed_heads = jnp.einsum(
        "kgqs,skd->qkgd",
        probabilities.astype(jnp.bfloat16),
        value_rows,
        preferred_element_type=jnp.float32,
    )
    mixed_heads = mixed_heads.reshape(row_count, head_count * head_dim).astype(jnp.bfloat16)
    middle = hidden + jnp.dot(mixed_heads, w_proj, preferred_element_type=jnp.float32)
    normed_mlp = rms_normalize(middle, gain_mlp).astype(jnp.bfloat16)
    gate_proj = jnp.dot(normed_mlp, w_gate, preferred_element_type=jnp.float32)
    up_proj = jnp.dot(normed_mlp, w_up, preferred_element_type=jnp.float32)
    inner_act = (jax.nn.silu(gate_proj) * up_proj).astype(jnp.bfloat16)
    result = middle + jnp.dot(inner_act, w_down, preferred_element_type=jnp.float32)
    saved_layer = (
        hidden,
        normed_attn,
        query_rot,
        key_rot,
        value_rows,
        probabilities,
        mixed_heads,
        middle,
        normed_mlp,
        gate_proj,
        up_proj,
        inner_act,
    )
    return (result, saved_layer)


def layer_backward(saved_layer, grad_top, params, tables):
    (
        hidden,
        normed_attn,
        query_rot,
        key_rot,
        value_rows,
        probabilities,
        mixed_heads,
        middle,
        normed_mlp,
        gate_proj,
        up_proj,
        inner_act,
    ) = saved_layer
    w_query, w_key, w_value, w_proj, w_gate, w_up, w_down, gain_attn, gain_mlp = params
    cosine_table, sine_table = tables
    row_count, head_count, head_dim = query_rot.shape
    kv_heads = key_rot.shape[1]
    group_size = head_count // kv_heads
    branch_grad = grad_top.astype(jnp.bfloat16)
    inner_grad = times_transposed(branch_grad, w_down)
    ignored, gate_pull = jax.vjp(
        lambda gate_in, up_in: jax.nn.silu(gate_in) * up_in, gate_proj, up_proj
    )
    gate_grad, up_grad = gate_pull(inner_grad)
    gate_grad = gate_grad.astype(jnp.bfloat16)
    up_grad = up_grad.astype(jnp.bfloat16)
    normed_mlp_grad = times_transposed(gate_grad, w_gate) + times_transposed(up_grad, w_up)
    ignored, mlp_norm_pull = jax.vjp(rms_normalize, middle, gain_mlp)
    middle_norm_grad, gain_mlp_grad = mlp_norm_pull(normed_mlp_grad)
    middle_grad = grad_top + middle_norm_grad
    attn_grad = middle_grad.astype(jnp.bfloat16)
    mixed_grad = times_transposed(attn_grad, w_proj).astype(jnp.bfloat16)
    mixed_grad = mixed_grad.reshape(row_count, kv_heads, group_size, head_dim)
    probs_grad = jnp.einsum(
        "qkgd,skd->kgqs", mixed_grad, value_rows, preferred_element_type=jnp.float32
    )
    value_grad = jnp.einsum(
        "kgqs,qkgd->skd",
        probabilities.astype(jnp.bfloat16),
        mixed_grad,
        preferred_element_type=jnp.float32,
    )
    value_grad = value_grad.astype(jnp.bfloat16).reshape(row_count, kv_heads * head_dim)
    weighted_sum = jnp.sum(probabilities * probs_grad, axis=-1, keepdims=True)
    score_grad = (probabilities * (probs_grad - weighted_sum)).astype(jnp.bfloat16)
    score_scale = head_dim ** (-0.5)
    grouped = query_rot.reshape(row_count, kv_heads, group_size, head_dim)
    query_rot_grad = (
        jnp.einsum("kgqs,skd->qkgd", score_grad, key_rot, preferred_element_type=jnp.float32)
        * score_scale
    )
    query_rot_grad = query_rot_grad.reshape(row_count, head_count, head_dim)
    key_rot_grad = (
        jnp.einsum("kgqs,qkgd->skd", score_grad, grouped, preferred_element_type=jnp.float32)
        * score_scale
    )
    query_grad = rotate(query_rot_grad, cosine_table, -sine_table).reshape(
        row_count, head_count * head_dim
    )
    query_grad = query_grad.astype(jnp.bfloat16)
    key_grad = rotate(key_rot_grad, cosine_table, -sine_table).reshape(
        row_count, kv_heads * head_dim
    )
    key_grad = key_grad.astype(jnp.bfloat16)
    normed_attn_grad = (
        times_transposed(query_grad, w_query)
        + times_transposed(key_grad, w_key)
        + times_transposed(value_grad, w_value)
    )
    ignored, attn_norm_pull = jax.vjp(rms_normalize, hidden, gain_attn)
    hidden_norm_grad, gain_attn_grad = attn_norm_pull(normed_attn_grad)
    hidden_grad = middle_grad + hidden_norm_grad
    terms = (
        (normed_attn, query_grad),
        (normed_attn, key_grad),
        (normed_attn, value_grad),
        (mixed_heads, attn_grad),
        (normed_mlp, gate_grad),
        (normed_mlp, up_grad),
        (inner_act, branch_grad),
    )
    return (hidden_grad, terms, (gain_attn_grad, gain_mlp_grad))


def pair_forward(hidden, params, length, tables):
    first_out, first_saved = layer_forward(hidden, params, length, tables)
    second_out, second_saved = layer_forward(first_out, params, length, tables)
    return (second_out, (first_saved, second_saved))


def pair_backward(saved_pair, grad_top, params, tables, totals):
    grad_middle, second_terms, second_gains = layer_backward(
        saved_pair[1], grad_top, params, tables
    )
    grad_bottom, first_terms, first_gains = layer_backward(
        saved_pair[0], grad_middle, params, tables
    )
    updated = []
    for running, first_term, second_term in zip(totals[:7], first_terms, second_terms):
        left_rows = jnp.concatenate([first_term[0], second_term[0]], axis=0)
        right_rows = jnp.concatenate([first_term[1], second_term[1]], axis=0)
        updated.append(running + rows_product(left_rows, right_rows))
    updated.append(totals[7] + first_gains[0] + second_gains[0])
    updated.append(totals[8] + first_gains[1] + second_gains[1])
    return (grad_bottom, tuple(updated))


def per_device(
    inputs,
    cotangent,
    lengths,
    w_query,
    w_key,
    w_value,
    w_proj,
    w_gate,
    w_up,
    w_down,
    gain_attn,
    gain_mlp,
):
    section_count = lax.axis_size("pipe")
    section_index = lax.axis_index("pipe")
    full_inputs, full_cotangent = (
        lax.all_gather(inputs, "pipe", axis=1, tiled=True),
        lax.all_gather(cotangent, "pipe", axis=1, tiled=True),
    )
    params = (
        w_query[0],
        w_key[0],
        w_value[0],
        w_proj[0],
        w_gate[0],
        w_up[0],
        w_down[0],
        gain_attn[0],
        gain_mlp[0],
    )
    total_rows, model_width = full_inputs.shape
    segment = total_rows // (MICRO + 1)
    slot_size = 2 * segment
    long_tables = rope_tables(slot_size, HEAD_DIM)
    short_tables = (long_tables[0][:segment], long_tables[1][:segment])
    group_lengths = lengths[0]
    tick_count = MICRO + section_count - 1
    tail_rows = jnp.zeros((segment, model_width), jnp.bfloat16)
    padded_inputs = jnp.concatenate([full_inputs, tail_rows], axis=0)
    padded_cotangent = jnp.concatenate([full_cotangent, tail_rows], axis=0)
    is_first = section_index == 0
    is_last = section_index == section_count - 1
    slot_positions = jnp.arange(slot_size)[:, None]

    def micro_offset(micro_index):
        return jnp.where(micro_index == 0, 0, segment * (micro_index + 1))

    forward_store = jnp.zeros((MICRO, slot_size, model_width), jnp.bfloat16)

    def forward_tick(step_number, loop_state):
        inbound, results, activation_store = loop_state
        micro_index = step_number - section_index
        active = (micro_index >= 0) & (micro_index < MICRO)
        current = jnp.clip(micro_index, 0, MICRO - 1)
        offset = micro_offset(current)
        length = group_lengths[current]
        own_rows = lax.dynamic_slice_in_dim(padded_inputs, offset, slot_size, 0)
        source = jnp.where(is_first, own_rows, inbound)
        selector = jnp.where(active, jnp.where(current == 0, 0, 1), 2)

        def forward_long_branch(operand):
            rows_in, kept_store = operand
            hidden, saved_pair = pair_forward(
                rows_in.astype(jnp.float32), params, length, long_tables
            )
            return (hidden, kept_store)

        def forward_short_branch(operand):
            rows_in, kept_store = operand
            hidden, saved_pair = pair_forward(
                rows_in[:segment].astype(jnp.float32), params, length, short_tables
            )
            return (jnp.pad(hidden, ((0, segment), (0, 0))), kept_store)

        def forward_spare_branch(operand):
            return (jnp.zeros((slot_size, model_width), jnp.float32), operand[1])

        hidden, activation_store = lax.switch(
            selector,
            [forward_long_branch, forward_short_branch, forward_spare_branch],
            (source, activation_store),
        )
        previous = lax.dynamic_index_in_dim(activation_store, current, 0, keepdims=False)
        activation_store = lax.dynamic_update_index_in_dim(
            activation_store, jnp.where(active, source, previous), current, 0
        )
        rounded = hidden.astype(jnp.bfloat16)
        final_rows = jnp.where(slot_positions < length, hidden, jnp.zeros_like(hidden))
        written = lax.dynamic_update_slice_in_dim(results, final_rows, offset, 0)
        results = jnp.where(is_last & active, written, results)
        inbound = from_behind(rounded, "pipe", 1)
        return (inbound, results, activation_store)

    ignored, results, activation_store = lax.fori_loop(
        0,
        tick_count,
        forward_tick,
        (
            jnp.zeros((slot_size, model_width), jnp.bfloat16),
            jnp.zeros((total_rows + segment, model_width), jnp.float32),
            forward_store,
        ),
    )
    start_totals = tuple((jnp.zeros(weight.shape, jnp.float32) for weight in params))

    def backward_tick(step_number, loop_state):
        inbound, input_grads, totals = loop_state
        micro_index = step_number - (section_count - 1 - section_index)
        active = (micro_index >= 0) & (micro_index < MICRO)
        current = jnp.clip(micro_index, 0, MICRO - 1)
        offset = micro_offset(current)
        length = group_lengths[current]
        top_rows = lax.dynamic_slice_in_dim(padded_cotangent, offset, slot_size, 0).astype(
            jnp.float32
        )
        top_grad = jnp.where(slot_positions < length, top_rows, 0.0)
        grad_source = jnp.where(is_last, top_grad, inbound.astype(jnp.float32))
        selector = jnp.where(active, jnp.where(current == 0, 0, 1), 2)

        def backward_long_branch(running):
            rows_in = lax.dynamic_index_in_dim(activation_store, current, 0, keepdims=False)
            saved_pair = pair_forward(rows_in.astype(jnp.float32), params, length, long_tables)[1]
            return pair_backward(saved_pair, grad_source, params, long_tables, running)

        def backward_short_branch(running):
            rows_in = lax.dynamic_index_in_dim(activation_store, current, 0, keepdims=False)[
                :segment
            ]
            saved_pair = pair_forward(rows_in.astype(jnp.float32), params, length, short_tables)[1]
            grad_bottom, running = pair_backward(
                saved_pair, grad_source[:segment], params, short_tables, running
            )
            return (jnp.pad(grad_bottom, ((0, segment), (0, 0))), running)

        def backward_spare_branch(running):
            return (jnp.zeros((slot_size, model_width), jnp.float32), running)

        grad_bottom, totals = lax.switch(
            selector, [backward_long_branch, backward_short_branch, backward_spare_branch], totals
        )
        written = lax.dynamic_update_slice_in_dim(input_grads, grad_bottom, offset, 0)
        input_grads = jnp.where(is_first & active, written, input_grads)
        inbound = from_behind(grad_bottom.astype(jnp.bfloat16), "pipe", -1)
        return (inbound, input_grads, totals)

    ignored, input_grads, totals = lax.fori_loop(
        0,
        tick_count,
        backward_tick,
        (
            jnp.zeros((slot_size, model_width), jnp.bfloat16),
            jnp.zeros((total_rows + segment, model_width), jnp.float32),
            start_totals,
        ),
    )
    summed = (
        lax.psum_scatter(totals[0], "dp", scatter_dimension=0, tiled=True),
        lax.psum_scatter(totals[1], "dp", scatter_dimension=0, tiled=True),
        lax.psum_scatter(totals[2], "dp", scatter_dimension=0, tiled=True),
        lax.psum_scatter(totals[3], "dp", scatter_dimension=0, tiled=True),
        lax.psum_scatter(totals[4], "dp", scatter_dimension=0, tiled=True),
        lax.psum_scatter(totals[5], "dp", scatter_dimension=0, tiled=True),
        lax.psum_scatter(totals[6], "dp", scatter_dimension=0, tiled=True),
        lax.psum_scatter(totals[7], "dp", scatter_dimension=0, tiled=True),
        lax.psum_scatter(totals[8], "dp", scatter_dimension=0, tiled=True),
    )
    columns = model_width // section_count
    start_column = section_index * columns
    all_outputs = broadcast(results[:total_rows], "pipe", section_count - 1)
    all_grads = broadcast(input_grads[:total_rows], "pipe", 0)
    layer_output = lax.dynamic_slice_in_dim(all_outputs, start_column, columns, 1)
    grad_input = lax.dynamic_slice_in_dim(all_grads, start_column, columns, 1)
    return (
        layer_output,
        grad_input,
        summed[0][None],
        summed[1][None],
        summed[2][None],
        summed[3][None],
        summed[4][None],
        summed[5][None],
        summed[6][None],
        summed[7][None],
        summed[8][None],
    )


def solution(mesh):
    placed = (
        P("dp", "pipe"),
        P("dp", "pipe"),
        P("dp", None),
        P("pipe", None, None),
        P("pipe", None, None),
        P("pipe", None, None),
        P("pipe", None, None),
        P("pipe", None, None),
        P("pipe", None, None),
        P("pipe", None, None),
        P("pipe", None),
        P("pipe", None),
    )
    return jax.shard_map(
        per_device,
        mesh=mesh,
        in_specs=placed,
        out_specs=(
            P("dp", "pipe"),
            P("dp", "pipe"),
            P("pipe", "dp", None),
            P("pipe", "dp", None),
            P("pipe", "dp", None),
            P("pipe", "dp", None),
            P("pipe", "dp", None),
            P("pipe", "dp", None),
            P("pipe", "dp", None),
            P("pipe", "dp"),
            P("pipe", "dp"),
        ),
        check_vma=False,
    )
```

profile of v0, /device:TPU:0, one launch (start us, length us, event | category | flops | bytes accessed | tf_op | source)
XLA Modules:
  0.0 2587.4 jit_solution(9190703818967111988)
XLA Ops:
  7.8 9.6 all-gather
  20.8 8.0 copy.307
  37.8 461.7 %while.58 = (s32[]{:T(128)}, bf16[128,960]{1,0:T(8,128)(2,1)}, f32[384,960]{1,0:T(8,128)}, bf16[4,128,960]{2,1,0:T(8,128)(2,1)}, s32[]{:T(128)}, /*index=5*/pred...) while((s32[]{:T(128)}, bf16[128,960]{1,0:T(8,128)(2,1)}, ...), condition=%wide.region_20.21_spmd.clone.clone.clone, body=%wide.region_0.20_spmd.clone.clone.clone.sunk | while | flops 5240218624 | bytes 73638400 | solution.py:334
  62.1 56.8 %conditional.10 = (f32[128,960]{1,0:T(8,128)S(1)}) conditional(s32[]{:T(128)} %clamp.24, (bf16[128,960]{1,0:T(8,128)(2,1)S(1)}, f32[1,960]{1,0:T(1,128)S(1)}, bf16[960,320]{1,0:T(8,128)(2,1)}, s32[]{:T(128)}, bf16[960,320]{1,0:T(8,128)(2,1)S(1)}, /*index=5*/f32[128,1,32]{0,2,1:T(8,128)S(1)}, f32[128,1,32]{0,2,1:T(8,128)S(1)}, ...), branch_computations={%region_1.9_spmd.clone, %region_10.18_spmd, %region_19.19_spmd} | conditional | flops 5239600128 | bytes 68065720 | solution.py:318
  81.5 7.1 multiply_reduce_fusion.15
  109.9 7.9 convolution_add_fusion.18
  131.1 54.4 %conditional.10 = (f32[128,960]{1,0:T(8,128)S(1)}) conditional(s32[]{:T(128)} %clamp.24, (bf16[128,960]{1,0:T(8,128)(2,1)S(1)}, f32[1,960]{1,0:T(1,128)S(1)}, bf16[960,320]{1,0:T(8,128)(2,1)}, s32[]{:T(128)}, bf16[960,320]{1,0:T(8,128)(2,1)S(1)}, /*index=5*/f32[128,1,32]{0,2,1:T(8,128)S(1)}, f32[128,1,32]{0,2,1:T(8,128)S(1)}, ...), branch_computations={%region_1.9_spmd.clone, %region_10.18_spmd, %region_19.19_spmd} | conditional | flops 5239600128 | bytes 68065720 | solution.py:318
  201.1 54.4 %conditional.10 = (f32[128,960]{1,0:T(8,128)S(1)}) conditional(s32[]{:T(128)} %clamp.24, (bf16[128,960]{1,0:T(8,128)(2,1)S(1)}, f32[1,960]{1,0:T(1,128)S(1)}, bf16[960,320]{1,0:T(8,128)(2,1)}, s32[]{:T(128)}, bf16[960,320]{1,0:T(8,128)(2,1)S(1)}, /*index=5*/f32[128,1,32]{0,2,1:T(8,128)S(1)}, f32[128,1,32]{0,2,1:T(8,128)S(1)}, ...), branch_computations={%region_1.9_spmd.clone, %region_10.18_spmd, %region_19.19_spmd} | conditional | flops 5239600128 | bytes 68065720 | solution.py:318
  270.5 54.4 %conditional.10 = (f32[128,960]{1,0:T(8,128)S(1)}) conditional(s32[]{:T(128)} %clamp.24, (bf16[128,960]{1,0:T(8,128)(2,1)S(1)}, f32[1,960]{1,0:T(1,128)S(1)}, bf16[960,320]{1,0:T(8,128)(2,1)}, s32[]{:T(128)}, bf16[960,320]{1,0:T(8,128)(2,1)S(1)}, /*index=5*/f32[128,1,32]{0,2,1:T(8,128)S(1)}, f32[128,1,32]{0,2,1:T(8,128)S(1)}, ...), branch_computations={%region_1.9_spmd.clone, %region_10.18_spmd, %region_19.19_spmd} | conditional | flops 5239600128 | bytes 68065720 | solution.py:318
  326.9 9.1 collective-permute-start
  346.8 61.0 %collective-permute-start = (bf16[128,960]{1,0:T(8,128)(2,1)}, bf16[128,960]{1,0:T(8,128)(2,1)S(1)}, u32[]{:S(2)}, u32[]{:S(2)}) collective-permute-start(bf16[128,960]{1,0:T(8,128)(2,1)} %get-tuple-element.3628), channel_id=1, source_target_pairs={{0,8},{8,16},{16,24},{1,9},{9,17},{17,25},{2,10},{10,18},{18,26},{... | collective-permute-start | bytes 737288 | tf_op jit(solution)/shard_map/while/body/eval_jaxpr/ppermute | solution.py:18
  436.1 61.0 %collective-permute-start = (bf16[128,960]{1,0:T(8,128)(2,1)}, bf16[128,960]{1,0:T(8,128)(2,1)S(1)}, u32[]{:S(2)}, u32[]{:S(2)}) collective-permute-start(bf16[128,960]{1,0:T(8,128)(2,1)} %get-tuple-element.3628), channel_id=1, source_target_pairs={{0,8},{8,16},{16,24},{1,9},{9,17},{17,25},{2,10},{10,18},{18,26},{... | collective-permute-start | bytes 737288 | tf_op jit(solution)/shard_map/while/body/eval_jaxpr/ppermute | solution.py:18
  502.1 58.8 %all-gather.1 = bf16[4,240,320]{1,2,0:T(8,128)(2,1)S(1)} all-gather(bf16[1,240,320]{1,2,0:T(8,128)(2,1)S(1)} %bitcast.1230), channel_id=1, replica_groups=mesh['pipe'=4,'dp'=8] {'pipe'}, dimensions={0}, use_global_device_ids=true | all-gather | bytes 768000 | tf_op jit(solution)/shard_map/all_gather | solution.py:258
  587.6 1107.5 %while.59 = (s32[]{:T(128)}, bf16[128,960]{1,0:T(8,128)(2,1)S(1)}, f32[384,960]{1,0:T(8,128)}, f32[960,960]{1,0:T(8,128)}, f32[960,320]{0,1:T(8,128)}, /*index=5...) while((s32[]{:T(128)}, bf16[128,960]{1,0:T(8,128)(2,1)S(1)}, ...), condition=%wide.region_62.63_spmd.clone.clone.clone, body=%wide.region_22.62_spmd.clone.clone.clone.sunk | while | flops 15045477376 | bytes 699122496 | solution.py:386
  591.4 24.2 conditional.11
  628.2 24.2 conditional.11
  665.0 24.2 conditional.11
  692.8 315.2 %collective-permute-done.1 = bf16[128,960]{1,0:T(8,128)(2,1)S(1)} collective-permute-done((bf16[128,960]{1,0:T(8,128)(2,1)S(1)}, bf16[128,960]{1,0:T(8,128)(2,1)S(1)}, u32[]{:S(2)}, u32[]{:S(2)}) %collective-permute-start.1) | collective-permute-done | bytes 245792 | tf_op jit(solution)/shard_map/while/body/eval_jaxpr/ppermute | solution.py:18
  1011.9 129.5 %conditional.11 = (f32[128,960]{1,0:T(8,128)}, f32[960,960]{1,0:T(8,128)}, f32[960,320]{0,1:T(8,128)}, f32[960,320]{0,1:T(8,128)}, f32[960,960]{1,0:T(8,128)}, /...) conditional(s32[]{:T(128)} %clamp.25, ...), branch_computations={%region_23.41_spmd.clone, %region_42.60_spmd, %region_61.61_spmd} | conditional | flops 15044736000 | bytes 695319744 | solution.py:378
  1145.0 62.2 %collective-permute-done.1 = bf16[128,960]{1,0:T(8,128)(2,1)S(1)} collective-permute-done((bf16[128,960]{1,0:T(8,128)(2,1)S(1)}, bf16[128,960]{1,0:T(8,128)(2,1)S(1)}, u32[]{:S(2)}, u32[]{:S(2)}) %collective-permute-start.1) | collective-permute-done | bytes 245792 | tf_op jit(solution)/shard_map/while/body/eval_jaxpr/ppermute | solution.py:18
  1211.1 148.5 %conditional.11 = (f32[128,960]{1,0:T(8,128)}, f32[960,960]{1,0:T(8,128)}, f32[960,320]{0,1:T(8,128)}, f32[960,320]{0,1:T(8,128)}, f32[960,960]{1,0:T(8,128)}, /...) conditional(s32[]{:T(128)} %clamp.25, ...), branch_computations={%region_23.41_spmd.clone, %region_42.60_spmd, %region_61.61_spmd} | conditional | flops 15044736000 | bytes 695319744 | solution.py:378
  1373.5 148.5 %conditional.11 = (f32[128,960]{1,0:T(8,128)}, f32[960,960]{1,0:T(8,128)}, f32[960,320]{0,1:T(8,128)}, f32[960,320]{0,1:T(8,128)}, f32[960,960]{1,0:T(8,128)}, /...) conditional(s32[]{:T(128)} %clamp.25, ...), branch_computations={%region_23.41_spmd.clone, %region_42.60_spmd, %region_61.61_spmd} | conditional | flops 15044736000 | bytes 695319744 | solution.py:378
  1536.0 148.5 %conditional.11 = (f32[128,960]{1,0:T(8,128)}, f32[960,960]{1,0:T(8,128)}, f32[960,320]{0,1:T(8,128)}, f32[960,320]{0,1:T(8,128)}, f32[960,960]{1,0:T(8,128)}, /...) conditional(s32[]{:T(128)} %clamp.25, ...), branch_computations={%region_23.41_spmd.clone, %region_42.60_spmd, %region_61.61_spmd} | conditional | flops 15044736000 | bytes 695319744 | solution.py:378
  1700.9 11.3 copy.313
  1714.2 21.9 all-reduce.8
  1736.7 21.5 all-reduce.16.cloned.1.call-done
  1760.5 117.7 %all-reduce.14.cloned.1.call-done = (f32[960,320]{0,1:T(8,128)}, f32[960,320]{0,1:T(8,128)}) async-done(((f32[960,320]{0,1:T(8,128)}, f32[960,320]{0,1:T(8,128)}), (f32[960,320]{0,1:T(8,128)}, f32[960,320]{0,1:T(8,128)})) %all-reduce.14.cloned.1.call-update) | async-done | bytes 2457616
  1880.2 85.7 %reduce-scatter.8.cloned.1.call-done = f32[120,960]{1,0:T(8,128)} async-done(((f32[960,960]{1,0:T(8,128)}), f32[120,960]{1,0:T(8,128)}) %reduce-scatter.8.cloned.1.call-update) | async-done | bytes 460816 | tf_op jit(solution)/shard_map/reduce_scatter | solution.py:397
  1965.9 88.6 %reduce-scatter.10.cloned.1.call-done = f32[120,960]{1,0:T(8,128)} async-done(((f32[960,960]{1,0:T(8,128)}), f32[120,960]{1,0:T(8,128)}) %reduce-scatter.10.cloned.1.call-update) | async-done | bytes 460816 | tf_op jit(solution)/shard_map/reduce_scatter | solution.py:400
  2054.5 172.6 %reduce-scatter.12.cloned.1.call-done = f32[120,2560]{1,0:T(8,128)} async-done(((f32[960,2560]{1,0:T(8,128)}), f32[120,2560]{1,0:T(8,128)}) %reduce-scatter.12.cloned.1.call-update) | async-done | bytes 1228816 | tf_op jit(solution)/shard_map/reduce_scatter | solution.py:401
  2227.0 172.0 %reduce-scatter.14.cloned.1.call-done = f32[120,2560]{1,0:T(8,128)} async-done(((f32[960,2560]{1,0:T(8,128)}), f32[120,2560]{1,0:T(8,128)}) %reduce-scatter.14.cloned.1.call-update) | async-done | bytes 1228816 | tf_op jit(solution)/shard_map/reduce_scatter | solution.py:402
  2399.0 181.3 %reduce-scatter.16.cloned.1.call-done = f32[320,960]{1,0:T(8,128)} async-done(((f32[2560,960]{1,0:T(8,128)}), f32[320,960]{1,0:T(8,128)}) %reduce-scatter.16.cloned.1.call-update) | async-done | bytes 1228816 | tf_op jit(solution)/shard_map/reduce_scatter | solution.py:403
  (1696 shorter events, 938.5 us)
Async XLA Ops:
  7.2 1751.0 %all-reduce.16.cloned.1.call-start = ((), (), s32[]{:S(2)}) async-start(), calls=%async_computation.11 | async-start | bytes 5242880 | tf_op jit(solution)/shard_map/psum | solution.py:23
  68.9 24.6 copy-start.128
  68.9 24.6 copy-start.129
  121.0 2.6 collective-permute-start
  187.5 6.1 collective-permute-start
  257.5 5.6 collective-permute-start
  326.9 10.4 collective-permute-start
  346.8 62.3 %collective-permute-start = (bf16[128,960]{1,0:T(8,128)(2,1)}, bf16[128,960]{1,0:T(8,128)(2,1)S(1)}, u32[]{:S(2)}, u32[]{:S(2)}) collective-permute-start(bf16[128,960]{1,0:T(8,128)(2,1)} %get-tuple-element.3628), channel_id=1, source_target_pairs={{0,8},{8,16},{16,24},{1,9},{9,17},{17,25},{2,10},{10,18},{18,26},{... | collective-permute-start | bytes 737288 | tf_op jit(solution)/shard_map/while/body/eval_jaxpr/ppermute | solution.py:18
  418.6 8.0 collective-permute-start
  436.1 62.3 %collective-permute-start = (bf16[128,960]{1,0:T(8,128)(2,1)}, bf16[128,960]{1,0:T(8,128)(2,1)S(1)}, u32[]{:S(2)}, u32[]{:S(2)}) collective-permute-start(bf16[128,960]{1,0:T(8,128)(2,1)} %get-tuple-element.3628), channel_id=1, source_target_pairs={{0,8},{8,16},{16,24},{1,9},{9,17},{17,25},{2,10},{10,18},{18,26},{... | collective-permute-start | bytes 737288 | tf_op jit(solution)/shard_map/while/body/eval_jaxpr/ppermute | solution.py:18
  618.0 3.4 collective-permute-start.1
  654.8 4.6 collective-permute-start.1
  691.5 316.5 %collective-permute-start.1 = (bf16[128,960]{1,0:T(8,128)(2,1)S(1)}, bf16[128,960]{1,0:T(8,128)(2,1)S(1)}, u32[]{:S(2)}, u32[]{:S(2)}) collective-permute-start(bf16[128,960]{1,0:T(8,128)(2,1)S(1)} %get-tuple-element.3662), channel_id=1, source_target_pairs={{8,0},{16,8},{24,16},{9,1},{17,9},{25,17},{10,2},{18,10},{26,18},{... | collective-permute-start | bytes 737288 | tf_op jit(solution)/shard_map/while/body/eval_jaxpr/ppermute | solution.py:18
  1143.7 63.5 %collective-permute-start.1 = (bf16[128,960]{1,0:T(8,128)(2,1)S(1)}, bf16[128,960]{1,0:T(8,128)(2,1)S(1)}, u32[]{:S(2)}, u32[]{:S(2)}) collective-permute-start(bf16[128,960]{1,0:T(8,128)(2,1)S(1)} %get-tuple-element.3662), channel_id=1, source_target_pairs={{8,0},{16,8},{24,16},{9,1},{17,9},{25,17},{10,2},{18,10},{26,18},{... | collective-permute-start | bytes 737288 | tf_op jit(solution)/shard_map/while/body/eval_jaxpr/ppermute | solution.py:18
  1250.5 22.0 copy-start.33
  1270.2 22.2 copy-start.175
  1297.2 13.0 slice-start.18
  1361.9 7.7 collective-permute-start.1
  1412.9 22.0 copy-start.33
  1432.6 22.2 copy-start.175
  1459.6 13.0 slice-start.18
  1524.5 7.6 collective-permute-start.1
  1575.4 22.0 copy-start.33
  1595.0 22.2 copy-start.175
  1622.1 13.0 slice-start.18
  1686.8 3.4 collective-permute-start.1
  1697.6 180.6 %all-reduce.14.cloned.1.call-start = ((), (), s32[]{:S(2)}) async-start(), calls=%async_computation.10 | async-start | bytes 5242880
  1698.4 267.5 %reduce-scatter.8.cloned.1.call-start = ((), (), s32[]{:S(2)}) async-start(), calls=%async_computation.5 | async-start | bytes 4423680 | tf_op jit(solution)/shard_map/reduce_scatter | solution.py:397
  1699.1 355.3 %reduce-scatter.10.cloned.1.call-start = ((), (), s32[]{:S(2)}) async-start(), calls=%async_computation.6 | async-start | bytes 4423680 | tf_op jit(solution)/shard_map/reduce_scatter | solution.py:400
  1699.7 527.3 %reduce-scatter.12.cloned.1.call-start = ((), (), s32[]{:S(2)}) async-start(), calls=%async_computation.7 | async-start | bytes 11059200 | tf_op jit(solution)/shard_map/reduce_scatter | solution.py:401
  1700.3 698.7 %reduce-scatter.14.cloned.1.call-start = ((), (), s32[]{:S(2)}) async-start(), calls=%async_computation.8 | async-start | bytes 11059200 | tf_op jit(solution)/shard_map/reduce_scatter | solution.py:402
  1700.9 879.5 %reduce-scatter.16.cloned.1.call-start = ((), (), s32[]{:S(2)}) async-start(), calls=%async_computation.9 | async-start | bytes 11796480 | tf_op jit(solution)/shard_map/reduce_scatter | solution.py:403
  (456 other events, 1839.8 us)
Sparse Core Ops, SparseCore 0:
  1697.8 60.4 all-reduce.15
  1761.9 116.2 all-reduce.13
  1882.5 83.3 reduce-scatter.7
  1970.4 83.9 reduce-scatter.9
  2058.5 168.4 reduce-scatter.11
  2231.1 167.8 reduce-scatter.13
  2403.2 177.1 reduce-scatter.15
where the time goes:
time: 2600 us; the launch traced here: 2590 us
  waiting for transfers between devices  1250 us (48%)
  matrix products  494 us (19%)
  local copies, waits for them, and re-layouts  271 us (10%)
  loops' own time  162 us (6%)
  starting transfers between devices  157 us (6%)
  other arithmetic  149 us (6%)
  blocking collectives  90.2 us (3%)
    ppermute x14, waiting for transfers between devices, from_behind(): return lax.ppermute(block, axis, route)  407 us
    reduce_scatter x1, waiting for transfers between devices, per_device(): lax.psum_scatter(totals[6], 'dp', scatter_dimension=0, tiled=True)  181 us
    reduce_scatter x1, waiting for transfers between devices, per_device(): lax.psum_scatter(totals[4], 'dp', scatter_dimension=0, tiled=True)  173 us
    reduce_scatter x1, waiting for transfers between devices, per_device(): lax.psum_scatter(totals[5], 'dp', scatter_dimension=0, tiled=True)  172 us
    ppermute x14, starting transfers between devices, from_behind(): return lax.ppermute(block, axis, route)  157 us
    another operation x7, loops' own time, backward_tick(): lax.switch(selector, [backward_long_branch, backward_short_branch, backwa...  132 us
    unnamed x8, waiting for transfers between devices  121 us
    dot_general x56, matrix products, times_transposed(): lax.dot_general(left_rows, right_rows, (((1,), (1,)), ((), ())), preferre...  97.5 us
  transfers between devices with their start and end apart: 21, of which 21 were waited for; matrix products, arithmetic and copies ran while one was open for 1% of the time, Pallas kernels for 0%

commit v1 on v0

v1 whole, which is shorter than its diff:
```python
import functools

import jax
import jax.numpy as jnp
import numpy as np
from jax import lax
from jax.experimental import pallas as pl
from jax.experimental.pallas import tpu as pltpu
from jax.sharding import PartitionSpec as P

HEAD_DIM = 64
HALF = HEAD_DIM // 2
LANES = 128
MICRO = 4
CHUNKS = 3
SCALE = HEAD_DIM**-0.5
BF16 = jnp.bfloat16
F32 = jnp.float32

epsilon = 1e-05
rope_base = 10000.0
masked_score = -1e30

SLOT, ACTIVE, EDGE, LONG, LEN_A, LEN_B = range(6)


def round_up(value, multiple):
    return -(-value // multiple) * multiple


def dot(left, right):
    return jnp.dot(left, right, preferred_element_type=F32)


def dot_t(left, right):
    return lax.dot_general(left, right, (((1,), (1,)), ((), ())), preferred_element_type=F32)


def dot_rows(left, right):
    return lax.dot_general(left, right, (((0,), (0,)), ((), ())), preferred_element_type=F32)


def lane_ids(rows):
    return lax.broadcasted_iota(jnp.int32, (rows, LANES), 1)


def in_low_half(rows):
    return lane_ids(rows) < HEAD_DIM


def rotate(slab, cosine, signed_sine):
    first = (lane_ids(slab.shape[0]) % HEAD_DIM) < HALF
    partner = jnp.where(
        first, pltpu.roll(slab, LANES - HALF, 1), pltpu.roll(slab, HALF, 1)
    )
    return slab * cosine + partner * signed_sine


def both_halves(slab, upper):
    swapped = pltpu.roll(slab, HEAD_DIM, 1)
    low = in_low_half(slab.shape[0])
    return jnp.where(low, swapped, slab) if upper else jnp.where(low, slab, swapped)


def reciprocal_rms(value):
    return lax.rsqrt(jnp.mean(value * value, axis=-1, keepdims=True) + epsilon)


def score_bias(meta, rows):
    query = lax.broadcasted_iota(jnp.int32, (rows, rows), 0)
    key = lax.broadcasted_iota(jnp.int32, (rows, rows), 1)
    segment = rows // 2
    is_long = meta[LONG] == 1
    bound = jnp.where(
        is_long,
        meta[LEN_A],
        jnp.where(key < segment, meta[LEN_A], meta[LEN_B] + segment),
    )
    start = jnp.where(is_long, 0, jnp.where(query < segment, 0, segment))
    allowed = (key <= query) & (key < bound) & (key >= start)
    return jnp.where(allowed, 0.0, masked_score).astype(F32)


def start_all(copies, condition):
    @pl.when(condition)
    def _():
        for copy in copies:
            copy.start()


def wait_one(copy, condition):
    @pl.when(condition)
    def _():
        copy.wait()


def forward_kernel(
    sizes,
    meta,
    first_in,
    inbound,
    cosine_ref,
    sine_ref,
    gain_attn,
    gain_mlp,
    w_query,
    w_key,
    w_value,
    w_proj,
    w_gate,
    w_up,
    w_down,
    *rest,
):
    store_count = 11
    rest = rest[sizes["aliased"] :]
    out_round, out_full = rest[0], rest[1]
    (
        hidden_out,
        normed_attn_out,
        query_out,
        key_out,
        value_out,
        probs_out,
        mixed_out,
        middle_out,
        normed_mlp_out,
        slopes_out,
        inner_out,
    ) = rest[2 : 2 + store_count]
    (
        hidden_s,
        query_s,
        key_s,
        value_s,
        wq,
        wk,
        wv,
        wp,
        wg,
        wu,
        wd,
        sems,
    ) = rest[2 + store_count :]
    rows, width = hidden_s.shape
    heads = width // HEAD_DIM
    kv_heads = w_key.shape[1] // HEAD_DIM
    share = heads // kv_heads
    ff = w_gate.shape[1]
    app = pl.program_id(0)
    pairs = (
        (w_query, wq),
        (w_key, wk),
        (w_value, wv),
        (w_proj, wp),
        (w_gate, wg),
        (w_up, wu),
        (w_down, wd),
    )
    copies = [
        pltpu.make_async_copy(source, target, sems.at[i]) for i, (source, target) in enumerate(pairs)
    ]

    @pl.when(meta[ACTIVE] == 1)
    def _():
        start_all(copies, app == 0)

        @pl.when(app == 0)
        def _():
            hidden_s[...] = jnp.where(
                meta[EDGE] == 1, first_in[...].astype(F32), inbound[...].astype(F32)
            )
            query_s[:, query_s.shape[1] - LANES :] = jnp.zeros((rows, LANES), F32)
            key_s[:, key_s.shape[1] - LANES :] = jnp.zeros((rows, LANES), F32)
            value_s[:, value_s.shape[1] - LANES :] = jnp.zeros((rows, LANES), F32)

        hidden = hidden_s[...]
        hidden_out[0, 0] = hidden
        normed = (hidden * reciprocal_rms(hidden) * gain_attn[...]).astype(BF16)
        normed_attn_out[0, 0] = normed
        wait_one(copies[0], app == 0)
        query_s[:, :width] = dot(normed, wq[...])
        wait_one(copies[1], app == 0)
        key_s[:, : kv_heads * HEAD_DIM] = dot(normed, wk[...])
        wait_one(copies[2], app == 0)
        value_s[:, : kv_heads * HEAD_DIM] = dot(normed, wv[...])
        cosine = cosine_ref[meta[LONG]]
        sine = sine_ref[meta[LONG]]
        low = in_low_half(rows)
        query_parts = []
        for j in range(query_s.shape[1] // LANES):
            slab = rotate(query_s[:, j * LANES : (j + 1) * LANES], cosine, sine)
            query_out[0, 0, :, j * LANES : (j + 1) * LANES] = slab.astype(BF16)
            query_parts.append(jnp.where(low, slab, 0.0).astype(BF16))
            query_parts.append(jnp.where(low, 0.0, slab).astype(BF16))
        keys, values = [], []
        for j in range(key_s.shape[1] // LANES):
            slab = rotate(key_s[:, j * LANES : (j + 1) * LANES], cosine, sine)
            key_out[0, 0, :, j * LANES : (j + 1) * LANES] = slab.astype(BF16)
            keys.append(both_halves(slab, False).astype(BF16))
            keys.append(both_halves(slab, True).astype(BF16))
            slab = value_s[:, j * LANES : (j + 1) * LANES]
            value_out[0, 0, :, j * LANES : (j + 1) * LANES] = slab.astype(BF16)
            values.append(both_halves(slab, False).astype(BF16))
            values.append(both_halves(slab, True).astype(BF16))
        bias = score_bias(meta, rows)
        bias = jnp.concatenate([bias] * share, axis=0)
        mixed_parts = []
        for kv in range(kv_heads):
            grouped = jnp.concatenate(query_parts[kv * share : (kv + 1) * share], axis=0)
            scores = dot_t(grouped, keys[kv]) * SCALE + bias
            exponent = jnp.exp(scores - jnp.max(scores, axis=-1, keepdims=True))
            total = jnp.sum(exponent, axis=-1, keepdims=True)
            probs = (exponent * (1.0 / total)).astype(BF16)
            probs_out[0, 0, kv] = probs
            mixed = dot(probs, values[kv])
            mixed_parts += [mixed[i * rows : (i + 1) * rows] for i in range(share)]
        for j in range(heads // 2):
            mixed_out[0, 0, :, j * LANES : (j + 1) * LANES] = jnp.where(
                low, mixed_parts[2 * j], mixed_parts[2 * j + 1]
            ).astype(BF16)
        if heads % 2:
            mixed_out[0, 0, :, width - HEAD_DIM :] = mixed_parts[-1][:, :HEAD_DIM].astype(BF16)
        wait_one(copies[3], app == 0)
        middle = hidden + dot(mixed_out[0, 0], wp[...])
        middle_out[0, 0] = middle
        normed = (middle * reciprocal_rms(middle) * gain_mlp[...]).astype(BF16)
        normed_mlp_out[0, 0] = normed
        wait_one(copies[4], app == 0)
        wait_one(copies[5], app == 0)
        step = sizes["ff_step"]
        for at in range(0, ff, step):
            gate = dot(normed, wg[:, at : at + step])
            up = dot(normed, wu[:, at : at + step])
            sigma = 1.0 / (1.0 + jnp.exp(-gate))
            silu = gate * sigma
            inner_out[0, 0, :, at : at + step] = (silu * up).astype(BF16)
            slopes_out[0, 0, 0, :, at : at + step] = (
                up * (sigma * (1.0 + gate * (1.0 - sigma)))
            ).astype(BF16)
            slopes_out[0, 0, 1, :, at : at + step] = silu.astype(BF16)
        wait_one(copies[6], app == 0)
        result = middle + dot(inner_out[0, 0], wd[...])
        hidden_s[...] = result
        out_round[...] = result.astype(BF16)
        out_full[0] = result


def backward_kernel(
    sizes,
    meta,
    top_rows,
    inbound,
    cosine_ref,
    sine_ref,
    gain_attn,
    gain_mlp,
    w_query,
    w_key,
    w_value,
    w_proj,
    w_gate,
    w_up,
    w_down,
    hidden_in,
    query_in,
    key_in,
    value_in,
    probs_in,
    middle_in,
    slopes_in,
    *rest,
):
    store_count = 8
    rest = rest[sizes["aliased"] :]
    out_round, out_full = rest[0], rest[1]
    (
        branch_out,
        gate_out,
        up_out,
        attn_out,
        query_out,
        key_out,
        value_out,
        gains_out,
    ) = rest[2 : 2 + store_count]
    (
        grad_s,
        mixed_s,
        wq,
        wk,
        wv,
        wp,
        wg,
        wu,
        wd,
        sems,
    ) = rest[2 + store_count :]
    rows, width = grad_s.shape
    heads = width // HEAD_DIM
    kv_heads = w_key.shape[1] // HEAD_DIM
    share = heads // kv_heads
    ff = w_gate.shape[1]
    step_id = pl.program_id(0)
    pairs = (
        (w_down, wd),
        (w_gate, wg),
        (w_up, wu),
        (w_proj, wp),
        (w_query, wq),
        (w_key, wk),
        (w_value, wv),
    )
    copies = [
        pltpu.make_async_copy(source, target, sems.at[i]) for i, (source, target) in enumerate(pairs)
    ]

    def rms_backward(value, gain, grad, running):
        scale = reciprocal_rms(value)
        unit = value * scale
        pulled = grad * gain
        gain_terms = grad * unit
        gain_rows = jnp.sum(gain_terms.reshape(rows // 8, 8, width), axis=0)
        shared = jnp.mean(gain_terms * gain, axis=-1, keepdims=True)
        return running + scale * (pulled - unit * shared), gain_rows

    @pl.when(meta[ACTIVE] == 1)
    def _():
        start_all(copies, step_id == 0)

        @pl.when(step_id == 0)
        def _():
            row = lax.broadcasted_iota(jnp.int32, (rows, 1), 0)
            segment = rows // 2
            bound = jnp.where(
                meta[LONG] == 1,
                meta[LEN_A],
                jnp.where(row < segment, meta[LEN_A], meta[LEN_B] + segment),
            )
            top = jnp.where(row < bound, top_rows[...].astype(F32), 0.0)
            grad_s[...] = jnp.where(meta[EDGE] == 1, top, inbound[...].astype(F32))
            mixed_s[:, mixed_s.shape[1] - LANES :] = jnp.zeros((rows, LANES), F32)

        low = in_low_half(rows)
        grad_top = grad_s[...]
        branch = grad_top.astype(BF16)
        branch_out[0, 0] = branch
        wait_one(copies[0], step_id == 0)
        step = sizes["ff_step"]
        for at in range(0, ff, step):
            inner_grad = dot_t(branch, wd[at : at + step, :])
            gate_out[0, 0, :, at : at + step] = (
                inner_grad * slopes_in[0, 0, 0, :, at : at + step].astype(F32)
            ).astype(BF16)
            up_out[0, 0, :, at : at + step] = (
                inner_grad * slopes_in[0, 0, 1, :, at : at + step].astype(F32)
            ).astype(BF16)
        wait_one(copies[1], step_id == 0)
        pulled = dot_t(gate_out[0, 0], wg[...])
        wait_one(copies[2], step_id == 0)
        pulled += dot_t(up_out[0, 0], wu[...])
        middle_grad, gain_rows = rms_backward(middle_in[0, 0], gain_mlp[...], pulled, grad_top)
        gains_out[0, 0, 1] = gain_rows
        attn_grad = middle_grad.astype(BF16)
        attn_out[0, 0] = attn_grad
        wait_one(copies[3], step_id == 0)
        mixed_s[:, :width] = dot_t(attn_grad, wp[...])
        mixed_parts, query_parts = [], []
        for j in range(mixed_s.shape[1] // LANES):
            slab = mixed_s[:, j * LANES : (j + 1) * LANES]
            mixed_parts.append(jnp.where(low, slab, 0.0).astype(BF16))
            mixed_parts.append(jnp.where(low, 0.0, slab).astype(BF16))
            slab = query_in[0, 0, :, j * LANES : (j + 1) * LANES].astype(F32)
            query_parts.append(jnp.where(low, slab, 0.0).astype(BF16))
            query_parts.append(jnp.where(low, 0.0, slab).astype(BF16))
        keys, values = [], []
        for j in range(key_in.shape[-1] // LANES):
            slab = key_in[0, 0, :, j * LANES : (j + 1) * LANES].astype(F32)
            keys.append(both_halves(slab, False).astype(BF16))
            keys.append(both_halves(slab, True).astype(BF16))
            slab = value_in[0, 0, :, j * LANES : (j + 1) * LANES].astype(F32)
            values.append(both_halves(slab, False).astype(BF16))
            values.append(both_halves(slab, True).astype(BF16))
        cosine = cosine_ref[meta[LONG]]
        sine = -sine_ref[meta[LONG]]
        query_grads, key_grads, value_grads = [], [], []
        for kv in range(kv_heads):
            mixed = jnp.concatenate(mixed_parts[kv * share : (kv + 1) * share], axis=0)
            grouped = jnp.concatenate(query_parts[kv * share : (kv + 1) * share], axis=0)
            probs = probs_in[0, 0, kv]
            probs_wide = probs.astype(F32)
            probs_grad = dot_t(mixed, values[kv])
            shared = jnp.sum(probs_wide * probs_grad, axis=-1, keepdims=True)
            score_grad = (probs_wide * (probs_grad - shared)).astype(BF16)
            pulled = dot(score_grad, keys[kv])
            query_grads += [pulled[i * rows : (i + 1) * rows] for i in range(share)]
            pulled = dot_rows(score_grad, grouped)
            key_grads.append(pulled + pltpu.roll(pulled, HEAD_DIM, 1))
            pulled = dot_rows(probs, mixed)
            value_grads.append(pulled + pltpu.roll(pulled, HEAD_DIM, 1))

        def put(target, parts, finish):
            count = len(parts)
            for j in range(count // 2):
                slab = jnp.where(low, parts[2 * j], parts[2 * j + 1])
                target[0, 0, :, j * LANES : (j + 1) * LANES] = finish(slab).astype(BF16)
            if count % 2:
                target[0, 0, :, (count - 1) * HEAD_DIM :] = finish(parts[-1])[:, :HEAD_DIM].astype(
                    BF16
                )

        put(query_out, query_grads, lambda slab: rotate(slab * SCALE, cosine, sine))
        put(key_out, key_grads, lambda slab: rotate(slab * SCALE, cosine, sine))
        put(value_out, value_grads, lambda slab: slab)
        wait_one(copies[4], step_id == 0)
        wait_one(copies[5], step_id == 0)
        wait_one(copies[6], step_id == 0)
        pulled = dot_t(query_out[0, 0], wq[...])
        pulled += dot_t(key_out[0, 0], wk[...])
        pulled += dot_t(value_out[0, 0], wv[...])
        result, gain_rows = rms_backward(hidden_in[0, 0], gain_attn[...], pulled, middle_grad)
        gains_out[0, 0, 0] = gain_rows
        grad_s[...] = result
        out_round[...] = result.astype(BF16)
        out_full[0] = result


def whole_block(shape):
    return pl.BlockSpec(shape, lambda i, meta: (0,) * len(shape))


def slot_block(shape, reverse=False):
    def place(i, meta):
        return (meta[SLOT], 1 - i if reverse else i) + (0,) * (len(shape) - 2)

    return pl.BlockSpec((1, 1) + tuple(shape[2:]), place)


def slot_only_block(shape):
    return pl.BlockSpec(
        (1,) + tuple(shape[1:]), lambda i, meta: (meta[SLOT],) + (0,) * (len(shape) - 1)
    )


def in_hbm():
    return pl.BlockSpec(memory_space=pl.ANY)


def weight_scratch(weights):
    return [pltpu.VMEM(weight.shape, weight.dtype) for weight in weights]


def run_tick(kernel, sizes, meta, blocks, weights, reads, state, shapes, scratch, reverse, name):
    rows, width = sizes["rows"], sizes["width"]
    slots = sizes["slots"]
    aliased = [] if state is None else list(state)
    outs = [
        jax.ShapeDtypeStruct((rows, width), BF16),
        jax.ShapeDtypeStruct((slots, rows, width), F32),
    ] + shapes
    out_specs = [whole_block((rows, width)), slot_only_block((slots, rows, width))]
    out_specs += [slot_block(shape.shape, reverse) for shape in shapes]
    in_specs = [whole_block(block.shape) for block in blocks]
    in_specs += [in_hbm() for _ in weights]
    in_specs += [slot_block(read.shape, reverse) for read in reads]
    in_specs += [in_hbm() for _ in aliased]
    first_alias = 1 + len(blocks) + len(weights) + len(reads)
    body = functools.partial(kernel, dict(sizes, aliased=len(aliased)))
    flops = 4 * rows * sum(int(np.prod(weight.shape)) for weight in weights)
    return pl.pallas_call(
        body,
        out_shape=outs,
        grid_spec=pltpu.PrefetchScalarGridSpec(
            num_scalar_prefetch=1,
            grid=(2,),
            in_specs=in_specs,
            out_specs=out_specs,
            scratch_shapes=scratch
            + weight_scratch(weights)
            + [pltpu.SemaphoreType.DMA((len(weights),))],
        ),
        input_output_aliases={first_alias + i: 1 + i for i in range(len(aliased))},
        compiler_params=pltpu.CompilerParams(
            dimension_semantics=("arbitrary",), vmem_limit_bytes=56 * 2**20
        ),
        cost_estimate=pl.CostEstimate(
            flops=flops, bytes_accessed=flops // (2 * rows), transcendentals=0
        ),
        name=name,
    )(meta, *blocks, *weights, *reads, *aliased)


def rope_tables(rows):
    segment = rows // 2
    frequency = rope_base ** (-np.arange(HALF, dtype=np.float64) / HALF)
    positions = np.stack([np.arange(rows) % segment, np.arange(rows)]).astype(np.float64)
    angles = np.tile(positions[:, :, None] * frequency, (1, 1, LANES // HALF))
    sign = np.where(np.arange(LANES) % HEAD_DIM < HALF, -1.0, 1.0)
    return (
        jnp.asarray(np.cos(angles), F32),
        jnp.asarray(np.sin(angles) * sign, F32),
    )


def per_device(
    inputs,
    cotangent,
    lengths,
    w_query,
    w_key,
    w_value,
    w_proj,
    w_gate,
    w_up,
    w_down,
    gain_attn,
    gain_mlp,
):
    sections = lax.axis_size("pipe")
    section = lax.axis_index("pipe")
    total_rows, columns = inputs.shape
    width = columns * sections
    rows = 2 * total_rows // (MICRO + 1)
    weights = (
        w_query[0],
        w_key[0],
        w_value[0],
        w_proj[0],
        w_gate[0],
        w_up[0],
        w_down[0],
    )
    kv_width = w_key.shape[-1]
    ff = w_gate.shape[-1]
    kv_heads = kv_width // HEAD_DIM
    share = width // kv_width
    ticks = CHUNKS + sections - 1
    slots = CHUNKS + 1
    sizes = dict(rows=rows, width=width, slots=slots, ff_step=ff // 4)
    cosine, sine = rope_tables(rows)
    is_first = section == 0
    is_last = section == sections - 1

    full_inputs = lax.all_gather(inputs, "pipe", axis=1, tiled=True)
    padding = jnp.zeros((CHUNKS * rows - total_rows, width), BF16)
    chunk_inputs = jnp.concatenate([full_inputs, padding], axis=0)

    spare = jnp.int32(rows // 2)
    group = lengths[0]
    bounds = jnp.stack(
        [
            jnp.stack([group[0], spare]),
            jnp.stack([group[1], group[2]]),
            jnp.stack([group[3], spare]),
        ]
    )

    def tick_scalars(chunk, edge):
        active = (chunk >= 0) & (chunk < CHUNKS)
        current = jnp.clip(chunk, 0, CHUNKS - 1)
        return jnp.stack(
            [
                jnp.where(active, current, CHUNKS),
                active.astype(jnp.int32),
                edge.astype(jnp.int32),
                (current == 0).astype(jnp.int32),
                bounds[current, 0],
                bounds[current, 1],
            ]
        ).astype(jnp.int32)

    def stored(*shape, dtype=BF16):
        return jax.ShapeDtypeStruct((slots, 2) + shape, dtype)

    query_pad, kv_pad = round_up(width, LANES), round_up(kv_width, LANES)
    forward_shapes = [
        stored(rows, width, dtype=F32),
        stored(rows, width),
        stored(rows, query_pad),
        stored(rows, kv_pad),
        stored(rows, kv_pad),
        stored(kv_heads, share * rows, rows),
        stored(rows, width),
        stored(rows, width, dtype=F32),
        stored(rows, width),
        stored(2, rows, ff),
        stored(rows, ff),
    ]
    forward_scratch = [
        pltpu.VMEM((rows, width), F32),
        pltpu.VMEM((rows, query_pad), F32),
        pltpu.VMEM((rows, kv_pad), F32),
        pltpu.VMEM((rows, kv_pad), F32),
    ]
    inbound = jnp.zeros((rows, width), BF16)
    state = None
    for tick in range(ticks):
        at = min(tick, CHUNKS - 1) * rows
        rounded, *state = run_tick(
            forward_kernel,
            sizes,
            tick_scalars(tick - section, is_first),
            (chunk_inputs[at : at + rows], inbound, cosine, sine, gain_attn, gain_mlp),
            weights,
            (),
            state,
            forward_shapes,
            forward_scratch,
            False,
            "layer_pair_forward",
        )
        route = [(s, s + 1) for s in range(sections - 1) if 0 <= tick - s < CHUNKS]
        if route:
            inbound = lax.ppermute(rounded, "pipe", route)
        if tick == 0:
            late_cotangent, _ = lax.optimization_barrier((cotangent, rounded))
    results = state[0]
    (
        hidden,
        normed_attn,
        query_rot,
        key_rot,
        value_rows,
        probs,
        mixed,
        middle,
        normed_mlp,
        slopes,
        inner,
    ) = state[1:]

    full_cotangent = lax.all_gather(late_cotangent, "pipe", axis=1, tiled=True)
    chunk_cotangent = jnp.concatenate([full_cotangent, padding], axis=0)

    backward_shapes = [
        stored(rows, width),
        stored(rows, ff),
        stored(rows, ff),
        stored(rows, width),
        stored(rows, width),
        stored(rows, kv_width),
        stored(rows, kv_width),
        stored(2, 8, width, dtype=F32),
    ]
    backward_scratch = [
        pltpu.VMEM((rows, width), F32),
        pltpu.VMEM((rows, query_pad), F32),
    ]
    reads = (hidden, query_rot, key_rot, value_rows, probs, middle, slopes)
    inbound = jnp.zeros((rows, width), BF16)
    state = None
    for tick in range(ticks):
        at = min(tick, CHUNKS - 1) * rows
        rounded, *state = run_tick(
            backward_kernel,
            sizes,
            tick_scalars(tick - (sections - 1 - section), is_last),
            (chunk_cotangent[at : at + rows], inbound, cosine, sine, gain_attn, gain_mlp),
            weights,
            reads,
            state,
            backward_shapes,
            backward_scratch,
            True,
            "layer_pair_backward",
        )
        route = [
            (s, s - 1) for s in range(1, sections) if 0 <= tick - (sections - 1 - s) < CHUNKS
        ]
        if route:
            inbound = lax.ppermute(rounded, "pipe", route)
    input_grads = state[0]
    branch, gate_grad, up_grad, attn_grad, query_grad, key_grad, value_grad, gains = state[1:]

    def product(left, right):
        left = left[:CHUNKS].reshape(CHUNKS * 2 * rows, left.shape[-1])
        right = right[:CHUNKS].reshape(CHUNKS * 2 * rows, right.shape[-1])
        return dot_rows(left, right).astype(BF16)

    def reduced(value):
        total = lax.psum_scatter(value, "dp", scatter_dimension=0, tiled=True)
        return total.astype(F32)[None]

    grad_down = reduced(product(inner, branch))
    grad_gate = reduced(product(normed_mlp, gate_grad))
    grad_up = reduced(product(normed_mlp, up_grad))
    grad_proj = reduced(product(mixed, attn_grad))
    grad_query = reduced(product(normed_attn, query_grad))
    grad_key = reduced(product(normed_attn, key_grad))
    grad_value = reduced(product(normed_attn, value_grad))
    gain_sums = jnp.sum(gains[:CHUNKS], axis=(0, 1, 3))
    grad_gain_attn = reduced(gain_sums[0])
    grad_gain_mlp = reduced(gain_sums[1])

    def spread(store, source):
        rows_all = store[:CHUNKS].reshape(CHUNKS * rows, width)[:total_rows]
        own = rows_all[:, source * columns : (source + 1) * columns]
        arrived = jnp.where(section == source, own, 0.0)
        for target in range(sections):
            if target != source:
                block = rows_all[:, target * columns : (target + 1) * columns]
                arrived = arrived + lax.ppermute(block, "pipe", [(source, target)])
        return arrived

    segment = rows // 2
    position = jnp.arange(total_rows)
    offsets = jnp.where(position < rows, position, position % segment)
    micro = jnp.where(position < rows, 0, position // segment - 1)
    valid = offsets < group[micro]
    layer_output = jnp.where(valid[:, None], spread(results, sections - 1), 0.0)
    grad_input = spread(input_grads, 0)
    return (
        layer_output,
        grad_input,
        grad_query,
        grad_key,
        grad_value,
        grad_proj,
        grad_gate,
        grad_up,
        grad_down,
        grad_gain_attn,
        grad_gain_mlp,
    )


def solution(mesh):
    placed = (
        P("dp", "pipe"),
        P("dp", "pipe"),
        P("dp", None),
        P("pipe", None, None),
        P("pipe", None, None),
        P("pipe", None, None),
        P("pipe", None, None),
        P("pipe", None, None),
        P("pipe", None, None),
        P("pipe", None, None),
        P("pipe", None),
        P("pipe", None),
    )
    return jax.shard_map(
        per_device,
        mesh=mesh,
        in_specs=placed,
        out_specs=(
            P("dp", "pipe"),
            P("dp", "pipe"),
            P("pipe", "dp", None),
            P("pipe", "dp", None),
            P("pipe", "dp", None),
            P("pipe", "dp", None),
            P("pipe", "dp", None),
            P("pipe", "dp", None),
            P("pipe", "dp", None),
            P("pipe", "dp"),
            P("pipe", "dp"),
        ),
        check_vma=False,
    )
```

time: 2600 us -> 950 us (0.37)
  waiting for transfers between devices: 1250 us -> 549 us
  matrix products: 494 us -> 39.2 us
  local copies, waits for them, and re-layouts: 271 us -> 54.3 us
  Pallas kernels: 0 us -> 177 us
  loops' own time: 162 us -> 0 us
  starting transfers between devices: 157 us -> 25 us
  other arithmetic: 149 us -> 22.6 us
  blocking collectives: 90.2 us -> 59 us
    dot_general x234 -> x7, matrix products: 461 us -> 39.2 us  [dot_rows(): lax.dot_general(left, right, (((0,), (0,)), ((), ())), preferred_element_...]
    ppermute x14 -> x16, waiting for transfers between devices: 407 us -> 113 us  [the longest x10 110 us: per_device(): inbound = lax.ppermute(rounded, 'pipe', route)]
    reduce_scatter x5, waiting for transfers between devices: 700 us -> 436 us  [reduced(): total = lax.psum_scatter(value, 'dp', scatter_dimension=0, tiled=True)]
    pallas_call x0 -> x12, Pallas kernels: none -> 177 us  [run_tick(): pl.pallas_call(body, out_shape=outs, grid_spec=pltpu.PrefetchScalarGridSp...]
    another operation x16 -> x0, loops' own time: 162 us -> none  [the longest x7 132 us: backward_tick(): lax.switch(selector, [backward_long_branch, backward_short_branch, backwa...]
    ppermute x14 -> x16, starting transfers between devices: 157 us -> 24.5 us  [the longest x10 13.6 us: per_device(): inbound = lax.ppermute(rounded, 'pipe', route)]
    unnamed x8 -> x7, waiting for transfers between devices: 121 us -> 0.1 us
    cond x912 -> x0, local copies, waits for them, and re-layouts: 92.3 us -> none
  transfers between devices with their start and end apart: 21 -> 22, of which waited for: 21 -> 9; matrix products, arithmetic and copies ran while one was open for 1% -> 8% of each run, Pallas kernels for 0% -> 0%
where the time goes in v1:
time: 950 us; the launch traced here: 942 us
  waiting for transfers between devices  549 us (58%)
  Pallas kernels  177 us (19%)
  blocking collectives  59 us (6%)
  local copies, waits for them, and re-layouts  54.3 us (6%)
  matrix products  39.2 us (4%)
  starting transfers between devices  25 us (3%)
  other arithmetic  22.6 us (2%)
  between operations  15.9 us (2%)
    reduce_scatter x5, waiting for transfers between devices, reduced(): total = lax.psum_scatter(value, 'dp', scatter_dimension=0, tiled=True)  436 us
    pallas_call x12, Pallas kernels, run_tick(): pl.pallas_call(body, out_shape=outs, grid_spec=pltpu.PrefetchScalarGridSp...  177 us
    ppermute x10, waiting for transfers between devices, per_device(): inbound = lax.ppermute(rounded, 'pipe', route)  110 us
    dot_general x7, matrix products, dot_rows(): lax.dot_general(left, right, (((0,), (0,)), ((), ())), preferred_element_...  39.2 us
    all_gather x1, blocking collectives, per_device(): full_cotangent = lax.all_gather(late_cotangent, 'pipe', axis=1, tiled=True)  27 us
    unnamed x50, local copies, waits for them, and re-layouts  23.2 us
    unnamed x1, blocking collectives  22.5 us
    another operation x12, local copies, waits for them, and re-layouts, tick_scalars(): jnp.stack([jnp.where(active, current, CHUNKS), active.astype(jnp.int32),...  22.4 us
  transfers between devices with their start and end apart: 22, of which 9 were waited for; matrix products, arithmetic and copies ran while one was open for 8% of the time, Pallas kernels for 0%

profile of v1, /device:TPU:0, one launch (start us, length us, event | category | flops | bytes accessed | tf_op | source)
XLA Modules:
  0.0 941.9 jit_solution(602777430238213383)
XLA Ops:
  8.8 9.6 %all-gather = bf16[4,240,320]{1,2,0:T(8,128)(2,1)S(1)} all-gather(bf16[1,240,320]{1,2,0:T(8,128)(2,1)} %bitcast.258), channel_id=1, replica_groups=mesh['pipe'=4,'dp'=8] {'pipe'}, dimensions={0}, use_global_device_ids=true | all-gather | bytes 768000 | tf_op jit(solution)/shard_map/all_gather | solution.py:544
  22.7 7.9 copy.167
  36.6 18.8 %layer_pair_forward.6 = (bf16[128,960]{1,0:T(8,128)(2,1)}, f32[4,128,960]{2,1,0:T(8,128)}, f32[4,2,128,960]{3,2,1,0:T(8,128)}, bf16[4,2,128,960]{3,2,1,0:T(8,128...) custom-call(s32[6]{0:T(128)} %stack.303.meta, ...), custom_call_target="tpu_custom_call" | custom-call | flops 5033164800 | bytes 19660800 | tf_op jit(solution)/shard_map/layer_pair_forward/pallas_call | solution.py:470
  59.6 18.8 %layer_pair_forward.7 = (bf16[128,960]{1,0:T(8,128)(2,1)}, f32[4,128,960]{2,1,0:T(8,128)}, f32[4,2,128,960]{3,2,1,0:T(8,128)}, bf16[4,2,128,960]{3,2,1,0:T(8,128...) custom-call(s32[6]{0:T(128)} %stack.297.meta, ...), custom_call_target="tpu_custom_call", output_to_operand_aliasing={{1}: (14, {}), {2}: (15, {}), {3}: (16, {}), {4}: (17, {}),... | custom-call | flops 5033164800 | bytes 19660800 | tf_op jit(solution)/shard_map/layer_pair_forward/pallas_call | solution.py:470
  82.4 18.7 %layer_pair_forward.8 = (bf16[128,960]{1,0:T(8,128)(2,1)}, f32[4,128,960]{2,1,0:T(8,128)}, f32[4,2,128,960]{3,2,1,0:T(8,128)}, bf16[4,2,128,960]{3,2,1,0:T(8,128...) custom-call(s32[6]{0:T(128)} %stack.291.meta, ...), custom_call_target="tpu_custom_call", output_to_operand_aliasing={{1}: (14, {}), {2}: (15, {}), {3}: (16, {}), {4}: (17, {}),... | custom-call | flops 5033164800 | bytes 19660800 | tf_op jit(solution)/shard_map/layer_pair_forward/pallas_call | solution.py:470
  101.1 3.9 collective-permute-start.2
  107.6 6.1 layer_pair_forward.9
  114.4 27.0 %all-gather.1 = bf16[4,240,320]{1,2,0:T(8,128)(2,1)S(1)} all-gather(bf16[1,240,320]{1,2,0:T(8,128)(2,1)S(1)} %bitcast.259), channel_id=1, replica_groups=mesh['pipe'=4,'dp'=8] {'pipe'}, dimensions={0}, use_global_device_ids=true | all-gather | bytes 768000 | tf_op jit(solution)/shard_map/all_gather | solution.py:632
  148.7 5.9 layer_pair_forward.10
  157.2 5.9 layer_pair_forward.11
  163.2 6.0 layer_pair_backward.6
  172.4 5.9 layer_pair_backward.7
  181.5 6.0 layer_pair_backward.8
  190.7 101.6 %collective-permute-done.10.inbound = bf16[128,960]{1,0:T(8,128)(2,1)S(1)} collective-permute-done((bf16[128,960]{1,0:T(8,128)(2,1)}, bf16[128,960]{1,0:T(8,128)(2,1)S(1)}, u32[]{:S(2)}, u32[]{:S(2)}) %collective-permute-start.10) | collective-permute-done | bytes 245792 | tf_op jit(solution)/shard_map/ppermute | solution.py:671
  292.9 28.5 %layer_pair_backward.9 = (bf16[128,960]{1,0:T(8,128)(2,1)}, f32[4,128,960]{2,1,0:T(8,128)}, bf16[4,2,128,960]{3,2,1,0:T(8,128)(2,1)}, bf16[4,2,128,2560]{3,2,1,0...) custom-call(s32[6]{0:T(128)} %stack.323.meta, ...), custom_call_target="tpu_custom_call", output_to_operand_aliasing={{1}: (21, {}), {2}: (22, {}), {3}: (23, {}), {4}: (24, {}),... | custom-call | flops 5033164800 | bytes 19660800 | tf_op jit(solution)/shard_map/layer_pair_backward/pallas_call | solution.py:470
  324.7 4.7 collective-permute-done.11.inbound
  330.1 28.2 %layer_pair_backward.10 = (bf16[128,960]{1,0:T(8,128)(2,1)}, f32[4,128,960]{2,1,0:T(8,128)}, bf16[4,2,128,960]{3,2,1,0:T(8,128)(2,1)}, bf16[4,2,128,2560]{3,2,1,...) custom-call(s32[6]{0:T(128)} %stack.317.meta, ...), custom_call_target="tpu_custom_call", output_to_operand_aliasing={{1}: (21, {}), {2}: (22, {}), {3}: (23, {}), {4}: (24, {}),... | custom-call | flops 5033164800 | bytes 19660800 | tf_op jit(solution)/shard_map/layer_pair_backward/pallas_call | solution.py:470
  361.5 4.1 collective-permute-done.12.inbound
  366.3 28.4 %layer_pair_backward.11 = (bf16[128,960]{1,0:T(8,128)(2,1)}, f32[4,128,960]{2,1,0:T(8,128)}, bf16[4,2,128,960]{3,2,1,0:T(8,128)(2,1)}, bf16[4,2,128,2560]{3,2,1,...) custom-call(s32[6]{0:T(128)} %stack.311.meta, ...), custom_call_target="tpu_custom_call", output_to_operand_aliasing={{1}: (21, {}), {2}: (22, {}), {3}: (23, {}), {4}: (24, {}),... | custom-call | flops 5033164800 | bytes 19660800 | tf_op jit(solution)/shard_map/layer_pair_backward/pallas_call | solution.py:470
  394.7 2.7 fusion.5
  399.0 4.9 bitcast_convert_fusion.3
  404.0 4.7 bitcast_convert_fusion.4
  409.0 9.3 bitcast_convert_fusion
  419.9 8.1 bitcast_convert_fusion.2
  428.1 8.0 bitcast_convert_fusion.1
  451.1 5.6 collective-permute-start.13
  459.4 22.5 %all-reduce.6 = (f32[960]{0:T(1024)S(1)}, f32[960]{0:T(1024)S(1)}) all-reduce(f32[960]{0:T(1024)S(1)} %bitcast.261, f32[960]{0:T(1024)S(1)} %bitcast.260), channel_id=9, replica_groups=mesh['pipe'=4,'dp'=8] {'dp'}, use_global_device_ids=true, to_apply=%region_8.9.clone | all-reduce | flops 1920 | bytes 15360
  488.2 65.0 %reduce-scatter.10.cloned.1.call-done = bf16[120,960]{1,0:T(8,128)(2,1)} async-done(((bf16[960,960]{1,0:T(8,128)(2,1)}), bf16[120,960]{1,0:T(8,128)(2,1)}) %reduce-scatter.10.cloned.1.call-update) | async-done | bytes 230416 | tf_op jit(solution)/shard_map/reduce_scatter | solution.py:681
  555.0 67.5 %reduce-scatter.8.cloned.1.call-done = bf16[120,960]{1,0:T(8,128)(2,1)} async-done(((bf16[960,960]{1,0:T(8,128)(2,1)}), bf16[120,960]{1,0:T(8,128)(2,1)}) %reduce-scatter.8.cloned.1.call-update) | async-done | bytes 230416 | tf_op jit(solution)/shard_map/reduce_scatter | solution.py:681
  624.3 103.6 %reduce-scatter.16.cloned.1.call-done = bf16[320,960]{1,0:T(8,128)(2,1)} async-done(((bf16[2560,960]{1,0:T(8,128)(2,1)}), bf16[320,960]{1,0:T(8,128)(2,1)}) %reduce-scatter.16.cloned.1.call-update) | async-done | bytes 614416 | tf_op jit(solution)/shard_map/reduce_scatter | solution.py:681
  730.2 100.2 %reduce-scatter.12.cloned.1.call-done = bf16[120,2560]{1,0:T(8,128)(2,1)} async-done(((bf16[960,2560]{1,0:T(8,128)(2,1)}), bf16[120,2560]{1,0:T(8,128)(2,1)}) %reduce-scatter.12.cloned.1.call-update) | async-done | bytes 614416 | tf_op jit(solution)/shard_map/reduce_scatter | solution.py:681
  832.6 99.8 %reduce-scatter.14.cloned.1.call-done = bf16[120,2560]{1,0:T(8,128)(2,1)} async-done(((bf16[960,2560]{1,0:T(8,128)(2,1)}), bf16[120,2560]{1,0:T(8,128)(2,1)}) %reduce-scatter.14.cloned.1.call-update) | async-done | bytes 614416 | tf_op jit(solution)/shard_map/reduce_scatter | solution.py:681
  (131 shorter events, 88.3 us)
Async XLA Ops:
  7.2 477.7 %all-reduce.10.cloned.1.call-start = ((), (), s32[]{:S(2)}) async-start(), calls=%async_computation.10 | async-start | bytes 2621440
  18.3 2.0 copy-start.8
  18.8 2.7 copy-start.9
  55.4 3.5 collective-permute-start
  78.4 3.3 collective-permute-start.1
  101.1 5.7 collective-permute-start.2
  107.6 6.8 copy-start.20
  113.7 34.4 %collective-permute-start.3 = (bf16[128,960]{1,0:T(8,128)(2,1)}, bf16[128,960]{1,0:T(8,128)(2,1)S(1)}, u32[]{:S(2)}, u32[]{:S(2)}) collective-permute-start(bf16[128,960]{1,0:T(8,128)(2,1)} %get-tuple-element.187), channel_id=1, source_target_pairs={{8,16},{16,24},{9,17},{17,25},{10,18},{18,26},{11,19},{19,27},{12,... | collective-permute-start | bytes 737288 | tf_op jit(solution)/shard_map/ppermute | solution.py:614
  154.7 1.8 collective-permute-start.4
  169.1 2.5 collective-permute-start.8
  178.3 2.5 collective-permute-start.9
  187.5 104.7 %collective-permute-start.10 = (bf16[128,960]{1,0:T(8,128)(2,1)}, bf16[128,960]{1,0:T(8,128)(2,1)S(1)}, u32[]{:S(2)}, u32[]{:S(2)}) collective-permute-start(bf16[128,960]{1,0:T(8,128)(2,1)} %get-tuple-element.242), channel_id=1, source_target_pairs={{8,0},{16,8},{24,16},{9,1},{17,9},{25,17},{10,2},{18,10},{26,18},{... | collective-permute-start | bytes 737288 | tf_op jit(solution)/shard_map/ppermute | solution.py:671
  321.5 7.9 collective-permute-start.11
  358.3 7.3 collective-permute-start.12
  366.3 28.4 %copy-start.2 = (bf16[4,2,128,960]{3,2,1,0:T(8,128)(2,1)S(1)}, bf16[4,2,128,960]{3,2,1,0:T(8,128)(2,1)}, u32[]{:S(2)}) copy-start(bf16[4,2,128,960]{3,2,1,0:T(8,128)(2,1)} %get-tuple-element.273) | copy-start | bytes 5898244
  394.6 2.7 copy-start.4
  398.9 154.3 %reduce-scatter.10.cloned.1.call-start = ((), (), s32[]{:S(2)}) async-start(), calls=%async_computation.6 | async-start | bytes 2211840 | tf_op jit(solution)/shard_map/reduce_scatter | solution.py:681
  403.9 218.6 %reduce-scatter.8.cloned.1.call-start = ((), (), s32[]{:S(2)}) async-start(), calls=%async_computation.5 | async-start | bytes 2211840 | tf_op jit(solution)/shard_map/reduce_scatter | solution.py:681
  408.7 319.2 %reduce-scatter.16.cloned.1.call-start = ((), (), s32[]{:S(2)}) async-start(), calls=%async_computation.9 | async-start | bytes 5898240 | tf_op jit(solution)/shard_map/reduce_scatter | solution.py:681
  418.3 412.0 %reduce-scatter.12.cloned.1.call-start = ((), (), s32[]{:S(2)}) async-start(), calls=%async_computation.7 | async-start | bytes 5529600 | tf_op jit(solution)/shard_map/reduce_scatter | solution.py:681
  428.0 504.3 %reduce-scatter.14.cloned.1.call-start = ((), (), s32[]{:S(2)}) async-start(), calls=%async_computation.8 | async-start | bytes 5529600 | tf_op jit(solution)/shard_map/reduce_scatter | solution.py:681
  436.0 1.6 copy-start
  437.7 5.0 copy-start.21
  437.8 12.7 %copy-start.1 = (f32[4,128,960]{2,1,0:T(8,128)S(1)}, f32[4,128,960]{2,1,0:T(8,128)}, u32[]{:S(2)}) copy-start(f32[4,128,960]{2,1,0:T(8,128)} %get-tuple-element.272) | copy-start | bytes 5898244
  440.0 8.6 collective-permute-start.5
  441.3 7.3 collective-permute-start.7
  442.0 6.6 collective-permute-start.6
  450.6 8.8 copy-start.5
  450.7 8.7 copy-start.7
  451.1 32.0 %collective-permute-start.13 = (f32[320,240]{1,0:T(8,128)S(1)}, f32[320,240]{1,0:T(8,128)S(1)}, u32[]{:S(2)}, u32[]{:S(2)}) collective-permute-start(f32[320,240]{1,0:T(8,128)S(1)} %get-tuple-element.289), channel_id=1, source_target_pairs={{0,8},{1,9},{2,10},{3,11},{4,12},{5,13},{6,14},{7,15}} | collective-permute-start | bytes 921608 | tf_op jit(solution)/shard_map/ppermute | solution.py:702
  456.7 26.4 %collective-permute-start.15 = (f32[320,240]{1,0:T(8,128)S(1)}, f32[320,240]{1,0:T(8,128)S(1)}, u32[]{:S(2)}, u32[]{:S(2)}) collective-permute-start(f32[320,240]{1,0:T(8,128)S(1)} %get-tuple-element.290), channel_id=1, source_target_pairs={{0,24},{1,25},{2,26},{3,27},{4,28},{5,29},{6,30},{7,31}} | collective-permute-start | bytes 921608 | tf_op jit(solution)/shard_map/ppermute | solution.py:702
  458.0 25.0 %collective-permute-start.14 = (f32[320,240]{1,0:T(8,128)S(1)}, f32[320,240]{1,0:T(8,128)S(1)}, u32[]{:S(2)}, u32[]{:S(2)}) collective-permute-start(f32[320,240]{1,0:T(8,128)S(1)} %get-tuple-element.291), channel_id=1, source_target_pairs={{0,16},{1,17},{2,18},{3,19},{4,20},{5,21},{6,22},{7,23}} | collective-permute-start | bytes 921608 | tf_op jit(solution)/shard_map/ppermute | solution.py:702
  (12 other events, 9.8 us)
Sparse Core Ops, SparseCore 0:
  399.1 84.1 all-reduce.9
  487.1 66.0 reduce-scatter.9
  556.7 65.7 reduce-scatter.7
  626.4 101.4 reduce-scatter.15
  731.9 98.4 reduce-scatter.11
  833.9 98.3 reduce-scatter.13

commit v2 on v1

v2 whole, which is shorter than its diff:
```python
import functools

import jax
import jax.numpy as jnp
import numpy as np
from jax import lax
from jax.experimental import pallas as pl
from jax.experimental.pallas import tpu as pltpu
from jax.sharding import PartitionSpec as P

HEAD_DIM = 64
HALF = HEAD_DIM // 2
LANES = 128
MICRO = 4
CHUNKS = 3
SCALE = HEAD_DIM**-0.5
BF16 = jnp.bfloat16
F32 = jnp.float32

epsilon = 1e-05
rope_base = 10000.0
masked_score = -1e30

def round_up(value, multiple):
    return -(-value // multiple) * multiple


def dot(left, right):
    return jnp.dot(left, right, preferred_element_type=F32)


def dot_t(left, right):
    return lax.dot_general(left, right, (((1,), (1,)), ((), ())), preferred_element_type=F32)


def dot_rows(left, right):
    return lax.dot_general(left, right, (((0,), (0,)), ((), ())), preferred_element_type=F32)


def lane_ids(rows):
    return lax.broadcasted_iota(jnp.int32, (rows, LANES), 1)


def in_low_half(rows):
    return lane_ids(rows) < HEAD_DIM


def rotate(slab, cosine, signed_sine):
    first = (lane_ids(slab.shape[0]) % HEAD_DIM) < HALF
    partner = jnp.where(
        first, pltpu.roll(slab, LANES - HALF, 1), pltpu.roll(slab, HALF, 1)
    )
    return slab * cosine + partner * signed_sine


def both_halves(slab, upper):
    swapped = pltpu.roll(slab, HEAD_DIM, 1)
    low = in_low_half(slab.shape[0])
    return jnp.where(low, swapped, slab) if upper else jnp.where(low, slab, swapped)


def reciprocal_rms(value):
    return lax.rsqrt(jnp.mean(value * value, axis=-1, keepdims=True) + epsilon)


class Tick:
    def __init__(self, sizes, lengths):
        sections, depth_step, segment = sizes["sections"], sizes["depth_step"], sizes["rows"] // 2
        section = lax.axis_index("pipe")
        depth = sections - 1 - section if sizes["backward"] else section
        chunk = sizes["tick"] - depth_step * depth
        self.active = (chunk >= 0) & (chunk < CHUNKS)
        self.slot = jnp.clip(chunk, 0, CHUNKS - 1)
        self.edge = depth == 0
        self.final = depth == sections - 1
        self.is_long = self.slot == 0
        self.table = jnp.where(self.is_long, 1, 0)
        self.first_length = jnp.where(
            self.is_long, lengths[0, 0], jnp.where(self.slot == 1, lengths[0, 1], lengths[0, 3])
        )
        self.second_length = jnp.where(self.slot == 1, lengths[0, 2], segment)

    def bound(self, position, segment):
        return jnp.where(
            self.is_long,
            self.first_length,
            jnp.where(position < segment, self.first_length, self.second_length + segment),
        )


def score_bias(tick, rows):
    query = lax.broadcasted_iota(jnp.int32, (rows, rows), 0)
    key = lax.broadcasted_iota(jnp.int32, (rows, rows), 1)
    segment = rows // 2
    start = jnp.where(tick.is_long, 0, jnp.where(query < segment, 0, segment))
    allowed = (key <= query) & (key < tick.bound(key, segment)) & (key >= start)
    return jnp.where(allowed, 0.0, masked_score).astype(F32)


def assemble(target, parts, at):
    rows = target.shape[0]
    count = min(rows, parts[0].shape[0] - at)
    target[:count, :] = jnp.concatenate(
        [part[at : at + count, :].astype(F32) for part in parts], axis=1
    )
    if count < rows:
        target[count:, :] = jnp.zeros((rows - count, target.shape[1]), F32)


def when(condition, action):
    pl.when(condition)(action)


def forward_kernel(sizes, lengths, *refs):
    tick = Tick(sizes, lengths)
    refs = list(refs)

    def take(count):
        taken = refs[:count]
        del refs[:count]
        return taken

    cosine_ref, sine_ref, gain_attn, gain_mlp = take(4)
    edge_parts, inbound = take(sizes["edge_parts"]), take(sizes["inbound"])
    wq, wk, wv, wp, wg, wu, wd = take(7)
    take(sizes["aliased"])
    out_round, out_full = take(2)
    stores = take(sizes["stores"])
    hidden_s, query_s, key_s, value_s = take(4)
    buffers = take(sizes["stores"])
    (
        hidden_b,
        normed_attn_b,
        query_b,
        key_b,
        value_b,
        probs_b,
        mixed_b,
        middle_b,
        normed_mlp_b,
        slopes_b,
        inner_b,
    ) = buffers
    store_sems, final_sem = refs
    rows, width = hidden_s.shape
    heads = width // HEAD_DIM
    kv_width = wk.shape[0]
    kv_heads = kv_width // HEAD_DIM
    share = heads // kv_heads
    ff = wg.shape[1]
    slot = tick.slot

    def store(buffer, app):
        i = [other is buffer for other in buffers].index(True)
        return pltpu.make_async_copy(
            buffer.at[app], stores[i].at[slot, app], store_sems.at[i, app]
        )

    def apply(app, carry):
        hidden = hidden_s[...]
        hidden_b[app] = hidden
        store(hidden_b, app).start()
        normed = (hidden * reciprocal_rms(hidden) * gain_attn[...]).astype(BF16)
        normed_attn_b[app] = normed
        store(normed_attn_b, app).start()
        query_s[:, :width] = dot(normed, wq[...])
        key_s[:, :kv_width] = dot_t(normed, wk[...])
        value_s[:, :kv_width] = dot_t(normed, wv[...])
        cosine = cosine_ref[tick.table]
        sine = sine_ref[tick.table]
        low = in_low_half(rows)
        query_parts = []
        for j in range(query_s.shape[1] // LANES):
            slab = rotate(query_s[:, j * LANES : (j + 1) * LANES], cosine, sine)
            query_b[app, :, j * LANES : (j + 1) * LANES] = slab.astype(BF16)
            query_parts.append(jnp.where(low, slab, 0.0).astype(BF16))
            query_parts.append(jnp.where(low, 0.0, slab).astype(BF16))
        store(query_b, app).start()
        keys, values = [], []
        for j in range(key_s.shape[1] // LANES):
            slab = rotate(key_s[:, j * LANES : (j + 1) * LANES], cosine, sine)
            key_b[app, :, j * LANES : (j + 1) * LANES] = slab.astype(BF16)
            keys.append(both_halves(slab, False).astype(BF16))
            keys.append(both_halves(slab, True).astype(BF16))
            slab = value_s[:, j * LANES : (j + 1) * LANES]
            value_b[app, :, j * LANES : (j + 1) * LANES] = slab.astype(BF16)
            values.append(both_halves(slab, False).astype(BF16))
            values.append(both_halves(slab, True).astype(BF16))
        store(key_b, app).start()
        store(value_b, app).start()
        bias = score_bias(tick, rows)
        bias = jnp.concatenate([bias] * share, axis=0)
        mixed_parts = []
        for kv in range(kv_heads):
            grouped = jnp.concatenate(query_parts[kv * share : (kv + 1) * share], axis=0)
            scores = dot_t(grouped, keys[kv]) * SCALE + bias
            exponent = jnp.exp(scores - jnp.max(scores, axis=-1, keepdims=True))
            total = jnp.sum(exponent, axis=-1, keepdims=True)
            probs = (exponent * (1.0 / total)).astype(BF16)
            probs_b[app, kv] = probs
            mixed = dot(probs, values[kv])
            mixed_parts += [mixed[i * rows : (i + 1) * rows] for i in range(share)]
        store(probs_b, app).start()
        for j in range(heads // 2):
            mixed_b[app, :, j * LANES : (j + 1) * LANES] = jnp.where(
                low, mixed_parts[2 * j], mixed_parts[2 * j + 1]
            ).astype(BF16)
        if heads % 2:
            mixed_b[app, :, width - HEAD_DIM :] = mixed_parts[-1][:, :HEAD_DIM].astype(BF16)
        store(mixed_b, app).start()
        middle = hidden + dot(mixed_b[app], wp[...])
        middle_b[app] = middle
        store(middle_b, app).start()
        normed = (middle * reciprocal_rms(middle) * gain_mlp[...]).astype(BF16)
        normed_mlp_b[app] = normed
        store(normed_mlp_b, app).start()
        step = sizes["ff_step"]
        for at in range(0, ff, step):
            gate = dot(normed, wg[:, at : at + step])
            up = dot(normed, wu[:, at : at + step])
            sigma = 1.0 / (1.0 + jnp.exp(-gate))
            silu = gate * sigma
            inner_b[app, :, at : at + step] = (silu * up).astype(BF16)
            slopes_b[app, 0, :, at : at + step] = (
                up * (sigma * (1.0 + gate * (1.0 - sigma)))
            ).astype(BF16)
            slopes_b[app, 1, :, at : at + step] = silu.astype(BF16)
        store(inner_b, app).start()
        store(slopes_b, app).start()
        hidden_s[...] = middle + dot(inner_b[app], wd[...])
        return carry

    @pl.when(tick.active)
    def _():
        if edge_parts:

            @pl.when(tick.edge)
            def _():
                assemble(hidden_s, edge_parts, sizes["tick"] * rows)

        if inbound:

            @pl.when(jnp.logical_not(tick.edge))
            def _():
                hidden_s[...] = inbound[0][...].astype(F32)

        query_s[:, query_s.shape[1] - LANES :] = jnp.zeros((rows, LANES), F32)
        key_s[:, key_s.shape[1] - LANES :] = jnp.zeros((rows, LANES), F32)
        value_s[:, value_s.shape[1] - LANES :] = jnp.zeros((rows, LANES), F32)
        lax.fori_loop(0, 2, apply, 0)
        out_round[...] = hidden_s[...].astype(BF16)
        final = pltpu.make_async_copy(hidden_s, out_full.at[slot], final_sem.at[0])
        when(tick.final, final.start)
        for buffer in buffers:
            store(buffer, 0).wait()
            store(buffer, 1).wait()
        when(tick.final, final.wait)


def backward_kernel(sizes, lengths, *refs):
    tick = Tick(sizes, lengths)
    refs = list(refs)

    def take(count):
        taken = refs[:count]
        del refs[:count]
        return taken

    cosine_ref, sine_ref, gain_attn, gain_mlp = take(4)
    edge_parts, inbound = take(sizes["edge_parts"]), take(sizes["inbound"])
    wq, wk, wv, wp, wg, wu, wd = take(7)
    saved = take(sizes["reads"])
    take(sizes["aliased"])
    out_round, out_full = take(2)
    stores = take(sizes["stores"])
    grad_s, mixed_s = take(2)
    kept = take(sizes["reads"])
    hidden_k, query_k, key_k, value_k, probs_k, middle_k, slopes_k = kept
    buffers = take(sizes["stores"])
    branch_b, gate_b, up_b, attn_b, query_b, key_b, value_b, gains_b = buffers
    read_sems, store_sems, final_sem = refs
    rows, width = grad_s.shape
    heads = width // HEAD_DIM
    kv_width = wk.shape[0]
    kv_heads = kv_width // HEAD_DIM
    share = heads // kv_heads
    ff = wd.shape[1]
    slot = tick.slot

    def read(buffer, app):
        i = [other is buffer for other in kept].index(True)
        return pltpu.make_async_copy(saved[i].at[slot, app], buffer.at[app], read_sems.at[i, app])

    def store(buffer, app):
        i = [other is buffer for other in buffers].index(True)
        return pltpu.make_async_copy(
            buffer.at[app], stores[i].at[slot, app], store_sems.at[i, app]
        )

    def rms_backward(value, gain, grad, running):
        scale = reciprocal_rms(value)
        unit = value * scale
        pulled = grad * gain
        gain_terms = grad * unit
        gain_rows = jnp.sum(gain_terms.reshape(rows // 8, 8, width), axis=0)
        shared = jnp.mean(gain_terms * gain, axis=-1, keepdims=True)
        return running + scale * (pulled - unit * shared), gain_rows

    def apply(step_id, carry):
        app = 1 - step_id

        low = in_low_half(rows)
        grad_top = grad_s[...]
        branch = grad_top.astype(BF16)
        branch_b[app] = branch
        store(branch_b, app).start()
        read(slopes_k, app).wait()
        step = sizes["ff_step"]
        for at in range(0, ff, step):
            inner_grad = dot(branch, wd[:, at : at + step])
            gate_b[app, :, at : at + step] = (
                inner_grad * slopes_k[app, 0, :, at : at + step].astype(F32)
            ).astype(BF16)
            up_b[app, :, at : at + step] = (
                inner_grad * slopes_k[app, 1, :, at : at + step].astype(F32)
            ).astype(BF16)
        store(gate_b, app).start()
        store(up_b, app).start()
        pulled = dot(gate_b[app], wg[...])
        pulled += dot(up_b[app], wu[...])
        read(middle_k, app).wait()
        middle_grad, gain_rows = rms_backward(middle_k[app], gain_mlp[...], pulled, grad_top)
        gains_b[app, 1] = gain_rows
        attn_grad = middle_grad.astype(BF16)
        attn_b[app] = attn_grad
        store(attn_b, app).start()
        mixed_s[:, :width] = dot(attn_grad, wp[...])
        mixed_parts, query_parts = [], []
        read(query_k, app).wait()
        for j in range(mixed_s.shape[1] // LANES):
            slab = mixed_s[:, j * LANES : (j + 1) * LANES]
            mixed_parts.append(jnp.where(low, slab, 0.0).astype(BF16))
            mixed_parts.append(jnp.where(low, 0.0, slab).astype(BF16))
            slab = query_k[app, :, j * LANES : (j + 1) * LANES].astype(F32)
            query_parts.append(jnp.where(low, slab, 0.0).astype(BF16))
            query_parts.append(jnp.where(low, 0.0, slab).astype(BF16))
        keys, values = [], []
        read(key_k, app).wait()
        read(value_k, app).wait()
        for j in range(key_k.shape[-1] // LANES):
            slab = key_k[app, :, j * LANES : (j + 1) * LANES].astype(F32)
            keys.append(both_halves(slab, False).astype(BF16))
            keys.append(both_halves(slab, True).astype(BF16))
            slab = value_k[app, :, j * LANES : (j + 1) * LANES].astype(F32)
            values.append(both_halves(slab, False).astype(BF16))
            values.append(both_halves(slab, True).astype(BF16))
        cosine = cosine_ref[tick.table]
        sine = -sine_ref[tick.table]
        query_grads, key_grads, value_grads = [], [], []
        read(probs_k, app).wait()
        for kv in range(kv_heads):
            mixed = jnp.concatenate(mixed_parts[kv * share : (kv + 1) * share], axis=0)
            grouped = jnp.concatenate(query_parts[kv * share : (kv + 1) * share], axis=0)
            probs = probs_k[app, kv]
            probs_wide = probs.astype(F32)
            probs_grad = dot_t(mixed, values[kv])
            shared = jnp.sum(probs_wide * probs_grad, axis=-1, keepdims=True)
            score_grad = (probs_wide * (probs_grad - shared)).astype(BF16)
            pulled = dot(score_grad, keys[kv])
            query_grads += [pulled[i * rows : (i + 1) * rows] for i in range(share)]
            pulled = dot_rows(score_grad, grouped)
            key_grads.append(pulled + pltpu.roll(pulled, HEAD_DIM, 1))
            pulled = dot_rows(probs, mixed)
            value_grads.append(pulled + pltpu.roll(pulled, HEAD_DIM, 1))

        def put(target, parts, finish):
            count = len(parts)
            for j in range(count // 2):
                slab = jnp.where(low, parts[2 * j], parts[2 * j + 1])
                target[app, :, j * LANES : (j + 1) * LANES] = finish(slab).astype(BF16)
            if count % 2:
                target[app, :, (count - 1) * HEAD_DIM :] = finish(parts[-1])[:, :HEAD_DIM].astype(
                    BF16
                )
            store(target, app).start()

        put(query_b, query_grads, lambda slab: rotate(slab * SCALE, cosine, sine))
        put(key_b, key_grads, lambda slab: rotate(slab * SCALE, cosine, sine))
        put(value_b, value_grads, lambda slab: slab)
        pulled = dot(query_b[app], wq[...])
        pulled += dot(key_b[app], wk[...])
        pulled += dot(value_b[app], wv[...])
        read(hidden_k, app).wait()
        result, gain_rows = rms_backward(hidden_k[app], gain_attn[...], pulled, middle_grad)
        gains_b[app, 0] = gain_rows
        store(gains_b, app).start()
        grad_s[...] = result
        return carry

    @pl.when(tick.active)
    def _():
        for app in (1, 0):
            for buffer in (slopes_k, middle_k, query_k, key_k, value_k, probs_k, hidden_k):
                read(buffer, app).start()
        if edge_parts:

            @pl.when(tick.edge)
            def _():
                assemble(grad_s, edge_parts, sizes["tick"] * rows)
                row = lax.broadcasted_iota(jnp.int32, (rows, 1), 0)
                grad_s[...] = jnp.where(row < tick.bound(row, rows // 2), grad_s[...], 0.0)

        if inbound:

            @pl.when(jnp.logical_not(tick.edge))
            def _():
                grad_s[...] = inbound[0][...].astype(F32)

        mixed_s[:, mixed_s.shape[1] - LANES :] = jnp.zeros((rows, LANES), F32)
        lax.fori_loop(0, 2, apply, 0)
        out_round[...] = grad_s[...].astype(BF16)
        final = pltpu.make_async_copy(grad_s, out_full.at[slot], final_sem.at[0])
        when(tick.final, final.start)
        for buffer in buffers:
            store(buffer, 0).wait()
            store(buffer, 1).wait()
        when(tick.final, final.wait)


def transpose_to(target, source):
    strip = 256 if source.shape[1] % 256 == 0 else source.shape[1]
    for at in range(0, source.shape[1], strip):
        target[at : at + strip, :] = jnp.transpose(source[:, at : at + strip])


def load_kernel(*refs):
    count = (len(refs) - 2) // 2
    sources, targets, turned, sems = refs[:count], refs[count : 2 * count], refs[-2], refs[-1]
    copies = [
        pltpu.make_async_copy(source, target, sems.at[i])
        for i, (source, target) in enumerate(zip(sources, targets))
    ]
    for copy in reversed(copies):
        copy.start()
    copies[-1].wait()
    transpose_to(turned, targets[-1])
    for copy in copies[:-1]:
        copy.wait()


def turn_kernel(*refs):
    count = len(refs) // 2
    for source, target in zip(refs[:count], refs[count:]):
        transpose_to(target, source)


def vmem_array(shape, dtype):
    return pltpu.VMEM(tuple(shape), dtype)


def load_weights(weights):
    turned = weights[-1].shape[::-1]
    return pl.pallas_call(
        load_kernel,
        out_shape=[vmem_array(weight.shape, weight.dtype) for weight in weights]
        + [vmem_array(turned, weights[-1].dtype)],
        in_specs=[in_hbm() for _ in weights],
        out_specs=[in_vmem() for _ in range(len(weights) + 1)],
        scratch_shapes=[pltpu.SemaphoreType.DMA((len(weights),))],
        compiler_params=pltpu.CompilerParams(vmem_limit_bytes=12 * 2**20),
        name="load_weights",
    )(*[pltpu.with_memory_space_constraint(weight, pltpu.HBM) for weight in weights])


def turn_weights(weights):
    return pl.pallas_call(
        turn_kernel,
        out_shape=[vmem_array(weight.shape[::-1], weight.dtype) for weight in weights],
        in_specs=[in_vmem() for _ in weights],
        out_specs=[in_vmem() for _ in weights],
        compiler_params=pltpu.CompilerParams(vmem_limit_bytes=12 * 2**20),
        name="turn_weights",
    )(*[pltpu.with_memory_space_constraint(weight, pltpu.VMEM) for weight in weights])


def in_vmem():
    return pl.BlockSpec(memory_space=pltpu.VMEM)


def in_hbm():
    return pl.BlockSpec(memory_space=pltpu.HBM)


def buffers_for(shapes):
    return [pltpu.VMEM(tuple(shape.shape[1:]), shape.dtype) for shape in shapes]


def run_tick(
    kernel, sizes, lengths, tables, edge_parts, inbound, weights, reads, state, shapes, scratch, name
):
    rows, width = sizes["rows"], sizes["width"]
    aliased = [] if state is None else list(state)
    inbound = [] if inbound is None else [inbound]
    outs = [jax.ShapeDtypeStruct((rows, width), BF16)] + [
        pltpu.HBM(shape.shape, shape.dtype)
        for shape in (jax.ShapeDtypeStruct((CHUNKS, rows, width), F32), *shapes)
    ]
    scratch = scratch + buffers_for(reads) + buffers_for(shapes)
    if reads:
        scratch.append(pltpu.SemaphoreType.DMA((len(reads), 2)))
    scratch.append(pltpu.SemaphoreType.DMA((len(shapes), 2)))
    scratch.append(pltpu.SemaphoreType.DMA((1,)))
    blocks = [*tables, *edge_parts, *inbound]
    first_alias = 1 + len(blocks) + len(weights) + len(reads)
    sizes = dict(
        sizes,
        edge_parts=len(edge_parts),
        inbound=len(inbound),
        aliased=len(aliased),
        stores=len(shapes),
        reads=len(reads),
    )
    flops = 4 * rows * sum(int(np.prod(weight.shape)) for weight in weights)
    return pl.pallas_call(
        functools.partial(kernel, sizes),
        out_shape=outs,
        grid_spec=pltpu.PrefetchScalarGridSpec(
            num_scalar_prefetch=1,
            grid=(1,),
            in_specs=[in_vmem() for _ in (*blocks, *weights)]
            + [in_hbm() for _ in (*reads, *aliased)],
            out_specs=[in_vmem()] + [in_hbm() for _ in outs[1:]],
            scratch_shapes=scratch,
        ),
        input_output_aliases={first_alias + i: 1 + i for i in range(len(aliased))},
        compiler_params=pltpu.CompilerParams(
            dimension_semantics=("arbitrary",), vmem_limit_bytes=18 * 2**20
        ),
        cost_estimate=pl.CostEstimate(
            flops=flops, bytes_accessed=flops // (2 * rows), transcendentals=0
        ),
        name=name,
    )(
        lengths,
        *blocks,
        *[pltpu.with_memory_space_constraint(weight, pltpu.VMEM) for weight in weights],
        *[pltpu.with_memory_space_constraint(array, pltpu.HBM) for array in (*reads, *aliased)],
    )


def rope_tables(rows):
    segment = rows // 2
    frequency = rope_base ** (-np.arange(HALF, dtype=np.float64) / HALF)
    positions = np.stack([np.arange(rows) % segment, np.arange(rows)]).astype(np.float64)
    angles = np.tile(positions[:, :, None] * frequency, (1, 1, LANES // HALF))
    sign = np.where(np.arange(LANES) % HEAD_DIM < HALF, -1.0, 1.0)
    return (
        jnp.asarray(np.cos(angles), F32),
        jnp.asarray(np.sin(angles) * sign, F32),
    )


def gather_to(block, target):
    return [
        block if source == target else lax.ppermute(block, "pipe", [(source, target)])
        for source in range(lax.axis_size("pipe"))
    ]


def swap_neighbours(mine_and_theirs, axis):
    devices = lax.axis_size("dp")
    odd = lax.axis_index("dp") % 2
    theirs = lax.dynamic_index_in_dim(mine_and_theirs, 1 - odd, axis, keepdims=False)
    mine = lax.dynamic_index_in_dim(mine_and_theirs, odd, axis, keepdims=False)
    return mine + lax.ppermute(theirs, "dp", [(i, i ^ 1) for i in range(devices)])


def line_scatter(value):
    devices = lax.axis_size("dp")
    lines = [list(range(first, devices, 2)) for first in range(2)]
    return lax.psum_scatter(
        value, "dp", scatter_dimension=0, tiled=True, axis_index_groups=lines
    )


def pair_first(value):
    devices = lax.axis_size("dp")
    rows, columns = value.shape
    part = swap_neighbours(value.reshape(devices // 2, 2, rows // devices, columns), 1)
    return line_scatter(part.reshape(rows // 2, columns)).astype(F32)


def line_first(value):
    devices = lax.axis_size("dp")
    rows, columns = value.shape
    part = line_scatter(value)
    return swap_neighbours(part.reshape(2, rows // devices, columns), 0).astype(F32)


def per_device(
    inputs,
    cotangent,
    lengths,
    w_query,
    w_key,
    w_value,
    w_proj,
    w_gate,
    w_up,
    w_down,
    gain_attn,
    gain_mlp,
):
    sections = lax.axis_size("pipe")
    section = lax.axis_index("pipe")
    total_rows, columns = inputs.shape
    width = columns * sections
    rows = 2 * total_rows // (MICRO + 1)
    segment = rows // 2
    kv_width = w_key.shape[-1]
    ff = w_gate.shape[-1]
    kv_heads = kv_width // HEAD_DIM
    share = width // kv_width
    depth_step = 2
    ticks = CHUNKS + depth_step * (sections - 1)
    sizes = dict(
        rows=rows, width=width, ff_step=ff // 4, sections=sections, depth_step=depth_step
    )
    tables = (*rope_tables(rows), gain_attn, gain_mlp)
    group = lengths[0]
    input_parts = gather_to(inputs, 0)
    wq, wk_t, wv_t, wp, wg, wu, wd_t, wd = load_weights(
        (
            w_query[0],
            jnp.swapaxes(w_key[0], 0, 1),
            jnp.swapaxes(w_value[0], 0, 1),
            w_proj[0],
            w_gate[0],
            w_up[0],
            jnp.swapaxes(w_down[0], 0, 1),
        )
    )
    wq_t, wp_t, wg_t, wu_t = turn_weights((wq, wp, wg, wu))
    forward_weights = (wq, wk_t, wv_t, wp, wg, wu, wd)
    backward_weights = (wq_t, wk_t, wv_t, wp_t, wg_t, wu_t, wd_t)

    def stored(*shape, dtype=BF16):
        return jax.ShapeDtypeStruct((CHUNKS, 2) + shape, dtype)

    query_pad, kv_pad = round_up(width, LANES), round_up(kv_width, LANES)
    forward_shapes = [
        stored(rows, width, dtype=F32),
        stored(rows, width),
        stored(rows, query_pad),
        stored(rows, kv_pad),
        stored(rows, kv_pad),
        stored(kv_heads, share * rows, rows),
        stored(rows, width),
        stored(rows, width, dtype=F32),
        stored(rows, width),
        stored(2, rows, ff),
        stored(rows, ff),
    ]
    forward_scratch = [
        pltpu.VMEM((rows, width), F32),
        pltpu.VMEM((rows, query_pad), F32),
        pltpu.VMEM((rows, kv_pad), F32),
        pltpu.VMEM((rows, kv_pad), F32),
    ]
    sent = {}
    state = None
    for tick in range(ticks):
        rounded, *state = run_tick(
            forward_kernel,
            dict(sizes, tick=tick, backward=False),
            lengths,
            tables,
            input_parts if tick < CHUNKS else (),
            sent.get(tick - depth_step),
            forward_weights,
            (),
            state,
            forward_shapes,
            forward_scratch,
            "layer_pair_forward",
        )
        route = [
            (s, s + 1) for s in range(sections - 1) if 0 <= tick - depth_step * s < CHUNKS
        ]
        if route:
            sent[tick] = lax.ppermute(rounded, "pipe", route)
        if tick == 0:
            late_cotangent, _ = lax.optimization_barrier((cotangent, rounded))
            cotangent_parts = gather_to(late_cotangent, sections - 1)
    results = state[0]
    (
        hidden,
        normed_attn,
        query_rot,
        key_rot,
        value_rows,
        probs,
        mixed,
        middle,
        normed_mlp,
        slopes,
        inner,
    ) = state[1:]

    backward_shapes = [
        stored(rows, width),
        stored(rows, ff),
        stored(rows, ff),
        stored(rows, width),
        stored(rows, width),
        stored(rows, kv_width),
        stored(rows, kv_width),
        stored(2, 8, width, dtype=F32),
    ]
    backward_scratch = [
        pltpu.VMEM((rows, width), F32),
        pltpu.VMEM((rows, query_pad), F32),
    ]
    reads = (hidden, query_rot, key_rot, value_rows, probs, middle, slopes)
    sent = {}
    state = None
    for tick in range(ticks):
        rounded, *state = run_tick(
            backward_kernel,
            dict(sizes, tick=tick, backward=True),
            lengths,
            tables,
            cotangent_parts if tick < CHUNKS else (),
            sent.get(tick - depth_step),
            backward_weights,
            reads,
            state,
            backward_shapes,
            backward_scratch,
            "layer_pair_backward",
        )
        route = [
            (s, s - 1)
            for s in range(1, sections)
            if 0 <= tick - depth_step * (sections - 1 - s) < CHUNKS
        ]
        if route:
            sent[tick] = lax.ppermute(rounded, "pipe", route)
    input_grads = state[0]
    branch, gate_grad, up_grad, attn_grad, query_grad, key_grad, value_grad, gains = state[1:]

    def all_rows(store):
        return store.reshape(CHUNKS * 2 * rows, store.shape[-1])

    def product(left, right):
        return dot_rows(all_rows(left), all_rows(right)).astype(BF16)

    attention_grads = jnp.concatenate(
        [all_rows(query_grad), all_rows(key_grad), all_rows(value_grad)], axis=1
    )
    grad_attention = line_first(dot_rows(all_rows(normed_attn), attention_grads).astype(BF16))
    grad_gate = pair_first(product(normed_mlp, gate_grad))
    grad_up = pair_first(product(normed_mlp, up_grad))
    grad_down = pair_first(product(inner, branch))
    grad_proj = pair_first(product(mixed, attn_grad))
    grad_query = grad_attention[:, :width]
    grad_key = grad_attention[:, width : width + kv_width]
    grad_value = grad_attention[:, width + kv_width :]
    gain_sums = jnp.sum(gains, axis=(0, 1, 3))
    grad_gain_attn = lax.psum_scatter(gain_sums[0], "dp", scatter_dimension=0, tiled=True)
    grad_gain_mlp = lax.psum_scatter(gain_sums[1], "dp", scatter_dimension=0, tiled=True)

    def spread(store, source):
        rows_all = store.reshape(CHUNKS * rows, width)[:total_rows]
        own = rows_all[:, source * columns : (source + 1) * columns]
        arrived = jnp.where(section == source, own, 0.0)
        for target in range(sections):
            if target != source:
                block = rows_all[:, target * columns : (target + 1) * columns]
                arrived = arrived + lax.ppermute(block, "pipe", [(source, target)])
        return arrived

    position = jnp.arange(total_rows)
    long_rows = position < rows
    offsets = jnp.where(long_rows, position, position % segment)
    micro = jnp.where(long_rows, 0, position // segment - 1)
    bound = jnp.zeros_like(position)
    for m in range(MICRO):
        bound = jnp.where(micro == m, group[m], bound)
    valid = (offsets < bound)[:, None]
    results, input_grads, _ = lax.optimization_barrier((results, input_grads, grad_gate))
    layer_output = jnp.where(valid, spread(results, sections - 1), 0.0)
    grad_input = spread(input_grads, 0)
    return (
        layer_output,
        grad_input,
        grad_query[None],
        grad_key[None],
        grad_value[None],
        grad_proj[None],
        grad_gate[None],
        grad_up[None],
        grad_down[None],
        grad_gain_attn[None],
        grad_gain_mlp[None],
    )


def solution(mesh):
    placed = (
        P("dp", "pipe"),
        P("dp", "pipe"),
        P("dp", None),
        P("pipe", None, None),
        P("pipe", None, None),
        P("pipe", None, None),
        P("pipe", None, None),
        P("pipe", None, None),
        P("pipe", None, None),
        P("pipe", None, None),
        P("pipe", None),
        P("pipe", None),
    )
    return jax.shard_map(
        per_device,
        mesh=mesh,
        in_specs=placed,
        out_specs=(
            P("dp", "pipe"),
            P("dp", "pipe"),
            P("pipe", "dp", None),
            P("pipe", "dp", None),
            P("pipe", "dp", None),
            P("pipe", "dp", None),
            P("pipe", "dp", None),
            P("pipe", "dp", None),
            P("pipe", "dp", None),
            P("pipe", "dp"),
            P("pipe", "dp"),
        ),
        check_vma=False,
    )
```

time: 950 us -> 521 us (0.55)
  waiting for transfers between devices: 549 us -> 208 us
  blocking collectives: 59 us -> 22.8 us
  Pallas kernels: 177 us -> 146 us
  local copies, waits for them, and re-layouts: 54.3 us -> 32.2 us
  matrix products: 39.2 us -> 28.8 us
  starting transfers between devices: 25 us -> 35 us
    reduce_scatter x5, waiting for transfers between devices: 436 us -> 0.01 us  [line_scatter(): lax.psum_scatter(value, 'dp', scatter_dimension=0, tiled=True, axis_index...]
    ppermute x10 -> x25, waiting for transfers between devices: 110 us -> 207 us  [the longest x5 149 us: swap_neighbours(): lax.ppermute(theirs, 'dp', [(i, i ^ 1) for i in range(devices)])]
    all_gather x2 -> x0, blocking collectives: 36.5 us -> none  [the longest x1 27 us: per_device(): full_cotangent = lax.all_gather(late_cotangent, 'pipe', axis=1, tiled=True)]
    pallas_call x12 -> x20, Pallas kernels: 177 us -> 146 us  [the longest x18 135 us: run_tick(): pl.pallas_call(functools.partial(kernel, sizes), out_shape=outs, grid_spe...]
    another operation x13 -> x0, local copies, waits for them, and re-layouts: 23.1 us -> none  [the longest x12 22.4 us: tick_scalars(): jnp.stack([jnp.where(active, current, CHUNKS), active.astype(jnp.int32),...]
    unnamed x50 -> x37, local copies, waits for them, and re-layouts: 23.2 us -> 6.67 us
    ppermute x10 -> x25, starting transfers between devices: 13.6 us -> 26.5 us  [the longest x14 13.2 us: per_device(): sent[tick] = lax.ppermute(rounded, 'pipe', route)]
    dot_general x7 -> x5, matrix products: 39.2 us -> 28.8 us  [dot_rows(): lax.dot_general(left, right, (((0,), (0,)), ((), ())), preferred_element_...]
  transfers between devices with their start and end apart: 22 -> 36, of which waited for: 9 -> 6; matrix products, arithmetic and copies ran while one was open for 8% -> 13% of each run, Pallas kernels for 0% -> 22%
where the time goes in v2:
time: 521 us; the launch traced here: 512 us
  waiting for transfers between devices  208 us (40%)
  Pallas kernels  146 us (28%)
  starting transfers between devices  35 us (7%)
  local copies, waits for them, and re-layouts  32.2 us (6%)
  matrix products  28.8 us (6%)
  other arithmetic  24.5 us (5%)
  blocking collectives  22.8 us (4%)
  between operations  15.4 us (3%)
    ppermute x5, waiting for transfers between devices, swap_neighbours(): lax.ppermute(theirs, 'dp', [(i, i ^ 1) for i in range(devices)])  149 us
    pallas_call x18, Pallas kernels, run_tick(): pl.pallas_call(functools.partial(kernel, sizes), out_shape=outs, grid_spe...  135 us
    ppermute x14, waiting for transfers between devices, per_device(): sent[tick] = lax.ppermute(rounded, 'pipe', route)  57.8 us
    dot_general x5, matrix products, dot_rows(): lax.dot_general(left, right, (((0,), (0,)), ((), ())), preferred_element_...  28.8 us
    unnamed x1, blocking collectives  22.8 us
    ppermute x14, starting transfers between devices, per_device(): sent[tick] = lax.ppermute(rounded, 'pipe', route)  13.2 us
  transfers between devices with their start and end apart: 36, of which 6 were waited for; matrix products, arithmetic and copies ran while one was open for 13% of the time, Pallas kernels for 22%

profile of v2, /device:TPU:0, one launch (start us, length us, event | category | flops | bytes accessed | tf_op | source)
XLA Modules:
  0.0 512.2 jit_solution(6194868852453225348)
XLA Ops:
  11.1 6.8 %load_weights.1 = (bf16[960,960]{1,0:T(8,128)(2,1)S(1)}, bf16[320,960]{1,0:T(8,128)(2,1)S(1)}, bf16[320,960]{1,0:T(8,128)(2,1)S(1)}, bf16[960,960]{1,0:T(8,128)(...) custom-call(bf16[960,960]{1,0:T(8,128)(2,1)} %bitcast.125, ...), custom_call_target="tpu_custom_call" | custom-call | tf_op jit(solution)/shard_map/load_weights/pallas_call | solution.py:463
  18.0 4.1 turn_weights.1
  22.2 13.2 %layer_pair_forward.9 = (bf16[128,960]{1,0:T(8,128)(2,1)S(1)}, f32[3,128,960]{2,1,0:T(8,128)}, f32[3,2,128,960]{3,2,1,0:T(8,128)}, bf16[3,2,128,960]{3,2,1,0:T(8...) custom-call(s32[1,4]{1,0:T(1,128)S(1)} %copy-done.6, ...), custom_call_target="tpu_custom_call" | custom-call | flops 5033164800 | bytes 19660800 | tf_op jit(solution)/shard_map/layer_pair_forward/pallas_call | solution.py:524
  39.4 13.7 %layer_pair_forward.10 = (bf16[128,960]{1,0:T(8,128)(2,1)S(1)}, f32[3,128,960]{2,1,0:T(8,128)}, f32[3,2,128,960]{3,2,1,0:T(8,128)}, bf16[3,2,128,960]{3,2,1,0:T(...) custom-call(s32[1,4]{1,0:T(1,128)S(1)} %copy-done.6, ...), custom_call_target="tpu_custom_call", output_to_operand_aliasing={{1}: (16, {}), {2}: (17, {}), {3}: (18, {}), {4}: (19, {}),... | custom-call | flops 5033164800 | bytes 19660800 | tf_op jit(solution)/shard_map/layer_pair_forward/pallas_call | solution.py:524
  54.4 13.3 %layer_pair_forward.11 = (bf16[128,960]{1,0:T(8,128)(2,1)S(1)}, f32[3,128,960]{2,1,0:T(8,128)}, f32[3,2,128,960]{3,2,1,0:T(8,128)}, bf16[3,2,128,960]{3,2,1,0:T(...) custom-call(s32[1,4]{1,0:T(1,128)S(1)} %copy-done.6, ...), custom_call_target="tpu_custom_call", output_to_operand_aliasing={{1}: (17, {}), {2}: (18, {}), {3}: (19, {}), {4}: (20, {}),... | custom-call | flops 5033164800 | bytes 19660800 | tf_op jit(solution)/shard_map/layer_pair_forward/pallas_call | solution.py:524
  70.5 8.2 %layer_pair_forward.13 = (bf16[128,960]{1,0:T(8,128)(2,1)S(1)}, f32[3,128,960]{2,1,0:T(8,128)}, f32[3,2,128,960]{3,2,1,0:T(8,128)}, bf16[3,2,128,960]{3,2,1,0:T(...) custom-call(s32[1,4]{1,0:T(1,128)S(1)} %copy-done.6, ...), custom_call_target="tpu_custom_call", output_to_operand_aliasing={{1}: (13, {}), {2}: (14, {}), {3}: (15, {}), {4}: (16, {}),... | custom-call | flops 5033164800 | bytes 19660800 | tf_op jit(solution)/shard_map/layer_pair_forward/pallas_call | solution.py:524
  82.5 9.7 %layer_pair_forward.16 = (bf16[128,960]{1,0:T(8,128)(2,1)}, f32[3,128,960]{2,1,0:T(8,128)}, f32[3,2,128,960]{3,2,1,0:T(8,128)}, bf16[3,2,128,960]{3,2,1,0:T(8,12...) custom-call(s32[1,4]{1,0:T(1,128)S(1)} %copy-done.6, ...), custom_call_target="tpu_custom_call", output_to_operand_aliasing={{1}: (13, {}), {2}: (14, {}), {3}: (15, {}), {4}: (16, {}),... | custom-call | flops 5033164800 | bytes 19660800 | tf_op jit(solution)/shard_map/layer_pair_forward/pallas_call | solution.py:524
  95.3 9.5 %layer_pair_backward.10 = (bf16[128,960]{1,0:T(8,128)(2,1)S(1)}, f32[3,128,960]{2,1,0:T(8,128)}, bf16[3,2,128,960]{3,2,1,0:T(8,128)(2,1)}, bf16[3,2,128,2560]{3,...) custom-call(s32[1,4]{1,0:T(1,128)S(1)} %copy-done.6, ...), custom_call_target="tpu_custom_call", output_to_operand_aliasing={{1}: (23, {}), {2}: (24, {}), {3}: (25, {}), {4}: (26, {}),... | custom-call | flops 5033164800 | bytes 19660800 | tf_op jit(solution)/shard_map/layer_pair_backward/pallas_call | solution.py:524
  108.6 9.6 %layer_pair_backward.13 = (bf16[128,960]{1,0:T(8,128)(2,1)S(1)}, f32[3,128,960]{2,1,0:T(8,128)}, bf16[3,2,128,960]{3,2,1,0:T(8,128)(2,1)}, bf16[3,2,128,2560]{3,...) custom-call(s32[1,4]{1,0:T(1,128)S(1)} %copy-done.6, ...), custom_call_target="tpu_custom_call", output_to_operand_aliasing={{1}: (20, {}), {2}: (21, {}), {3}: (22, {}), {4}: (23, {}),... | custom-call | flops 5033164800 | bytes 19660800 | tf_op jit(solution)/shard_map/layer_pair_backward/pallas_call | solution.py:524
  121.8 57.8 %collective-permute-done.16.refs_4_ = bf16[128,960]{1,0:T(8,128)(2,1)S(1)} collective-permute-done((bf16[128,960]{1,0:T(8,128)(2,1)S(1)}, bf16[128,960]{1,0:T(8,128)(2,1)S(1)}, u32[]{:S(2)}, u32[]{:S(2)}) %collective-permute-start.16) | collective-permute-done | bytes 245792 | tf_op jit(solution)/shard_map/ppermute | solution.py:748
  179.5 16.2 %layer_pair_backward.15 = (bf16[128,960]{1,0:T(8,128)(2,1)S(1)}, f32[3,128,960]{2,1,0:T(8,128)}, bf16[3,2,128,960]{3,2,1,0:T(8,128)(2,1)}, bf16[3,2,128,2560]{3,...) custom-call(s32[1,4]{1,0:T(1,128)S(1)} %copy-done.6, ...), custom_call_target="tpu_custom_call", output_to_operand_aliasing={{1}: (20, {}), {2}: (21, {}), {3}: (22, {}), {4}: (23, {}),... | custom-call | flops 5033164800 | bytes 19660800 | tf_op jit(solution)/shard_map/layer_pair_backward/pallas_call | solution.py:524
  197.1 17.3 %layer_pair_backward.16 = (bf16[128,960]{1,0:T(8,128)(2,1)}, f32[3,128,960]{2,1,0:T(8,128)}, bf16[3,2,128,960]{3,2,1,0:T(8,128)(2,1)}, bf16[3,2,128,2560]{3,2,1,...) custom-call(s32[1,4]{1,0:T(1,128)S(1)} %copy-done.6, ...), custom_call_target="tpu_custom_call", output_to_operand_aliasing={{1}: (20, {}), {2}: (21, {}), {3}: (22, {}), {4}: (23, {}),... | custom-call | flops 5033164800 | bytes 19660800 | tf_op jit(solution)/shard_map/layer_pair_backward/pallas_call | solution.py:524
  214.4 16.9 %layer_pair_backward.17 = (bf16[128,960]{1,0:T(8,128)(2,1)}, f32[3,128,960]{2,1,0:T(8,128)}, bf16[3,2,128,960]{3,2,1,0:T(8,128)(2,1)}, bf16[3,2,128,2560]{3,2,1,...) custom-call(s32[1,4]{1,0:T(1,128)S(1)} %copy-done.6, ...), custom_call_target="tpu_custom_call", output_to_operand_aliasing={{1}: (20, {}), {2}: (21, {}), {3}: (22, {}), {4}: (23, {}),... | custom-call | flops 5033164800 | bytes 19660800 | tf_op jit(solution)/shard_map/layer_pair_backward/pallas_call | solution.py:524
  231.3 5.5 %concatenate.3 = bf16[768,1600]{1,0:T(8,128)(2,1)} concatenate(bf16[768,960]{1,0:T(8,128)(2,1)} %bitcast.104, bf16[768,320]{1,0:T(8,128)(2,1)} %bitcast.110, bf16[768,320]{1,0:T(8,128)(2,1)} %bitcast.111), dimensions={1} | concatenate | bytes 4915200 | tf_op jit(solution)/shard_map/concatenate | solution.py:758
  236.8 6.3 %convolution_convert_fusion = bf16[960,1600]{1,0:T(8,128)(2,1)} fusion(bf16[768,960]{1,0:T(8,128)(2,1)S(1)} %bitcast.109, bf16[768,1600]{1,0:T(8,128)(2,1)} %concatenate.3), kind=kOutput, calls=%fused_computation.4 | convolution fusion | flops 2360832000 | bytes 7004160 | tf_op jit(solution)/shard_map/dot_general | solution.py:37
  244.5 3.3 bitcast_convert_fusion.3
  250.2 2.9 collective-permute-start.28
  253.1 5.9 %bitcast_convert_fusion = bf16[2560,960]{0,1:T(8,128)(2,1)} fusion(bf16[3,2,128,2560]{3,2,1,0:T(8,128)(2,1)S(1)} %copy-done.7, bf16[3,2,128,960]{3,2,1,0:T(8,128)(2,1)S(1)} %copy-done.12), kind=kOutput, calls=%fused_computation | convolution fusion | flops 3777331200 | bytes 10321920 | tf_op jit(solution)/shard_map/dot_general | solution.py:37
  259.1 7.8 %copy.213 = bf16[2560,960]{1,0:T(8,128)(2,1)} copy(bf16[2560,960]{0,1:T(8,128)(2,1)} %bitcast_convert_fusion) | data formatting | bytes 9830400 | tf_op jit(solution)/shard_map/convert_element_type | solution.py:756
  266.9 3.6 dynamic-slice_bitcast_fusion
  270.5 2.5 bitcast_add_fusion.3
  273.1 50.1 %collective-permute-done.30 = bf16[4,320,960]{2,1,0:T(8,128)(2,1)S(1)} collective-permute-done((bf16[4,320,960]{2,1,0:T(8,128)(2,1)}, bf16[4,320,960]{2,1,0:T(8,128)(2,1)S(1)}, u32[]{:S(2)}, u32[]{:S(2)}) %collective-permute-start.30) | collective-permute-done | bytes 2457632 | tf_op jit(solution)/shard_map/ppermute | solution.py:575
  323.2 3.6 bitcast_add_fusion
  328.2 6.6 %bitcast_convert_fusion.1 = bf16[960,2560]{1,0:T(8,128)(2,1)S(1)} fusion(bf16[3,2,128,960]{3,2,1,0:T(8,128)(2,1)S(1)} %copy-done.11, bf16[3,2,128,2560]{3,2,1,0:T(8,128)(2,1)} %get-tuple-element.443), kind=kOutput, calls=%fused_computation.1 | convolution fusion | flops 3777331200 | bytes 10321920 | tf_op jit(solution)/shard_map/dot_general | solution.py:37
  336.8 48.2 %collective-permute-done.29 = bf16[4,120,2560]{2,1,0:T(8,128)(2,1)S(1)} collective-permute-done((bf16[4,120,2560]{2,1,0:T(8,128)(2,1)S(1)}, bf16[4,120,2560]{2,1,0:T(8,128)(2,1)S(1)}, u32[]{:S(2)}, u32[]{:S(2)}) %collective-permute-start.29) | collective-permute-done | bytes 2457632 | tf_op jit(solution)/shard_map/ppermute | solution.py:575
  386.8 6.7 %bitcast_convert_fusion.2 = bf16[960,2560]{1,0:T(8,128)(2,1)S(1)} fusion(bf16[3,2,128,960]{3,2,1,0:T(8,128)(2,1)S(1)} %copy-done.11, bf16[3,2,128,2560]{3,2,1,0:T(8,128)(2,1)} %get-tuple-element.434), kind=kOutput, calls=%fused_computation.2 | convolution fusion | flops 3777331200 | bytes 10321920 | tf_op jit(solution)/shard_map/dot_general | solution.py:37
  395.7 47.3 %collective-permute-done.20 = bf16[4,120,2560]{2,1,0:T(8,128)(2,1)S(1)} collective-permute-done((bf16[4,120,2560]{2,1,0:T(8,128)(2,1)S(1)}, bf16[4,120,2560]{2,1,0:T(8,128)(2,1)S(1)}, u32[]{:S(2)}, u32[]{:S(2)}) %collective-permute-start.20) | collective-permute-done | bytes 2457632 | tf_op jit(solution)/shard_map/ppermute | solution.py:575
  447.1 2.6 fusion.15
  449.7 2.9 fusion.18
  459.8 22.8 %all-reduce.2 = (f32[960]{0:T(1024)S(1)}, f32[960]{0:T(1024)S(1)}) all-reduce(f32[960]{0:T(1024)S(1)} %bitcast.134, f32[960]{0:T(1024)S(1)} %bitcast.133), channel_id=7, replica_groups=mesh['pipe'=4,'dp'=8] {'dp'}, use_global_device_ids=true, to_apply=%region_6.7.clone | all-reduce | flops 1920 | bytes 15360
  493.1 3.1 collective-permute-done.27
  498.8 2.3 bitcast_convert_fusion.4
  (135 shorter events, 66.6 us)
Async XLA Ops:
  7.2 480.0 %reduce-scatter.8.cloned.1.call-start = ((), (), s32[]{:S(2)}) async-start(), calls=%async_computation.6 | async-start | bytes 3993600 | tf_op jit(solution)/shard_map/reduce_scatter | solution.py:581
  7.2 14.9 %collective-permute-start = (bf16[320,240]{1,0:T(8,128)(2,1)}, bf16[320,240]{1,0:T(8,128)(2,1)S(1)}, u32[]{:S(2)}, u32[]{:S(2)}) collective-permute-start(bf16[320,240]{1,0:T(8,128)(2,1)} %refs_4_.5), channel_id=1, source_target_pairs={{8,0},{9,1},{10,2},{11,3},{12,4},{13,5},{14,6},{15,7}} | collective-permute-start | bytes 460808 | tf_op jit(solution)/shard_map/ppermute | solution.py:565
  8.5 13.6 %collective-permute-start.1 = (bf16[320,240]{1,0:T(8,128)(2,1)}, bf16[320,240]{1,0:T(8,128)(2,1)S(1)}, u32[]{:S(2)}, u32[]{:S(2)}) collective-permute-start(bf16[320,240]{1,0:T(8,128)(2,1)} %refs_4_.5), channel_id=1, source_target_pairs={{16,0},{17,1},{18,2},{19,3},{20,4},{21,5},{22,6},{23,7}} | collective-permute-start | bytes 460808 | tf_op jit(solution)/shard_map/ppermute | solution.py:565
  9.8 12.3 %collective-permute-start.2 = (bf16[320,240]{1,0:T(8,128)(2,1)}, bf16[320,240]{1,0:T(8,128)(2,1)S(1)}, u32[]{:S(2)}, u32[]{:S(2)}) collective-permute-start(bf16[320,240]{1,0:T(8,128)(2,1)} %refs_4_.5), channel_id=1, source_target_pairs={{24,0},{25,1},{26,2},{27,3},{28,4},{29,5},{30,6},{31,7}} | collective-permute-start | bytes 460808 | tf_op jit(solution)/shard_map/ppermute | solution.py:565
  35.4 19.0 %collective-permute-start.3 = (bf16[128,960]{1,0:T(8,128)(2,1)S(1)}, bf16[128,960]{1,0:T(8,128)(2,1)S(1)}, u32[]{:S(2)}, u32[]{:S(2)}) collective-permute-start(bf16[128,960]{1,0:T(8,128)(2,1)S(1)} %get-tuple-element.236), channel_id=1, source_target_pairs={{0,8},{1,9},{2,10},{3,11},{4,12},{5,13},{6,14},{7,15}} | collective-permute-start | bytes 737288 | tf_op jit(solution)/shard_map/ppermute | solution.py:691
  36.7 56.9 %collective-permute-start.10 = (bf16[320,240]{1,0:T(8,128)(2,1)S(1)}, bf16[320,240]{1,0:T(8,128)(2,1)S(1)}, u32[]{:S(2)}, u32[]{:S(2)}) collective-permute-start(bf16[320,240]{1,0:T(8,128)(2,1)S(1)} %copy-done.2), channel_id=1, source_target_pairs={{0,24},{1,25},{2,26},{3,27},{4,28},{5,29},{6,30},{7,31}} | collective-permute-start | bytes 460808 | tf_op jit(solution)/shard_map/ppermute | solution.py:565
  38.0 55.6 %collective-permute-start.11 = (bf16[320,240]{1,0:T(8,128)(2,1)S(1)}, bf16[320,240]{1,0:T(8,128)(2,1)S(1)}, u32[]{:S(2)}, u32[]{:S(2)}) collective-permute-start(bf16[320,240]{1,0:T(8,128)(2,1)S(1)} %copy-done.2), channel_id=1, source_target_pairs={{8,24},{9,25},{10,26},{11,27},{12,28},{13,29},{14,30},{15,31}} | collective-permute-start | bytes 460808 | tf_op jit(solution)/shard_map/ppermute | solution.py:565
  38.7 55.0 %collective-permute-start.12 = (bf16[320,240]{1,0:T(8,128)(2,1)S(1)}, bf16[320,240]{1,0:T(8,128)(2,1)S(1)}, u32[]{:S(2)}, u32[]{:S(2)}) collective-permute-start(bf16[320,240]{1,0:T(8,128)(2,1)S(1)} %copy-done.2), channel_id=1, source_target_pairs={{16,24},{17,25},{18,26},{19,27},{20,28},{21,29},{22,30},{23,31}} | collective-permute-start | bytes 460808 | tf_op jit(solution)/shard_map/ppermute | solution.py:565
  53.1 15.9 %collective-permute-start.5 = (bf16[128,960]{1,0:T(8,128)(2,1)S(1)}, bf16[128,960]{1,0:T(8,128)(2,1)S(1)}, u32[]{:S(2)}, u32[]{:S(2)}) collective-permute-start(bf16[128,960]{1,0:T(8,128)(2,1)S(1)} %get-tuple-element.262), channel_id=1, source_target_pairs={{0,8},{1,9},{2,10},{3,11},{4,12},{5,13},{6,14},{7,15}} | collective-permute-start | bytes 737288 | tf_op jit(solution)/shard_map/ppermute | solution.py:691
  67.7 2.8 collective-permute-start.4
  69.8 9.6 %collective-permute-start.7 = (bf16[128,960]{1,0:T(8,128)(2,1)S(1)}, bf16[128,960]{1,0:T(8,128)(2,1)S(1)}, u32[]{:S(2)}, u32[]{:S(2)}) collective-permute-start(bf16[128,960]{1,0:T(8,128)(2,1)S(1)} %get-tuple-element.288), channel_id=1, source_target_pairs={{8,16},{9,17},{10,18},{11,19},{12,20},{13,21},{14,22},{15,23}} | collective-permute-start | bytes 737288 | tf_op jit(solution)/shard_map/ppermute | solution.py:691
  81.8 10.4 %collective-permute-start.8 = (bf16[128,960]{1,0:T(8,128)(2,1)S(1)}, bf16[128,960]{1,0:T(8,128)(2,1)S(1)}, u32[]{:S(2)}, u32[]{:S(2)}) collective-permute-start(bf16[128,960]{1,0:T(8,128)(2,1)S(1)} %get-tuple-element.313), channel_id=1, source_target_pairs={{16,24},{17,25},{18,26},{19,27},{20,28},{21,29},{22,30},{23,31}} | collective-permute-start | bytes 737288 | tf_op jit(solution)/shard_map/ppermute | solution.py:691
  94.6 10.9 %collective-permute-start.13 = (bf16[128,960]{1,0:T(8,128)(2,1)S(1)}, bf16[128,960]{1,0:T(8,128)(2,1)S(1)}, u32[]{:S(2)}, u32[]{:S(2)}) collective-permute-start(bf16[128,960]{1,0:T(8,128)(2,1)S(1)} %get-tuple-element.353), channel_id=1, source_target_pairs={{24,16},{25,17},{26,18},{27,19},{28,20},{29,21},{30,22},{31,23}} | collective-permute-start | bytes 737288 | tf_op jit(solution)/shard_map/ppermute | solution.py:748
  107.9 11.6 %collective-permute-start.17 = (bf16[128,960]{1,0:T(8,128)(2,1)S(1)}, bf16[128,960]{1,0:T(8,128)(2,1)S(1)}, u32[]{:S(2)}, u32[]{:S(2)}) collective-permute-start(bf16[128,960]{1,0:T(8,128)(2,1)S(1)} %get-tuple-element.393), channel_id=1, source_target_pairs={{16,8},{17,9},{18,10},{19,11},{20,12},{21,13},{22,14},{23,15}} | collective-permute-start | bytes 737288 | tf_op jit(solution)/shard_map/ppermute | solution.py:748
  118.3 61.3 %collective-permute-start.16 = (bf16[128,960]{1,0:T(8,128)(2,1)S(1)}, bf16[128,960]{1,0:T(8,128)(2,1)S(1)}, u32[]{:S(2)}, u32[]{:S(2)}) collective-permute-start(bf16[128,960]{1,0:T(8,128)(2,1)S(1)} %get-tuple-element.392), channel_id=1, source_target_pairs={{8,0},{16,8},{9,1},{17,9},{10,2},{18,10},{11,3},{19,11},{12,4},{20... | collective-permute-start | bytes 737288 | tf_op jit(solution)/shard_map/ppermute | solution.py:748
  120.5 76.6 %collective-permute-start.19 = (bf16[128,960]{1,0:T(8,128)(2,1)S(1)}, bf16[128,960]{1,0:T(8,128)(2,1)S(1)}, u32[]{:S(2)}, u32[]{:S(2)}) collective-permute-start(bf16[128,960]{1,0:T(8,128)(2,1)S(1)} %get-tuple-element.413), channel_id=1, source_target_pairs={{8,0},{9,1},{10,2},{11,3},{12,4},{13,5},{14,6},{15,7}} | collective-permute-start | bytes 737288 | tf_op jit(solution)/shard_map/ppermute | solution.py:748
  195.7 18.7 %collective-permute-start.18 = (bf16[128,960]{1,0:T(8,128)(2,1)S(1)}, bf16[128,960]{1,0:T(8,128)(2,1)S(1)}, u32[]{:S(2)}, u32[]{:S(2)}) collective-permute-start(bf16[128,960]{1,0:T(8,128)(2,1)S(1)} %get-tuple-element.412), channel_id=1, source_target_pairs={{8,0},{9,1},{10,2},{11,3},{12,4},{13,5},{14,6},{15,7}} | collective-permute-start | bytes 737288 | tf_op jit(solution)/shard_map/ppermute | solution.py:748
  243.1 248.2 %reduce-scatter.10.cloned.1.call-start = ((), (), s32[]{:S(2)}) async-start(), calls=%async_computation.7 | async-start | bytes 1228800 | tf_op jit(solution)/shard_map/reduce_scatter | solution.py:581
  250.2 20.3 %collective-permute-start.28 = (bf16[4,120,960]{2,1,0:T(8,128)(2,1)}, bf16[4,120,960]{2,1,0:T(8,128)(2,1)}, u32[]{:S(2)}, u32[]{:S(2)}) collective-permute-start(bf16[4,120,960]{2,1,0:T(8,128)(2,1)} %dynamic-slice_bitcast_fusion.3), channel_id=1, source_target_pairs={{0,1},{1,0},{2,3},{3,2},{4,5},{5,4},{6,7},{7,6},{8,9},{9,8},{10,11... | collective-permute-start | bytes 2764808 | tf_op jit(solution)/shard_map/ppermute | solution.py:575
  270.5 52.7 %collective-permute-start.30 = (bf16[4,320,960]{2,1,0:T(8,128)(2,1)}, bf16[4,320,960]{2,1,0:T(8,128)(2,1)S(1)}, u32[]{:S(2)}, u32[]{:S(2)}) collective-permute-start(bf16[4,320,960]{2,1,0:T(8,128)(2,1)} %dynamic-slice_bitcast_fusion), channel_id=1, source_target_pairs={{0,1},{1,0},{2,3},{3,2},{4,5},{5,4},{6,7},{7,6},{8,9},{9,8},{10,11... | collective-permute-start | bytes 7372808 | tf_op jit(solution)/shard_map/ppermute | solution.py:575
  273.1 225.7 %reduce-scatter.14.cloned.1.call-start = ((), (), s32[]{:S(2)}) async-start(), calls=%async_computation.9 | async-start | bytes 3276800 | tf_op jit(solution)/shard_map/reduce_scatter | solution.py:581
  326.8 174.3 %reduce-scatter.12.cloned.1.call-start = ((), (), s32[]{:S(2)}) async-start(), calls=%async_computation.8 | async-start | bytes 3072000 | tf_op jit(solution)/shard_map/reduce_scatter | solution.py:581
  335.0 50.0 %collective-permute-start.29 = (bf16[4,120,2560]{2,1,0:T(8,128)(2,1)S(1)}, bf16[4,120,2560]{2,1,0:T(8,128)(2,1)S(1)}, u32[]{:S(2)}, u32[]{:S(2)}) collective-permute-start(bf16[4,120,2560]{2,1,0:T(8,128)(2,1)S(1)} %dynamic-slice_bitcast_fusion.1), channel_id=1, source_target_pairs={{0,1},{1,0},{2,3},{3,2},{4,5},{5,4},{6,7},{7,6},{8,9},{9,8},{10,11... | collective-permute-start | bytes 7372808 | tf_op jit(solution)/shard_map/ppermute | solution.py:575
  386.8 116.5 %reduce-scatter.6.cloned.1.call-start = ((), (), s32[]{:S(2)}) async-start(), calls=%async_computation.5 | async-start | bytes 3072000 | tf_op jit(solution)/shard_map/reduce_scatter | solution.py:581
  393.7 49.3 %collective-permute-start.20 = (bf16[4,120,2560]{2,1,0:T(8,128)(2,1)S(1)}, bf16[4,120,2560]{2,1,0:T(8,128)(2,1)S(1)}, u32[]{:S(2)}, u32[]{:S(2)}) collective-permute-start(bf16[4,120,2560]{2,1,0:T(8,128)(2,1)S(1)} %dynamic-slice_bitcast_fusion.2), channel_id=1, source_target_pairs={{0,1},{1,0},{2,3},{3,2},{4,5},{5,4},{6,7},{7,6},{8,9},{9,8},{10,11... | collective-permute-start | bytes 7372808 | tf_op jit(solution)/shard_map/ppermute | solution.py:575
  452.6 35.8 %collective-permute-start.24 = (f32[320,240]{1,0:T(8,128)}, f32[320,240]{1,0:T(8,128)S(1)}, u32[]{:S(2)}, u32[]{:S(2)}) collective-permute-start(f32[320,240]{1,0:T(8,128)} %get-tuple-element.471), channel_id=1, source_target_pairs={{0,8},{1,9},{2,10},{3,11},{4,12},{5,13},{6,14},{7,15}} | collective-permute-start | bytes 921608 | tf_op jit(solution)/shard_map/ppermute | solution.py:780
  453.9 34.5 %collective-permute-start.25 = (f32[320,240]{1,0:T(8,128)}, f32[320,240]{1,0:T(8,128)S(1)}, u32[]{:S(2)}, u32[]{:S(2)}) collective-permute-start(f32[320,240]{1,0:T(8,128)} %get-tuple-element.473), channel_id=1, source_target_pairs={{0,16},{1,17},{2,18},{3,19},{4,20},{5,21},{6,22},{7,23}} | collective-permute-start | bytes 921608 | tf_op jit(solution)/shard_map/ppermute | solution.py:780
  456.3 26.8 %collective-permute-start.21 = (f32[320,240]{1,0:T(8,128)}, f32[320,240]{1,0:T(8,128)S(1)}, u32[]{:S(2)}, u32[]{:S(2)}) collective-permute-start(f32[320,240]{1,0:T(8,128)} %get-tuple-element.474), channel_id=1, source_target_pairs={{24,0},{25,1},{26,2},{27,3},{28,4},{29,5},{30,6},{31,7}} | collective-permute-start | bytes 921608 | tf_op jit(solution)/shard_map/ppermute | solution.py:780
  457.6 27.6 %collective-permute-start.22 = (f32[320,240]{1,0:T(8,128)}, f32[320,240]{1,0:T(8,128)S(1)}, u32[]{:S(2)}, u32[]{:S(2)}) collective-permute-start(f32[320,240]{1,0:T(8,128)} %get-tuple-element.476), channel_id=1, source_target_pairs={{24,8},{25,9},{26,10},{27,11},{28,12},{29,13},{30,14},{31,15}} | collective-permute-start | bytes 921608 | tf_op jit(solution)/shard_map/ppermute | solution.py:780
  458.3 26.9 %collective-permute-start.23 = (f32[320,240]{1,0:T(8,128)}, f32[320,240]{1,0:T(8,128)}, u32[]{:S(2)}, u32[]{:S(2)}) collective-permute-start(f32[320,240]{1,0:T(8,128)} %get-tuple-element.475), channel_id=1, source_target_pairs={{24,16},{25,17},{26,18},{27,19},{28,20},{29,21},{30,22},{31,23}} | collective-permute-start | bytes 921608 | tf_op jit(solution)/shard_map/ppermute | solution.py:780
  483.1 6.3 %collective-permute-start.26 = (f32[320,240]{1,0:T(8,128)}, f32[320,240]{1,0:T(8,128)}, u32[]{:S(2)}, u32[]{:S(2)}) collective-permute-start(f32[320,240]{1,0:T(8,128)} %get-tuple-element.472), channel_id=1, source_target_pairs={{0,24},{1,25},{2,26},{3,27},{4,28},{5,29},{6,30},{7,31}} | collective-permute-start | bytes 921608 | tf_op jit(solution)/shard_map/ppermute | solution.py:780
  488.3 7.9 %collective-permute-start.27 = (bf16[120,1600]{1,0:T(8,128)(2,1)S(1)}, bf16[120,1600]{1,0:T(8,128)(2,1)S(1)}, u32[]{:S(2)}, u32[]{:S(2)}) collective-permute-start(bf16[120,1600]{1,0:T(8,128)(2,1)S(1)} %dynamic-slice_bitcast_fusion.4), channel_id=1, source_target_pairs={{0,1},{1,0},{2,3},{3,2},{4,5},{5,4},{6,7},{7,6},{8,9},{9,8},{10,11... | collective-permute-start | bytes 1152008 | tf_op jit(solution)/shard_map/ppermute | solution.py:575
  (21 other events, 110.7 us)
Sparse Core Ops, SparseCore 0:
  243.3 62.9 reduce-scatter.7
  309.2 26.1 reduce-scatter.9
  337.8 50.6 reduce-scatter.13
  390.7 49.2 reduce-scatter.11
  444.8 49.7 reduce-scatter.5

commit v3 on v2

v3 whole, which is shorter than its diff:
```python
import functools

import jax
import jax.numpy as jnp
import numpy as np
from jax import lax
from jax.experimental import pallas as pl
from jax.experimental.layout import Layout, with_layout_constraint
from jax.experimental.pallas import tpu as pltpu
from jax.sharding import PartitionSpec as P

HEAD_DIM = 64
HALF = HEAD_DIM // 2
LANES = 128
MICRO = 4
CHUNKS = 3
SCALE = HEAD_DIM**-0.5
BF16 = jnp.bfloat16
F32 = jnp.float32

epsilon = 1e-05
rope_base = 10000.0
masked_score = -1e30

def round_up(value, multiple):
    return -(-value // multiple) * multiple


def dot(left, right):
    return jnp.dot(left, right, preferred_element_type=F32)


def dot_t(left, right):
    return lax.dot_general(left, right, (((1,), (1,)), ((), ())), preferred_element_type=F32)


def dot_rows(left, right):
    return lax.dot_general(left, right, (((0,), (0,)), ((), ())), preferred_element_type=F32)


def lane_ids(rows):
    return lax.broadcasted_iota(jnp.int32, (rows, LANES), 1)


def in_low_half(rows):
    return lane_ids(rows) < HEAD_DIM


def rotate(slab, cosine, signed_sine):
    first = (lane_ids(slab.shape[0]) % HEAD_DIM) < HALF
    partner = jnp.where(
        first, pltpu.roll(slab, LANES - HALF, 1), pltpu.roll(slab, HALF, 1)
    )
    return slab * cosine + partner * signed_sine


def both_halves(slab, upper):
    swapped = pltpu.roll(slab, HEAD_DIM, 1)
    low = in_low_half(slab.shape[0])
    return jnp.where(low, swapped, slab) if upper else jnp.where(low, slab, swapped)


def sort_halves(slab, j, low, heads, kv_heads, key_rows, queries, keys, values):
    for head in (2 * j, 2 * j + 1):
        upper = head % 2 == 1
        if head < heads:
            kept = jnp.where(low, 0.0, slab) if upper else jnp.where(low, slab, 0.0)
            queries.append(kept.astype(BF16))
        elif head < heads + kv_heads:
            keys.append(pad_rows(both_halves(slab, upper).astype(BF16), key_rows))
        elif head < heads + 2 * kv_heads:
            values.append(pad_rows(both_halves(slab, upper).astype(BF16), key_rows))


def reciprocal_rms(value):
    return lax.rsqrt(jnp.mean(value * value, axis=-1, keepdims=True) + epsilon)


class Tick:
    def __init__(self, sizes, lengths):
        sections, depth_step, segment = sizes["sections"], sizes["depth_step"], sizes["rows"] // 2
        section = lax.axis_index("pipe")
        depth = sections - 1 - section if sizes["backward"] else section
        chunk = sizes["tick"] - depth_step * depth
        self.active = (chunk >= 0) & (chunk < CHUNKS)
        self.slot = jnp.clip(chunk, 0, CHUNKS - 1)
        self.edge = depth == 0
        self.final = depth == sections - 1
        self.is_long = self.slot == 0
        self.table = jnp.where(self.is_long, 1, 0)
        self.first_length = jnp.where(
            self.is_long, lengths[0, 0], jnp.where(self.slot == 1, lengths[0, 1], lengths[0, 3])
        )
        self.second_length = jnp.where(self.slot == 1, lengths[0, 2], segment)

    def bound(self, position, segment):
        return jnp.where(
            self.is_long,
            self.first_length,
            jnp.where(position < segment, self.first_length, self.second_length + segment),
        )


def score_bias(tick, query_rows, key_rows):
    query = lax.broadcasted_iota(jnp.int32, (query_rows, key_rows), 0)
    key = lax.broadcasted_iota(jnp.int32, (query_rows, key_rows), 1)
    segment = key_rows // 2
    start = jnp.where(tick.is_long, 0, jnp.where(query < segment, 0, segment))
    allowed = (key <= query) & (key < tick.bound(key, segment)) & (key >= start)
    return jnp.where(allowed, 0.0, masked_score).astype(F32)


def assemble(target, parts, at):
    count = min(target.shape[0], parts[0].shape[0] - at)
    target[:count, :] = jnp.concatenate(
        [part[at : at + count, :].astype(F32) for part in parts], axis=1
    )


def kept_at(kind, buffer, array, app, slot, rows, chunk, columns=None):
    columns = pl.ds(0, buffer.shape[-1]) if columns is None else columns
    if kind == "gains":
        return buffer.at[app], array.at[slot, app]
    if kind == "probs":
        taken = pl.ds(0, buffer.shape[2] * rows // chunk)
        return buffer.at[app, :, taken], array.at[slot, app, :, taken]
    at = pl.ds(pl.multiple_of(slot * chunk, chunk), rows)
    if kind == "slopes":
        return buffer.at[app, :, pl.ds(0, rows), columns], array.at[app, :, at, columns]
    return buffer.at[app, pl.ds(0, rows), columns], array.at[app, at, columns]


def chunk_sizes(sizes):
    full, total = sizes["rows"], sizes["total_rows"]
    found = {}
    for depth in range(sizes["sections"]):
        slot = sizes["tick"] - sizes["depth_step"] * depth
        if 0 <= slot < CHUNKS:
            found.setdefault(min(full, total - slot * full), []).append(slot)
    return found


def pad_rows(value, rows):
    missing = rows - value.shape[0]
    if not missing:
        return value
    return jnp.concatenate([value, jnp.zeros((missing, value.shape[1]), value.dtype)], axis=0)


def when(condition, action):
    pl.when(condition)(action)


def run_active(tick, sizes, run):
    found = chunk_sizes(sizes)
    for rows, slots in found.items():
        mine = functools.reduce(jnp.logical_or, [tick.slot == slot for slot in slots])
        when(tick.active & mine, functools.partial(run, rows))


def final_at(rows_s, array, slot, rows):
    chunk = rows_s.shape[0]
    at = pl.ds(pl.multiple_of(slot * chunk, chunk), rows)
    return rows_s.at[pl.ds(0, rows)], array.at[at]


def forward_kernel(sizes, lengths, *refs):
    tick = Tick(sizes, lengths)
    refs = list(refs)

    def take(count):
        taken = refs[:count]
        del refs[:count]
        return taken

    cosine_ref, sine_ref, gain_attn, gain_mlp = take(4)
    edge_parts, inbound = take(sizes["edge_parts"]), take(sizes["inbound"])
    w_heads, wp, wg, wu, wd = take(5)
    take(sizes["aliased"])
    out_round, out_full = take(2)
    stores = take(sizes["stores"])
    hidden_s, heads_s = take(2)
    buffers = take(sizes["stores"])
    (
        hidden_b,
        normed_attn_b,
        heads_b,
        probs_b,
        mixed_b,
        middle_b,
        normed_mlp_b,
        slopes_b,
        inner_b,
    ) = buffers
    store_sems, final_sem = refs
    chunk, width = hidden_s.shape
    heads = width // HEAD_DIM
    all_width = w_heads.shape[1]
    kv_heads = (all_width // HEAD_DIM - heads) // 2
    share = heads // kv_heads
    ff = wg.shape[1]
    slot = tick.slot

    step = sizes["ff_step"]

    def store(buffer, app, rows, part=None):
        i = [other is buffer for other in buffers].index(True)
        columns = None if part is None else pl.ds(part * step, step)
        source, target = kept_at(
            sizes["store_kinds"][i], buffer, stores[i], app, slot, rows, chunk, columns
        )
        return pltpu.make_async_copy(source, target, store_sems.at[i, app, part or 0])

    def apply(rows, app, carry):
        hidden = hidden_s[:rows]
        hidden_b[app, :rows] = hidden
        store(hidden_b, app, rows).start()
        normed = (hidden * reciprocal_rms(hidden) * gain_attn[...]).astype(BF16)
        normed_attn_b[app, :rows] = normed
        store(normed_attn_b, app, rows).start()
        heads_s[:rows, :all_width] = dot(normed, w_heads[...])
        cosine = cosine_ref[tick.table, :rows]
        sine = sine_ref[tick.table, :rows]
        low = in_low_half(rows)
        query_parts, keys, values = [], [], []
        for j in range(heads_s.shape[1] // LANES):
            slab = heads_s[:rows, j * LANES : (j + 1) * LANES]
            if 2 * j < heads + kv_heads:
                slab = rotate(slab, cosine, sine)
            heads_b[app, :rows, j * LANES : (j + 1) * LANES] = slab.astype(BF16)
            sort_halves(slab, j, low, heads, kv_heads, chunk, query_parts, keys, values)
        store(heads_b, app, rows).start()
        bias = score_bias(tick, rows, chunk)
        bias = jnp.concatenate([bias] * share, axis=0)
        mixed_parts = []
        for kv in range(kv_heads):
            grouped = jnp.concatenate(query_parts[kv * share : (kv + 1) * share], axis=0)
            scores = dot_t(grouped, keys[kv]) * SCALE + bias
            exponent = jnp.exp(scores - jnp.max(scores, axis=-1, keepdims=True))
            total = jnp.sum(exponent, axis=-1, keepdims=True)
            probs = (exponent * (1.0 / total)).astype(BF16)
            probs_b[app, kv, : share * rows] = probs
            mixed = dot(probs, values[kv])
            mixed_parts += [mixed[i * rows : (i + 1) * rows] for i in range(share)]
        store(probs_b, app, rows).start()
        for j in range(heads // 2):
            mixed_b[app, :rows, j * LANES : (j + 1) * LANES] = jnp.where(
                low, mixed_parts[2 * j], mixed_parts[2 * j + 1]
            ).astype(BF16)
        if heads % 2:
            mixed_b[app, :rows, width - HEAD_DIM :] = mixed_parts[-1][:, :HEAD_DIM].astype(BF16)
        store(mixed_b, app, rows).start()
        middle = hidden + dot(mixed_b[app, :rows], wp[...])
        middle_b[app, :rows] = middle
        store(middle_b, app, rows).start()
        normed = (middle * reciprocal_rms(middle) * gain_mlp[...]).astype(BF16)
        normed_mlp_b[app, :rows] = normed
        store(normed_mlp_b, app, rows).start()
        for part, at in enumerate(range(0, ff, step)):
            gate = dot(normed, wg[:, at : at + step])
            up = dot(normed, wu[:, at : at + step])
            sigma = 1.0 / (1.0 + jnp.exp(-gate))
            silu = gate * sigma
            inner_b[app, :rows, at : at + step] = (silu * up).astype(BF16)
            slopes_b[app, 0, :rows, at : at + step] = (
                up * (sigma * (1.0 + gate * (1.0 - sigma)))
            ).astype(BF16)
            slopes_b[app, 1, :rows, at : at + step] = silu.astype(BF16)
            store(inner_b, app, rows, part).start()
            store(slopes_b, app, rows, part).start()
        hidden_s[:rows] = middle + dot(inner_b[app, :rows], wd[...])
        return carry

    def run(rows):
        if edge_parts:

            @pl.when(tick.edge)
            def _():
                assemble(hidden_s, edge_parts, sizes["tick"] * chunk)

        if inbound:

            @pl.when(jnp.logical_not(tick.edge))
            def _():
                hidden_s[:rows] = inbound[0][:rows].astype(F32)

        heads_s[:, heads_s.shape[1] - LANES :] = jnp.zeros((chunk, LANES), F32)
        lax.fori_loop(0, 2, functools.partial(apply, rows), 0)
        out_round[:rows] = hidden_s[:rows].astype(BF16)
        source, target = final_at(hidden_s, out_full, slot, rows)
        final = pltpu.make_async_copy(source, target, final_sem.at[0])
        when(tick.final, final.start)
        for app in (0, 1):
            for buffer in buffers[:-2]:
                store(buffer, app, rows).wait()
            for part in range(ff // step):
                store(inner_b, app, rows, part).wait()
                store(slopes_b, app, rows, part).wait()
        when(tick.final, final.wait)

    run_active(tick, sizes, run)


def backward_kernel(sizes, lengths, *refs):
    tick = Tick(sizes, lengths)
    refs = list(refs)

    def take(count):
        taken = refs[:count]
        del refs[:count]
        return taken

    cosine_ref, sine_ref, gain_attn, gain_mlp = take(4)
    edge_parts, inbound = take(sizes["edge_parts"]), take(sizes["inbound"])
    w_heads, wp, wg, wu, wd = take(5)
    saved = take(sizes["reads"])
    take(sizes["aliased"])
    out_round, out_full = take(2)
    stores = take(sizes["stores"])
    grad_s, mixed_s, inner_s = take(3)
    kept = take(sizes["reads"])
    hidden_k, heads_k, probs_k, middle_k, slopes_k = kept
    buffers = take(sizes["stores"])
    branch_b, gate_b, up_b, attn_b, heads_b, gains_b = buffers
    read_sems, store_sems, final_sem = refs
    chunk, width = grad_s.shape
    heads = width // HEAD_DIM
    all_width = w_heads.shape[0]
    kv_heads = (all_width // HEAD_DIM - heads) // 2
    share = heads // kv_heads
    ff = wd.shape[1]
    slot = tick.slot

    def read(buffer, app, rows):
        i = [other is buffer for other in kept].index(True)
        kind = sizes["read_kinds"][i]
        target, source = kept_at(kind, buffer, saved[i], app, slot, rows, chunk)
        return pltpu.make_async_copy(source, target, read_sems.at[i, app])

    def store(buffer, app, rows):
        i = [other is buffer for other in buffers].index(True)
        kind = sizes["store_kinds"][i]
        source, target = kept_at(kind, buffer, stores[i], app, slot, rows, chunk)
        return pltpu.make_async_copy(source, target, store_sems.at[i, app, 0])

    def rms_backward(value, gain, grad, running):
        scale = reciprocal_rms(value)
        unit = value * scale
        pulled = grad * gain
        gain_terms = grad * unit
        gain_rows = jnp.sum(gain_terms.reshape(grad.shape[0] // 8, 8, width), axis=0)
        shared = jnp.mean(gain_terms * gain, axis=-1, keepdims=True)
        return running + scale * (pulled - unit * shared), gain_rows

    def apply(rows, step_id, carry):
        app = 1 - step_id
        low = in_low_half(rows)
        grad_top = grad_s[:rows]
        branch = grad_top.astype(BF16)
        branch_b[app, :rows] = branch
        store(branch_b, app, rows).start()
        step = sizes["ff_step"]
        inner_s[:rows] = dot(branch, wd[...])
        read(slopes_k, app, rows).wait()
        for at in range(0, ff, step):
            inner_grad = inner_s[:rows, at : at + step]
            gate_b[app, :rows, at : at + step] = (
                inner_grad * slopes_k[app, 0, :rows, at : at + step].astype(F32)
            ).astype(BF16)
            up_b[app, :rows, at : at + step] = (
                inner_grad * slopes_k[app, 1, :rows, at : at + step].astype(F32)
            ).astype(BF16)
        store(gate_b, app, rows).start()
        store(up_b, app, rows).start()
        pulled = dot(gate_b[app, :rows], wg[...])
        pulled += dot(up_b[app, :rows], wu[...])
        read(middle_k, app, rows).wait()
        middle_grad, gain_rows = rms_backward(
            middle_k[app, :rows], gain_mlp[...], pulled, grad_top
        )
        gains_b[app, 1] = gain_rows
        attn_grad = middle_grad.astype(BF16)
        attn_b[app, :rows] = attn_grad
        store(attn_b, app, rows).start()
        mixed_s[:rows, :width] = dot(attn_grad, wp[...])
        mixed_parts, query_parts, keys, values = [], [], [], []
        for j in range(mixed_s.shape[1] // LANES):
            slab = mixed_s[:rows, j * LANES : (j + 1) * LANES]
            mixed_parts.append(jnp.where(low, slab, 0.0).astype(BF16))
            mixed_parts.append(jnp.where(low, 0.0, slab).astype(BF16))
        read(heads_k, app, rows).wait()
        for j in range(heads_k.shape[-1] // LANES):
            slab = heads_k[app, :rows, j * LANES : (j + 1) * LANES].astype(F32)
            sort_halves(slab, j, low, heads, kv_heads, chunk, query_parts, keys, values)
        cosine = cosine_ref[tick.table, :rows]
        sine = -sine_ref[tick.table, :rows]
        ones = jnp.ones((chunk, LANES), BF16)
        query_grads, key_grads, value_grads = [], [], []
        read(probs_k, app, rows).wait()
        for kv in range(kv_heads):
            mixed = jnp.concatenate(mixed_parts[kv * share : (kv + 1) * share], axis=0)
            grouped = jnp.concatenate(query_parts[kv * share : (kv + 1) * share], axis=0)
            probs = probs_k[app, kv, : share * rows]
            probs_wide = probs.astype(F32)
            probs_grad = dot_t(mixed, values[kv])
            weighted = probs_wide * probs_grad
            shared = dot(weighted.astype(BF16), ones)
            score_grad = (weighted - probs_wide * shared).astype(BF16)
            pulled = dot(score_grad, keys[kv])
            query_grads += [pulled[i * rows : (i + 1) * rows] for i in range(share)]
            pulled = dot_rows(score_grad, grouped)[:rows]
            key_grads.append(pulled + pltpu.roll(pulled, HEAD_DIM, 1))
            pulled = dot_rows(probs, mixed)[:rows]
            value_grads.append(pulled + pltpu.roll(pulled, HEAD_DIM, 1))

        parts = query_grads + key_grads + value_grads
        for j in range(len(parts) // 2):
            slab = jnp.where(low, parts[2 * j], parts[2 * j + 1])
            if 2 * j < heads + kv_heads:
                slab = rotate(slab * SCALE, cosine, sine)
            heads_b[app, :rows, j * LANES : (j + 1) * LANES] = slab.astype(BF16)
        if len(parts) % 2:
            heads_b[app, :rows, all_width - HEAD_DIM :] = parts[-1][:, :HEAD_DIM].astype(BF16)
        store(heads_b, app, rows).start()
        pulled = dot(heads_b[app, :rows], w_heads[...])
        read(hidden_k, app, rows).wait()
        result, gain_rows = rms_backward(
            hidden_k[app, :rows], gain_attn[...], pulled, middle_grad
        )
        gains_b[app, 0] = gain_rows
        store(gains_b, app, rows).start()
        grad_s[:rows] = result
        return carry

    def run(rows):
        for app in (1, 0):
            for buffer in (slopes_k, middle_k, heads_k, probs_k, hidden_k):
                read(buffer, app, rows).start()
        if edge_parts:

            @pl.when(tick.edge)
            def _():
                assemble(grad_s, edge_parts, sizes["tick"] * chunk)
                row = lax.broadcasted_iota(jnp.int32, (chunk, 1), 0)
                grad_s[...] = jnp.where(row < tick.bound(row, chunk // 2), grad_s[...], 0.0)

        if inbound:

            @pl.when(jnp.logical_not(tick.edge))
            def _():
                grad_s[:rows] = inbound[0][:rows].astype(F32)

        mixed_s[:, mixed_s.shape[1] - LANES :] = jnp.zeros((chunk, LANES), F32)
        lax.fori_loop(0, 2, functools.partial(apply, rows), 0)
        out_round[:rows] = grad_s[:rows].astype(BF16)
        source, target = final_at(grad_s, out_full, slot, rows)
        final = pltpu.make_async_copy(source, target, final_sem.at[0])
        when(tick.final, final.start)
        for buffer in buffers:
            store(buffer, 0, rows).wait()
            store(buffer, 1, rows).wait()
        when(tick.final, final.wait)

    run_active(tick, sizes, run)


def transpose_to(target, source):
    for at in range(0, source.shape[1], 256):
        end = min(at + 256, source.shape[1])
        target[at:end, :] = jnp.transpose(source[:, at:end])


def load_kernel(extras, *refs):
    key_t, value_t, query, proj, gate, up, down_t = refs[:7]
    extra_in, refs = refs[7 : 7 + extras], refs[7 + extras :]
    heads_t, heads, proj_v, gate_v, up_v, down_tv, down = refs[:7]
    extra_out, (query_v, sems) = refs[7 : 7 + extras], refs[7 + extras :]
    width, kv_width = query.shape[1], key_t.shape[0]
    pairs = (
        (down_t, down_tv),
        (query, query_v),
        (key_t, heads_t.at[pl.ds(width, kv_width)]),
        (value_t, heads_t.at[pl.ds(width + kv_width, kv_width)]),
        (proj, proj_v),
        (gate, gate_v),
        (up, up_v),
        *zip(extra_in, extra_out),
    )
    copies = [
        pltpu.make_async_copy(source, target, sems.at[i])
        for i, (source, target) in enumerate(pairs)
    ]
    for copy in copies:
        copy.start()
    copies[0].wait()
    transpose_to(down, down_tv)
    copies[1].wait()
    transpose_to(heads_t, query_v)
    copies[2].wait()
    copies[3].wait()
    transpose_to(heads, heads_t)
    for copy in copies[4:]:
        copy.wait()


def turn_kernel(first, count, *refs):
    sources, targets = refs[:count], refs[-count:]

    @pl.when((lax.axis_index("pipe") == 0) == first)
    def _():
        for source, target in zip(sources, targets):
            transpose_to(target, source)


def load_weights(query, key_t, value_t, proj, gate, up, down_t, *extra):
    sources = (key_t, value_t, query, proj, gate, up, down_t, *extra)
    all_width = query.shape[1] + 2 * key_t.shape[0]
    shapes = (
        (all_width, query.shape[0]),
        (query.shape[0], all_width),
        proj.shape,
        gate.shape,
        up.shape,
        down_t.shape,
        down_t.shape[::-1],
    )
    outs = [pltpu.VMEM(tuple(shape), BF16) for shape in shapes]
    outs += [pltpu.VMEM(array.shape, array.dtype) for array in extra]
    return pl.pallas_call(
        functools.partial(load_kernel, len(extra)),
        out_shape=outs,
        in_specs=[in_hbm() for _ in sources],
        out_specs=[in_vmem() for _ in outs],
        scratch_shapes=[
            pltpu.VMEM(query.shape, BF16),
            pltpu.SemaphoreType.DMA((len(sources),)),
        ],
        compiler_params=pltpu.CompilerParams(vmem_limit_bytes=12 * 2**20),
        name="load_weights",
    )(*[pltpu.with_memory_space_constraint(array, pltpu.HBM) for array in sources])


def turn_weights(weights, first, turned=()):
    count = len(weights)
    return pl.pallas_call(
        functools.partial(turn_kernel, first, count),
        out_shape=[pltpu.VMEM(tuple(weight.shape[::-1]), BF16) for weight in weights],
        in_specs=[in_vmem() for _ in (*weights, *turned)],
        out_specs=[in_vmem() for _ in weights],
        input_output_aliases={count + i: i for i in range(len(turned))},
        compiler_params=pltpu.CompilerParams(vmem_limit_bytes=12 * 2**20),
        name="turn_weights",
    )(*[pltpu.with_memory_space_constraint(weight, pltpu.VMEM) for weight in (*weights, *turned)])


def in_vmem():
    return pl.BlockSpec(memory_space=pltpu.VMEM)


def in_hbm():
    return pl.BlockSpec(memory_space=pltpu.HBM)


def kind_of(array):
    return {5: "probs" if array.dtype == BF16 else "gains", 4: "slopes", 3: "rows"}[len(array.shape)]


def buffers_for(arrays, rows):
    shapes = []
    for array in arrays:
        kind, shape = kind_of(array), tuple(array.shape)
        if kind in ("probs", "gains"):
            shapes.append(shape[1:])
        else:
            shapes.append(shape[:-2] + (rows, shape[-1]))
    return [pltpu.VMEM(shape, array.dtype) for shape, array in zip(shapes, arrays)]


def run_tick(
    kernel, sizes, lengths, tables, edge_parts, inbound, weights, reads, state, shapes, scratch, name
):
    rows, width = sizes["rows"], sizes["width"]
    aliased = [] if state is None else list(state)
    inbound = [] if inbound is None else [inbound]
    outs = [jax.ShapeDtypeStruct((rows, width), BF16)] + [
        pltpu.HBM(shape.shape, shape.dtype)
        for shape in (jax.ShapeDtypeStruct((sizes["total_rows"], width), F32), *shapes)
    ]
    scratch = scratch + buffers_for(reads, rows) + buffers_for(shapes, rows)
    if reads:
        scratch.append(pltpu.SemaphoreType.DMA((len(reads), 2)))
    scratch.append(pltpu.SemaphoreType.DMA((len(shapes), 2, 2)))
    scratch.append(pltpu.SemaphoreType.DMA((1,)))
    blocks = [*tables, *edge_parts, *inbound]
    tables = [pltpu.with_memory_space_constraint(array, pltpu.VMEM) for array in tables]
    first_alias = 1 + len(blocks) + len(weights) + len(reads)
    sizes = dict(
        sizes,
        edge_parts=len(edge_parts),
        inbound=len(inbound),
        aliased=len(aliased),
        stores=len(shapes),
        reads=len(reads),
        store_kinds=[kind_of(shape) for shape in shapes],
        read_kinds=[kind_of(read) for read in reads],
    )
    flops = 4 * rows * sum(int(np.prod(weight.shape)) for weight in weights)
    return pl.pallas_call(
        functools.partial(kernel, sizes),
        out_shape=outs,
        grid_spec=pltpu.PrefetchScalarGridSpec(
            num_scalar_prefetch=1,
            grid=(1,),
            in_specs=[in_vmem() for _ in (*blocks, *weights)]
            + [in_hbm() for _ in (*reads, *aliased)],
            out_specs=[in_vmem()] + [in_hbm() for _ in outs[1:]],
            scratch_shapes=scratch,
        ),
        input_output_aliases={first_alias + i: 1 + i for i in range(len(aliased))},
        compiler_params=pltpu.CompilerParams(
            dimension_semantics=("arbitrary",), vmem_limit_bytes=18 * 2**20
        ),
        cost_estimate=pl.CostEstimate(
            flops=flops, bytes_accessed=flops // (2 * rows), transcendentals=0
        ),
        name=name,
    )(
        lengths,
        *tables,
        *edge_parts,
        *inbound,
        *[pltpu.with_memory_space_constraint(weight, pltpu.VMEM) for weight in weights],
        *[pltpu.with_memory_space_constraint(array, pltpu.HBM) for array in (*reads, *aliased)],
    )


def rope_tables(rows):
    segment = rows // 2
    frequency = rope_base ** (-np.arange(HALF, dtype=np.float64) / HALF)
    positions = np.stack([np.arange(rows) % segment, np.arange(rows)]).astype(np.float64)
    angles = np.tile(positions[:, :, None] * frequency, (1, 1, LANES // HALF))
    sign = np.where(np.arange(LANES) % HEAD_DIM < HALF, -1.0, 1.0)
    return (
        jnp.asarray(np.cos(angles), F32),
        jnp.asarray(np.sin(angles) * sign, F32),
    )


def gather_ends(inputs, cotangent):
    sections, section = lax.axis_size("pipe"), lax.axis_index("pipe")
    last = sections - 1
    input_parts, cotangent_parts = [inputs] * sections, [cotangent] * sections
    for source in range(1, sections):
        mirror = last - source
        if mirror == source:
            input_parts[source] = lax.ppermute(inputs, "pipe", [(source, 0)])
            cotangent_parts[source] = lax.ppermute(cotangent, "pipe", [(source, last)])
            continue
        sent = jnp.where(section == mirror, cotangent, inputs)
        got = lax.ppermute(sent, "pipe", [(source, 0), (mirror, last)])
        input_parts[source] = cotangent_parts[mirror] = got
    return input_parts, cotangent_parts


def after(values, *tokens):
    return lax.optimization_barrier((values, tokens))[0]


def by_rows(value):
    return with_layout_constraint(value, Layout(major_to_minor=(0, 1)))


def odd_device():
    return lax.axis_index("dp") % 2


def pair_view(value):
    devices = lax.axis_size("dp")
    rows, columns = value.shape
    return value.reshape(devices // 2, 2, rows // devices, columns)


def neighbours_half(view):
    return lax.dynamic_index_in_dim(view, 1 - odd_device(), 1, keepdims=False)


def own_half(view):
    return lax.dynamic_index_in_dim(view, odd_device(), 1, keepdims=False)


def to_neighbour(part):
    devices = lax.axis_size("dp")
    return lax.ppermute(part, "dp", [(i, i ^ 1) for i in range(devices)])


def line_scatter(part):
    devices = lax.axis_size("dp")
    lines = [list(range(first, devices, 2)) for first in range(2)]
    line, rows, columns = part.shape
    return lax.psum_scatter(
        part.reshape(line * rows, columns),
        "dp",
        scatter_dimension=0,
        tiled=True,
        axis_index_groups=lines,
    )


def per_device(
    inputs,
    cotangent,
    lengths,
    w_query,
    w_key,
    w_value,
    w_proj,
    w_gate,
    w_up,
    w_down,
    gain_attn,
    gain_mlp,
):
    sections = lax.axis_size("pipe")
    section = lax.axis_index("pipe")
    total_rows, columns = inputs.shape
    width = columns * sections
    rows = 2 * total_rows // (MICRO + 1)
    segment = rows // 2
    kv_width = w_key.shape[-1]
    ff = w_gate.shape[-1]
    kv_heads = kv_width // HEAD_DIM
    share = width // kv_width
    depth_step = 2
    ticks = CHUNKS + depth_step * (sections - 1)
    sizes = dict(
        rows=rows,
        total_rows=total_rows,
        width=width,
        ff_step=ff // 2,
        sections=sections,
        depth_step=depth_step,
    )
    group = lengths[0]
    input_parts, cotangent_parts = gather_ends(inputs, cotangent)
    w_heads_t, w_heads, wp, wg, wu, wd_t, wd, *tables = load_weights(
        w_query[0],
        jnp.swapaxes(w_key[0], 0, 1),
        jnp.swapaxes(w_value[0], 0, 1),
        w_proj[0],
        w_gate[0],
        w_up[0],
        jnp.swapaxes(w_down[0], 0, 1),
        *rope_tables(rows),
        gain_attn,
        gain_mlp,
        inputs,
    )
    input_parts[0] = tables.pop()
    turned = turn_weights((wp, wg, wu), False)
    forward_weights = (w_heads, wp, wg, wu, wd)

    def stored(*shape, dtype=BF16):
        return jax.ShapeDtypeStruct(shape, dtype)

    query_pad = round_up(width, LANES)
    all_width = width + 2 * kv_width
    heads_pad = round_up(all_width, LANES)
    forward_shapes = [
        stored(2, total_rows, width, dtype=F32),
        stored(2, total_rows, width),
        stored(2, total_rows, heads_pad),
        stored(CHUNKS, 2, kv_heads, share * rows, rows),
        stored(2, total_rows, width),
        stored(2, total_rows, width, dtype=F32),
        stored(2, total_rows, width),
        stored(2, 2, total_rows, ff),
        stored(2, total_rows, ff),
    ]
    forward_scratch = [
        pltpu.VMEM((rows, width), F32),
        pltpu.VMEM((rows, heads_pad), F32),
    ]
    sent = {}
    state = None
    for tick in range(ticks):
        rounded, *state = run_tick(
            forward_kernel,
            dict(sizes, tick=tick, backward=False),
            lengths,
            tables,
            input_parts if tick < CHUNKS else (),
            sent.get(tick - depth_step),
            forward_weights,
            (),
            state,
            forward_shapes,
            forward_scratch,
            "layer_pair_forward",
        )
        route = [
            (s, s + 1) for s in range(sections - 1) if 0 <= tick - depth_step * s < CHUNKS
        ]
        if route:
            sent[tick] = lax.ppermute(rounded, "pipe", route)
        if tick == CHUNKS - 1:
            ready, _ = lax.optimization_barrier(((wp, wg, wu), rounded))
            turned = turn_weights(ready, True, turned)
    backward_weights = (w_heads_t, *turned, wd_t)
    results = state[0]
    hidden, normed_attn, heads, probs, mixed, middle, normed_mlp, slopes, inner = state[1:]

    backward_shapes = [
        stored(2, total_rows, width),
        stored(2, total_rows, ff),
        stored(2, total_rows, ff),
        stored(2, total_rows, width),
        stored(2, total_rows, all_width),
        stored(CHUNKS, 2, 2, 8, width, dtype=F32),
    ]
    backward_scratch = [
        pltpu.VMEM((rows, width), F32),
        pltpu.VMEM((rows, query_pad), F32),
        pltpu.VMEM((rows, ff), F32),
    ]
    reads = (hidden, heads, probs, middle, slopes)
    sent = {}
    state = None
    for tick in range(ticks):
        rounded, *state = run_tick(
            backward_kernel,
            dict(sizes, tick=tick, backward=True),
            lengths,
            tables,
            cotangent_parts if tick < CHUNKS else (),
            sent.get(tick - depth_step),
            backward_weights,
            reads,
            state,
            backward_shapes,
            backward_scratch,
            "layer_pair_backward",
        )
        route = [
            (s, s - 1)
            for s in range(1, sections)
            if 0 <= tick - depth_step * (sections - 1 - s) < CHUNKS
        ]
        if route:
            sent[tick] = lax.ppermute(rounded, "pipe", route)
    input_grads = state[0]
    branch, gate_grad, up_grad, attn_grad, heads_grad, gains = state[1:]

    def product(left, right):
        left = left.reshape(2 * total_rows, left.shape[-1])
        right = right.reshape(2 * total_rows, right.shape[-1])
        return by_rows(dot_rows(left, right).astype(BF16))

    heads_grads = product(normed_attn, heads_grad)
    line = lax.axis_size("dp") // 2
    own_heads = line_scatter(heads_grads.reshape(line, width // line, all_width))
    gate_view = pair_view(product(*after((normed_mlp, gate_grad), heads_grads)))
    gate_sent = neighbours_half(gate_view)
    gate_got = to_neighbour(gate_sent)
    up_view = pair_view(product(*after((normed_mlp, up_grad), gate_sent)))
    up_sent = neighbours_half(up_view)
    up_got = to_neighbour(up_sent)
    down_view = pair_view(product(*after((inner, branch), up_sent)))
    down_sent = neighbours_half(down_view)
    down_got = to_neighbour(down_sent)
    proj_view = pair_view(product(*after((mixed, attn_grad), down_sent)))
    proj_sent = neighbours_half(proj_view)
    proj_got = to_neighbour(proj_sent)

    gate_part = own_half(gate_view) + after(gate_got, proj_sent)
    grad_gate = line_scatter(gate_part)
    up_part = own_half(up_view) + after(up_got, gate_part)
    grad_up = line_scatter(after(up_part, own_heads))
    down_part = own_half(down_view) + after(down_got, up_part)
    grad_down = line_scatter(after(down_part, grad_gate))
    proj_part = own_half(proj_view) + after(proj_got, down_part)
    grad_proj = line_scatter(after(proj_part, grad_up)).astype(F32)
    grad_gate, grad_up, grad_down = [
        grad.astype(F32) for grad in (grad_gate, grad_up, grad_down)
    ]

    own_heads = own_heads.reshape(1, 2, width // (2 * line), all_width)
    heads_got = to_neighbour(neighbours_half(own_heads))
    grad_heads = (own_half(own_heads) + heads_got)[0].astype(F32)
    grad_query = grad_heads[:, :width]
    grad_key = grad_heads[:, width : width + kv_width]
    grad_value = grad_heads[:, width + kv_width :]
    gain_sums = jnp.sum(gains, axis=(0, 1, 3))
    grad_gain_attn = lax.psum_scatter(gain_sums[0], "dp", scatter_dimension=0, tiled=True)
    grad_gain_mlp = lax.psum_scatter(gain_sums[1], "dp", scatter_dimension=0, tiled=True)

    def spread(store, source):
        own = store[:, source * columns : (source + 1) * columns]
        arrived = jnp.where(section == source, own, 0.0)
        for target in range(sections):
            if target != source:
                block = store[:, target * columns : (target + 1) * columns]
                arrived = arrived + lax.ppermute(block, "pipe", [(source, target)])
        return arrived

    position = jnp.arange(total_rows)
    long_rows = position < rows
    offsets = jnp.where(long_rows, position, position % segment)
    micro = jnp.where(long_rows, 0, position // segment - 1)
    bound = jnp.zeros_like(position)
    for m in range(MICRO):
        bound = jnp.where(micro == m, group[m], bound)
    valid = (offsets < bound)[:, None]
    results, input_grads = after((results, input_grads), up_part)
    layer_output = jnp.where(valid, spread(results, sections - 1), 0.0)
    grad_input = spread(input_grads, 0)
    return (
        layer_output,
        grad_input,
        grad_query[None],
        grad_key[None],
        grad_value[None],
        grad_proj[None],
        grad_gate[None],
        grad_up[None],
        grad_down[None],
        grad_gain_attn[None],
        grad_gain_mlp[None],
    )


def solution(mesh):
    placed = (
        P("dp", "pipe"),
        P("dp", "pipe"),
        P("dp", None),
        P("pipe", None, None),
        P("pipe", None, None),
        P("pipe", None, None),
        P("pipe", None, None),
        P("pipe", None, None),
        P("pipe", None, None),
        P("pipe", None, None),
        P("pipe", None),
        P("pipe", None),
    )
    return jax.shard_map(
        per_device,
        mesh=mesh,
        in_specs=placed,
        out_specs=(
            P("dp", "pipe"),
            P("dp", "pipe"),
            P("pipe", "dp", None),
            P("pipe", "dp", None),
            P("pipe", "dp", None),
            P("pipe", "dp", None),
            P("pipe", "dp", None),
            P("pipe", "dp", None),
            P("pipe", "dp", None),
            P("pipe", "dp"),
            P("pipe", "dp"),
        ),
        check_vma=False,
    )
```

time: 521 us -> 480 us (0.921)
  waiting for transfers between devices: 208 us -> 188 us
  local copies, waits for them, and re-layouts: 32.2 us -> 18 us
  matrix products: 28.8 us -> 22.6 us
    ppermute x14, waiting for transfers between devices: 57.8 us -> 34 us  [per_device(): sent[tick] = lax.ppermute(rounded, 'pipe', route)]
    ppermute x11 -> x8, waiting for transfers between devices: 149 us -> 125 us  [the longest x5 125 us: to_neighbour(): return lax.ppermute(part, 'dp', [(i, i ^ 1) for i in range(devices)])]
    reduce_scatter x5, waiting for transfers between devices: 0.01 us -> 22.7 us  [line_scatter(): lax.psum_scatter(part.reshape(line * rows, columns), 'dp', scatter_dimens...]
    convert_element_type x1 -> x0, local copies, waits for them, and re-layouts: 7.85 us -> none  [product(): return dot_rows(all_rows(left), all_rows(right)).astype(BF16)]
    dot_general x5, matrix products: 28.8 us -> 22.6 us  [dot_rows(): lax.dot_general(left, right, (((0,), (0,)), ((), ())), preferred_element_...]
    unnamed x37 -> x45, local copies, waits for them, and re-layouts: 6.67 us -> 12.2 us
    concatenate x1 -> x0, local copies, waits for them, and re-layouts: 5.46 us -> none  [per_device(): jnp.concatenate([all_rows(query_grad), all_rows(key_grad), all_rows(value...]
    pallas_call x2 -> x3, Pallas kernels: 10.9 us -> 10.4 us  [the longest x1 7.04 us: load_weights(): pl.pallas_call(functools.partial(load_kernel, len(extra)), out_shape=outs...]
  transfers between devices with their start and end apart: 36 -> 33, of which waited for: 6 -> 7; matrix products, arithmetic and copies ran while one was open for 13% -> 9% of each run, Pallas kernels for 22% -> 25%
where the time goes in v3:
time: 480 us; the launch traced here: 472 us
  waiting for transfers between devices  188 us (39%)
  Pallas kernels  145 us (30%)
  starting transfers between devices  33.3 us (7%)
  blocking collectives  25.9 us (5%)
  other arithmetic  22.8 us (5%)
  matrix products  22.6 us (5%)
  local copies, waits for them, and re-layouts  18 us (4%)
  between operations  15.5 us (3%)
    pallas_call x18, Pallas kernels, run_tick(): pl.pallas_call(functools.partial(kernel, sizes), out_shape=outs, grid_spe...  135 us
    ppermute x5, waiting for transfers between devices, to_neighbour(): return lax.ppermute(part, 'dp', [(i, i ^ 1) for i in range(devices)])  125 us
    ppermute x14, waiting for transfers between devices, per_device(): sent[tick] = lax.ppermute(rounded, 'pipe', route)  34 us
    unnamed x1, blocking collectives  25.9 us
    reduce_scatter x5, waiting for transfers between devices, line_scatter(): lax.psum_scatter(part.reshape(line * rows, columns), 'dp', scatter_dimens...  22.7 us
    dot_general x5, matrix products, dot_rows(): lax.dot_general(left, right, (((0,), (0,)), ((), ())), preferred_element_...  22.6 us
    ppermute x14, starting transfers between devices, per_device(): sent[tick] = lax.ppermute(rounded, 'pipe', route)  13.2 us
    unnamed x45, local copies, waits for them, and re-layouts  12.2 us
  transfers between devices with their start and end apart: 33, of which 7 were waited for; matrix products, arithmetic and copies ran while one was open for 9% of the time, Pallas kernels for 25%

profile of v3, /device:TPU:0, one launch (start us, length us, event | category | flops | bytes accessed | tf_op | source)
XLA Modules:
  0.0 471.8 jit_solution(5104060731989099348)
XLA Ops:
  10.9 4.3 collective-permute-start.2
  15.2 7.0 %load_weights.1 = (bf16[1600,960]{1,0:T(8,128)(2,1)S(1)}, bf16[960,1600]{1,0:T(8,128)(2,1)S(1)}, bf16[960,960]{1,0:T(8,128)(2,1)S(1)}, bf16[960,2560]{1,0:T(8,12...) custom-call(bf16[320,960]{1,0:T(8,128)(2,1)} %bitcast.115, ...), custom_call_target="tpu_custom_call" | custom-call | tf_op jit(solution)/shard_map/load_weights/pallas_call | solution.py:529
  22.9 10.9 %layer_pair_forward.9 = (bf16[128,960]{1,0:T(8,128)(2,1)S(1)}, f32[320,960]{1,0:T(8,128)}, f32[2,320,960]{2,1,0:T(8,128)}, bf16[2,320,960]{2,1,0:T(8,128)(2,1)},...) custom-call(s32[1,4]{1,0:T(1,128)S(1)} %copy-done.1, ...), custom_call_target="tpu_custom_call" | custom-call | flops 5033164800 | bytes 19660800 | tf_op jit(solution)/shard_map/layer_pair_forward/pallas_call | solution.py:608
  35.2 11.6 %layer_pair_forward.10 = (bf16[128,960]{1,0:T(8,128)(2,1)S(1)}, f32[320,960]{1,0:T(8,128)}, f32[2,320,960]{2,1,0:T(8,128)}, bf16[2,320,960]{2,1,0:T(8,128)(2,1)}...) custom-call(s32[1,4]{1,0:T(1,128)S(1)} %copy-done.1, ...), custom_call_target="tpu_custom_call", output_to_operand_aliasing={{1}: (14, {}), {2}: (15, {}), {3}: (16, {}), {4}: (17, {}),... | custom-call | flops 5033164800 | bytes 19660800 | tf_op jit(solution)/shard_map/layer_pair_forward/pallas_call | solution.py:608
  48.1 10.7 %layer_pair_forward.11 = (bf16[128,960]{1,0:T(8,128)(2,1)S(1)}, f32[320,960]{1,0:T(8,128)}, f32[2,320,960]{2,1,0:T(8,128)}, bf16[2,320,960]{2,1,0:T(8,128)(2,1)}...) custom-call(s32[1,4]{1,0:T(1,128)S(1)} %copy-done.1, ...), custom_call_target="tpu_custom_call", output_to_operand_aliasing={{1}: (15, {}), {2}: (16, {}), {3}: (17, {}), {4}: (18, {}),... | custom-call | flops 5033164800 | bytes 19660800 | tf_op jit(solution)/shard_map/layer_pair_forward/pallas_call | solution.py:608
  60.1 9.0 %layer_pair_forward.12 = (bf16[128,960]{1,0:T(8,128)(2,1)S(1)}, f32[320,960]{1,0:T(8,128)}, f32[2,320,960]{2,1,0:T(8,128)}, bf16[2,320,960]{2,1,0:T(8,128)(2,1)}...) custom-call(s32[1,4]{1,0:T(1,128)S(1)} %copy-done.1, ...), custom_call_target="tpu_custom_call", output_to_operand_aliasing={{1}: (11, {}), {2}: (12, {}), {3}: (13, {}), {4}: (14, {}),... | custom-call | flops 5033164800 | bytes 19660800 | tf_op jit(solution)/shard_map/layer_pair_forward/pallas_call | solution.py:608
  69.8 3.4 turn_weights.3
  74.9 7.2 %layer_pair_forward.14 = (bf16[128,960]{1,0:T(8,128)(2,1)S(1)}, f32[320,960]{1,0:T(8,128)}, f32[2,320,960]{2,1,0:T(8,128)}, bf16[2,320,960]{2,1,0:T(8,128)(2,1)}...) custom-call(s32[1,4]{1,0:T(1,128)S(1)} %copy-done.1, ...), custom_call_target="tpu_custom_call", output_to_operand_aliasing={{1}: (11, {}), {2}: (12, {}), {3}: (13, {}), {4}: (14, {}),... | custom-call | flops 5033164800 | bytes 19660800 | tf_op jit(solution)/shard_map/layer_pair_forward/pallas_call | solution.py:608
  84.4 8.8 %layer_pair_forward.16 = (bf16[128,960]{1,0:T(8,128)(2,1)}, f32[320,960]{1,0:T(8,128)}, f32[2,320,960]{2,1,0:T(8,128)}, bf16[2,320,960]{2,1,0:T(8,128)(2,1)}, bf...) custom-call(s32[1,4]{1,0:T(1,128)S(1)} %copy-done.1, ...), custom_call_target="tpu_custom_call", output_to_operand_aliasing={{1}: (11, {}), {2}: (12, {}), {3}: (13, {}), {4}: (14, {}),... | custom-call | flops 5033164800 | bytes 19660800 | tf_op jit(solution)/shard_map/layer_pair_forward/pallas_call | solution.py:608
  96.4 8.0 %layer_pair_backward.10 = (bf16[128,960]{1,0:T(8,128)(2,1)S(1)}, f32[320,960]{1,0:T(8,128)}, bf16[2,320,960]{2,1,0:T(8,128)(2,1)}, bf16[2,320,2560]{2,1,0:T(8,12...) custom-call(s32[1,4]{1,0:T(1,128)S(1)} %copy-done.1, ...), custom_call_target="tpu_custom_call", output_to_operand_aliasing={{1}: (19, {}), {2}: (20, {}), {3}: (21, {}), {4}: (22, {}),... | custom-call | flops 5033164800 | bytes 19660800 | tf_op jit(solution)/shard_map/layer_pair_backward/pallas_call | solution.py:608
  106.7 8.7 %layer_pair_backward.12 = (bf16[128,960]{1,0:T(8,128)(2,1)S(1)}, f32[320,960]{1,0:T(8,128)}, bf16[2,320,960]{2,1,0:T(8,128)(2,1)}, bf16[2,320,2560]{2,1,0:T(8,12...) custom-call(s32[1,4]{1,0:T(1,128)S(1)} %copy-done.1, ...), custom_call_target="tpu_custom_call", output_to_operand_aliasing={{1}: (16, {}), {2}: (17, {}), {3}: (18, {}), {4}: (19, {}),... | custom-call | flops 5033164800 | bytes 19660800 | tf_op jit(solution)/shard_map/layer_pair_backward/pallas_call | solution.py:608
  118.3 7.9 %layer_pair_backward.14 = (bf16[128,960]{1,0:T(8,128)(2,1)S(1)}, f32[320,960]{1,0:T(8,128)}, bf16[2,320,960]{2,1,0:T(8,128)(2,1)}, bf16[2,320,2560]{2,1,0:T(8,12...) custom-call(s32[1,4]{1,0:T(1,128)S(1)} %copy-done.1, ...), custom_call_target="tpu_custom_call", output_to_operand_aliasing={{1}: (16, {}), {2}: (17, {}), {3}: (18, {}), {4}: (19, {}),... | custom-call | flops 5033164800 | bytes 19660800 | tf_op jit(solution)/shard_map/layer_pair_backward/pallas_call | solution.py:608
  127.6 33.9 %collective-permute-done.13.refs_4_ = bf16[128,960]{1,0:T(8,128)(2,1)S(1)} collective-permute-done((bf16[128,960]{1,0:T(8,128)(2,1)S(1)}, bf16[128,960]{1,0:T(8,128)(2,1)S(1)}, u32[]{:S(2)}, u32[]{:S(2)}) %collective-permute-start.13) | collective-permute-done | bytes 245792 | tf_op jit(solution)/shard_map/ppermute | solution.py:849
  161.5 14.7 %layer_pair_backward.15 = (bf16[128,960]{1,0:T(8,128)(2,1)S(1)}, f32[320,960]{1,0:T(8,128)}, bf16[2,320,960]{2,1,0:T(8,128)(2,1)}, bf16[2,320,2560]{2,1,0:T(8,12...) custom-call(s32[1,4]{1,0:T(1,128)S(1)} %copy-done.1, ...), custom_call_target="tpu_custom_call", output_to_operand_aliasing={{1}: (16, {}), {2}: (17, {}), {3}: (18, {}), {4}: (19, {}),... | custom-call | flops 5033164800 | bytes 19660800 | tf_op jit(solution)/shard_map/layer_pair_backward/pallas_call | solution.py:608
  177.5 15.9 %layer_pair_backward.16 = (bf16[128,960]{1,0:T(8,128)(2,1)}, f32[320,960]{1,0:T(8,128)}, bf16[2,320,960]{2,1,0:T(8,128)(2,1)}, bf16[2,320,2560]{2,1,0:T(8,128)(2...) custom-call(s32[1,4]{1,0:T(1,128)S(1)} %copy-done.1, ...), custom_call_target="tpu_custom_call", output_to_operand_aliasing={{1}: (16, {}), {2}: (17, {}), {3}: (18, {}), {4}: (19, {}),... | custom-call | flops 5033164800 | bytes 19660800 | tf_op jit(solution)/shard_map/layer_pair_backward/pallas_call | solution.py:608
  193.4 15.5 %layer_pair_backward.17 = (bf16[128,960]{1,0:T(8,128)(2,1)}, f32[320,960]{1,0:T(8,128)}, bf16[2,320,960]{2,1,0:T(8,128)(2,1)}, bf16[2,320,2560]{2,1,0:T(8,128)(2...) custom-call(s32[1,4]{1,0:T(1,128)S(1)} %copy-done.1, ...), custom_call_target="tpu_custom_call", output_to_operand_aliasing={{1}: (16, {}), {2}: (17, {}), {3}: (18, {}), {4}: (19, {}),... | custom-call | flops 5033164800 | bytes 19660800 | tf_op jit(solution)/shard_map/layer_pair_backward/pallas_call | solution.py:608
  208.9 6.4 %bitcast_convert_fusion.3 = bf16[960,1600]{1,0:T(8,128)(2,1)} fusion(bf16[2,320,960]{2,1,0:T(8,128)(2,1)S(1)} %copy-done.7, bf16[2,320,1600]{2,1,0:T(8,128)(2,1)} %get-tuple-element.398), kind=kOutput, calls=%fused_computation.3 | convolution fusion | flops 1967616000 | bytes 6348800 | tf_op jit(solution)/shard_map/dot_general | solution.py:38
  215.6 5.6 %bitcast_convert_fusion.2 = bf16[960,2560]{1,0:T(8,128)(2,1)S(1)} fusion(bf16[2,320,960]{2,1,0:T(8,128)(2,1)} %get-tuple-element.401, bf16[2,320,2560]{2,1,0:T(8,128)(2,1)S(1)} %copy-done.3), kind=kOutput, calls=%fused_computation.2 | convolution fusion | flops 3148185600 | bytes 9420800 | tf_op jit(solution)/shard_map/dot_general | solution.py:38
  223.9 4.3 bitcast_convert_fusion.1
  229.9 2.0 copy-done.14
  233.2 4.5 bitcast_convert_fusion
  245.4 27.5 %collective-permute-done.18 = bf16[4,120,2560]{2,1,0:T(8,128)(2,1)S(1)} collective-permute-done((bf16[4,120,2560]{2,1,0:T(8,128)(2,1)S(1)}, bf16[4,120,2560]{2,1,0:T(8,128)(2,1)S(1)}, u32[]{:S(2)}, u32[]{:S(2)}) %collective-permute-start.18) | collective-permute-done | bytes 2457632 | tf_op jit(solution)/shard_map/ppermute | solution.py:693
  276.2 48.6 %collective-permute-done.17 = bf16[4,120,2560]{2,1,0:T(8,128)(2,1)S(1)} collective-permute-done((bf16[4,120,2560]{2,1,0:T(8,128)(2,1)}, bf16[4,120,2560]{2,1,0:T(8,128)(2,1)S(1)}, u32[]{:S(2)}, u32[]{:S(2)}) %collective-permute-start.17) | collective-permute-done | bytes 2457632 | tf_op jit(solution)/shard_map/ppermute | solution.py:693
  324.7 3.5 bitcast_add_fusion.2
  329.8 49.3 %collective-permute-done.27 = bf16[4,320,960]{2,1,0:T(8,128)(2,1)S(1)} collective-permute-done((bf16[4,320,960]{2,1,0:T(8,128)(2,1)S(1)}, bf16[4,320,960]{2,1,0:T(8,128)(2,1)S(1)}, u32[]{:S(2)}, u32[]{:S(2)}) %collective-permute-start.27) | collective-permute-done | bytes 2457632 | tf_op jit(solution)/shard_map/ppermute | solution.py:693
  379.1 3.5 bitcast_add_fusion
  386.6 2.6 fusion.7
  389.3 25.9 %all-reduce.2 = (f32[960]{0:T(1024)S(1)}, f32[960]{0:T(1024)S(1)}) all-reduce(f32[960]{0:T(1024)S(1)} %bitcast.118, f32[960]{0:T(1024)S(1)} %bitcast.117), channel_id=7, replica_groups=mesh['pipe'=4,'dp'=8] {'dp'}, use_global_device_ids=true, to_apply=%region_6.7.clone | all-reduce | flops 1920 | bytes 15360
  421.8 2.3 bitcast_add_fusion.3
  426.4 6.0 %collective-permute-done.19 = f32[320,240]{1,0:T(8,128)S(1)} collective-permute-done((f32[320,240]{1,0:T(8,128)S(1)}, f32[320,240]{1,0:T(8,128)S(1)}, u32[]{:S(2)}, u32[]{:S(2)}) %collective-permute-start.19) | collective-permute-done | bytes 307232 | tf_op jit(solution)/shard_map/ppermute | solution.py:902
  438.3 2.3 bitcast_convert_fusion.5
  440.6 22.6 %reduce-scatter.10.cloned.1.call-done = bf16[120,960]{1,0:T(8,128)(2,1)} async-done(((bf16[480,960]{1,0:T(8,128)(2,1)}), bf16[120,960]{1,0:T(8,128)(2,1)}) %reduce-scatter.10.cloned.1.call-update) | async-done | bytes 230416 | tf_op jit(solution)/shard_map/reduce_scatter | solution.py:700
  (137 shorter events, 61.9 us)
Async XLA Ops:
  7.2 321.1 %reduce-scatter.6.cloned.1.call-start = ((), (), s32[]{:S(2)}) async-start(), calls=%async_computation.5 | async-start | bytes 3993600 | tf_op jit(solution)/shard_map/reduce_scatter | solution.py:700
  8.3 14.0 %collective-permute-start = (bf16[320,240]{1,0:T(8,128)(2,1)S(1)}, bf16[320,240]{1,0:T(8,128)(2,1)S(1)}, u32[]{:S(2)}, u32[]{:S(2)}) collective-permute-start(bf16[320,240]{1,0:T(8,128)(2,1)S(1)} %get-tuple-element.455), channel_id=1, source_target_pairs={{8,0},{16,24},{9,1},{17,25},{10,2},{18,26},{11,3},{19,27},{12,4},{... | collective-permute-start | bytes 460808 | tf_op jit(solution)/shard_map/ppermute | solution.py:660
  9.6 12.7 %collective-permute-start.1 = (bf16[320,240]{1,0:T(8,128)(2,1)S(1)}, bf16[320,240]{1,0:T(8,128)(2,1)S(1)}, u32[]{:S(2)}, u32[]{:S(2)}) collective-permute-start(bf16[320,240]{1,0:T(8,128)(2,1)S(1)} %get-tuple-element.454), channel_id=1, source_target_pairs={{16,0},{8,24},{17,1},{9,25},{18,2},{10,26},{19,3},{11,27},{20,4},{... | collective-permute-start | bytes 460808 | tf_op jit(solution)/shard_map/ppermute | solution.py:660
  10.9 11.4 %collective-permute-start.2 = (bf16[320,240]{1,0:T(8,128)(2,1)S(1)}, bf16[320,240]{1,0:T(8,128)(2,1)S(1)}, u32[]{:S(2)}, u32[]{:S(2)}) collective-permute-start(bf16[320,240]{1,0:T(8,128)(2,1)S(1)} %get-tuple-element.453), channel_id=1, source_target_pairs={{24,0},{0,24},{25,1},{1,25},{26,2},{2,26},{27,3},{3,27},{28,4},{4,... | collective-permute-start | bytes 460808 | tf_op jit(solution)/shard_map/ppermute | solution.py:660
  33.8 14.3 %collective-permute-start.3 = (bf16[128,960]{1,0:T(8,128)(2,1)S(1)}, bf16[128,960]{1,0:T(8,128)(2,1)S(1)}, u32[]{:S(2)}, u32[]{:S(2)}) collective-permute-start(bf16[128,960]{1,0:T(8,128)(2,1)S(1)} %get-tuple-element.226), channel_id=1, source_target_pairs={{0,8},{1,9},{2,10},{3,11},{4,12},{5,13},{6,14},{7,15}} | collective-permute-start | bytes 737288 | tf_op jit(solution)/shard_map/ppermute | solution.py:804
  46.8 13.4 %collective-permute-start.5 = (bf16[128,960]{1,0:T(8,128)(2,1)S(1)}, bf16[128,960]{1,0:T(8,128)(2,1)S(1)}, u32[]{:S(2)}, u32[]{:S(2)}) collective-permute-start(bf16[128,960]{1,0:T(8,128)(2,1)S(1)} %get-tuple-element.248), channel_id=1, source_target_pairs={{0,8},{1,9},{2,10},{3,11},{4,12},{5,13},{6,14},{7,15}} | collective-permute-start | bytes 737288 | tf_op jit(solution)/shard_map/ppermute | solution.py:804
  58.8 14.4 %collective-permute-start.4 = (bf16[128,960]{1,0:T(8,128)(2,1)S(1)}, bf16[128,960]{1,0:T(8,128)(2,1)S(1)}, u32[]{:S(2)}, u32[]{:S(2)}) collective-permute-start(bf16[128,960]{1,0:T(8,128)(2,1)S(1)} %get-tuple-element.247), channel_id=1, source_target_pairs={{0,8},{8,16},{1,9},{9,17},{2,10},{10,18},{3,11},{11,19},{4,12},{12... | collective-permute-start | bytes 737288 | tf_op jit(solution)/shard_map/ppermute | solution.py:804
  69.1 5.7 %collective-permute-start.7 = (bf16[128,960]{1,0:T(8,128)(2,1)S(1)}, bf16[128,960]{1,0:T(8,128)(2,1)S(1)}, u32[]{:S(2)}, u32[]{:S(2)}) collective-permute-start(bf16[128,960]{1,0:T(8,128)(2,1)S(1)} %get-tuple-element.270), channel_id=1, source_target_pairs={{8,16},{9,17},{10,18},{11,19},{12,20},{13,21},{14,22},{15,23}} | collective-permute-start | bytes 737288 | tf_op jit(solution)/shard_map/ppermute | solution.py:804
  74.2 8.6 %collective-permute-start.6 = (bf16[128,960]{1,0:T(8,128)(2,1)S(1)}, bf16[128,960]{1,0:T(8,128)(2,1)S(1)}, u32[]{:S(2)}, u32[]{:S(2)}) collective-permute-start(bf16[128,960]{1,0:T(8,128)(2,1)S(1)} %get-tuple-element.269), channel_id=1, source_target_pairs={{8,16},{16,24},{9,17},{17,25},{10,18},{18,26},{11,19},{19,27},{12,... | collective-permute-start | bytes 737288 | tf_op jit(solution)/shard_map/ppermute | solution.py:804
  82.0 2.3 collective-permute-start.9
  83.7 9.5 %collective-permute-start.8 = (bf16[128,960]{1,0:T(8,128)(2,1)S(1)}, bf16[128,960]{1,0:T(8,128)(2,1)S(1)}, u32[]{:S(2)}, u32[]{:S(2)}) collective-permute-start(bf16[128,960]{1,0:T(8,128)(2,1)S(1)} %get-tuple-element.291), channel_id=1, source_target_pairs={{16,24},{17,25},{18,26},{19,27},{20,28},{21,29},{22,30},{23,31}} | collective-permute-start | bytes 737288 | tf_op jit(solution)/shard_map/ppermute | solution.py:804
  95.7 9.4 %collective-permute-start.10 = (bf16[128,960]{1,0:T(8,128)(2,1)S(1)}, bf16[128,960]{1,0:T(8,128)(2,1)S(1)}, u32[]{:S(2)}, u32[]{:S(2)}) collective-permute-start(bf16[128,960]{1,0:T(8,128)(2,1)S(1)} %get-tuple-element.330), channel_id=1, source_target_pairs={{24,16},{25,17},{26,18},{27,19},{28,20},{29,21},{30,22},{31,23}} | collective-permute-start | bytes 737288 | tf_op jit(solution)/shard_map/ppermute | solution.py:849
  106.0 10.1 %collective-permute-start.11 = (bf16[128,960]{1,0:T(8,128)(2,1)S(1)}, bf16[128,960]{1,0:T(8,128)(2,1)S(1)}, u32[]{:S(2)}, u32[]{:S(2)}) collective-permute-start(bf16[128,960]{1,0:T(8,128)(2,1)S(1)} %get-tuple-element.345), channel_id=1, source_target_pairs={{16,8},{24,16},{17,9},{25,17},{18,10},{26,18},{19,11},{27,19},{20,... | collective-permute-start | bytes 737288 | tf_op jit(solution)/shard_map/ppermute | solution.py:849
  115.4 2.9 collective-permute-start.14
  117.0 44.4 %collective-permute-start.13 = (bf16[128,960]{1,0:T(8,128)(2,1)S(1)}, bf16[128,960]{1,0:T(8,128)(2,1)S(1)}, u32[]{:S(2)}, u32[]{:S(2)}) collective-permute-start(bf16[128,960]{1,0:T(8,128)(2,1)S(1)} %get-tuple-element.361), channel_id=1, source_target_pairs={{8,0},{16,8},{9,1},{17,9},{10,2},{18,10},{11,3},{19,11},{12,4},{20... | collective-permute-start | bytes 737288 | tf_op jit(solution)/shard_map/ppermute | solution.py:849
  126.3 51.2 %collective-permute-start.16 = (bf16[128,960]{1,0:T(8,128)(2,1)S(1)}, bf16[128,960]{1,0:T(8,128)(2,1)S(1)}, u32[]{:S(2)}, u32[]{:S(2)}) collective-permute-start(bf16[128,960]{1,0:T(8,128)(2,1)S(1)} %get-tuple-element.378), channel_id=1, source_target_pairs={{8,0},{9,1},{10,2},{11,3},{12,4},{13,5},{14,6},{15,7}} | collective-permute-start | bytes 737288 | tf_op jit(solution)/shard_map/ppermute | solution.py:849
  176.2 17.2 %collective-permute-start.15 = (bf16[128,960]{1,0:T(8,128)(2,1)S(1)}, bf16[128,960]{1,0:T(8,128)(2,1)S(1)}, u32[]{:S(2)}, u32[]{:S(2)}) collective-permute-start(bf16[128,960]{1,0:T(8,128)(2,1)S(1)} %get-tuple-element.377), channel_id=1, source_target_pairs={{8,0},{9,1},{10,2},{11,3},{12,4},{13,5},{14,6},{15,7}} | collective-permute-start | bytes 737288 | tf_op jit(solution)/shard_map/ppermute | solution.py:849
  215.3 167.3 %reduce-scatter.12.cloned.1.call-start = ((), (), s32[]{:S(2)}) async-start(), calls=%async_computation.8 | async-start | bytes 3072000 | tf_op jit(solution)/shard_map/reduce_scatter | solution.py:700
  221.4 51.5 %collective-permute-start.18 = (bf16[4,120,2560]{2,1,0:T(8,128)(2,1)S(1)}, bf16[4,120,2560]{2,1,0:T(8,128)(2,1)S(1)}, u32[]{:S(2)}, u32[]{:S(2)}) collective-permute-start(bf16[4,120,2560]{2,1,0:T(8,128)(2,1)S(1)} %dynamic-slice_bitcast_fusion.2), channel_id=1, source_target_pairs={{0,1},{1,0},{2,3},{3,2},{4,5},{5,4},{6,7},{7,6},{8,9},{9,8},{10,11... | collective-permute-start | bytes 7372808 | tf_op jit(solution)/shard_map/ppermute | solution.py:693
  274.6 159.7 %reduce-scatter.8.cloned.1.call-start = ((), (), s32[]{:S(2)}) async-start(), calls=%async_computation.6 | async-start | bytes 3072000 | tf_op jit(solution)/shard_map/reduce_scatter | solution.py:700
  274.6 50.1 %collective-permute-start.17 = (bf16[4,120,2560]{2,1,0:T(8,128)(2,1)}, bf16[4,120,2560]{2,1,0:T(8,128)(2,1)S(1)}, u32[]{:S(2)}, u32[]{:S(2)}) collective-permute-start(bf16[4,120,2560]{2,1,0:T(8,128)(2,1)} %dynamic-slice_bitcast_fusion.1), channel_id=1, source_target_pairs={{0,1},{1,0},{2,3},{3,2},{4,5},{5,4},{6,7},{7,6},{8,9},{9,8},{10,11... | collective-permute-start | bytes 7372808 | tf_op jit(solution)/shard_map/ppermute | solution.py:693
  328.3 110.1 %reduce-scatter.14.cloned.1.call-start = ((), (), s32[]{:S(2)}) async-start(), calls=%async_computation.9 | async-start | bytes 3276800 | tf_op jit(solution)/shard_map/reduce_scatter | solution.py:700
  328.3 50.8 %collective-permute-start.27 = (bf16[4,320,960]{2,1,0:T(8,128)(2,1)S(1)}, bf16[4,320,960]{2,1,0:T(8,128)(2,1)S(1)}, u32[]{:S(2)}, u32[]{:S(2)}) collective-permute-start(bf16[4,320,960]{2,1,0:T(8,128)(2,1)S(1)} %dynamic-slice_bitcast_fusion), channel_id=1, source_target_pairs={{0,1},{1,0},{2,3},{3,2},{4,5},{5,4},{6,7},{7,6},{8,9},{9,8},{10,11... | collective-permute-start | bytes 7372808 | tf_op jit(solution)/shard_map/ppermute | solution.py:693
  382.7 80.6 %reduce-scatter.10.cloned.1.call-start = ((), (), s32[]{:S(2)}) async-start(), calls=%async_computation.7 | async-start | bytes 1228800 | tf_op jit(solution)/shard_map/reduce_scatter | solution.py:700
  385.1 35.4 %collective-permute-start.26 = (bf16[4,120,960]{2,1,0:T(8,128)(2,1)}, bf16[4,120,960]{2,1,0:T(8,128)(2,1)}, u32[]{:S(2)}, u32[]{:S(2)}) collective-permute-start(bf16[4,120,960]{2,1,0:T(8,128)(2,1)} %dynamic-slice_bitcast_fusion.3), channel_id=1, source_target_pairs={{0,1},{1,0},{2,3},{3,2},{4,5},{5,4},{6,7},{7,6},{8,9},{9,8},{10,11... | collective-permute-start | bytes 2764808 | tf_op jit(solution)/shard_map/ppermute | solution.py:693
  416.1 8.0 %collective-permute-start.24 = (f32[320,240]{1,0:T(8,128)S(1)}, f32[320,240]{1,0:T(8,128)S(1)}, u32[]{:S(2)}, u32[]{:S(2)}) collective-permute-start(f32[320,240]{1,0:T(8,128)S(1)} %get-tuple-element.446), channel_id=1, source_target_pairs={{0,24},{1,25},{2,26},{3,27},{4,28},{5,29},{6,30},{7,31}} | collective-permute-start | bytes 921608 | tf_op jit(solution)/shard_map/ppermute | solution.py:902
  417.8 8.7 %collective-permute-start.21 = (f32[320,240]{1,0:T(8,128)S(1)}, f32[320,240]{1,0:T(8,128)S(1)}, u32[]{:S(2)}, u32[]{:S(2)}) collective-permute-start(f32[320,240]{1,0:T(8,128)S(1)} %get-tuple-element.449), channel_id=1, source_target_pairs={{24,16},{25,17},{26,18},{27,19},{28,20},{29,21},{30,22},{31,23}} | collective-permute-start | bytes 921608 | tf_op jit(solution)/shard_map/ppermute | solution.py:902
  418.5 8.0 %collective-permute-start.20 = (f32[320,240]{1,0:T(8,128)S(1)}, f32[320,240]{1,0:T(8,128)S(1)}, u32[]{:S(2)}, u32[]{:S(2)}) collective-permute-start(f32[320,240]{1,0:T(8,128)S(1)} %get-tuple-element.450), channel_id=1, source_target_pairs={{24,8},{25,9},{26,10},{27,11},{28,12},{29,13},{30,14},{31,15}} | collective-permute-start | bytes 921608 | tf_op jit(solution)/shard_map/ppermute | solution.py:902
  419.1 6.4 %collective-permute-start.23 = (f32[320,240]{1,0:T(8,128)S(1)}, f32[320,240]{1,0:T(8,128)S(1)}, u32[]{:S(2)}, u32[]{:S(2)}) collective-permute-start(f32[320,240]{1,0:T(8,128)S(1)} %get-tuple-element.447), channel_id=1, source_target_pairs={{0,16},{1,17},{2,18},{3,19},{4,20},{5,21},{6,22},{7,23}} | collective-permute-start | bytes 921608 | tf_op jit(solution)/shard_map/ppermute | solution.py:902
  420.5 5.1 %collective-permute-start.22 = (f32[320,240]{1,0:T(8,128)S(1)}, f32[320,240]{1,0:T(8,128)S(1)}, u32[]{:S(2)}, u32[]{:S(2)}) collective-permute-start(f32[320,240]{1,0:T(8,128)S(1)} %get-tuple-element.445), channel_id=1, source_target_pairs={{0,8},{1,9},{2,10},{3,11},{4,12},{5,13},{6,14},{7,15}} | collective-permute-start | bytes 921608 | tf_op jit(solution)/shard_map/ppermute | solution.py:902
  424.1 8.4 %collective-permute-start.19 = (f32[320,240]{1,0:T(8,128)S(1)}, f32[320,240]{1,0:T(8,128)S(1)}, u32[]{:S(2)}, u32[]{:S(2)}) collective-permute-start(f32[320,240]{1,0:T(8,128)S(1)} %get-tuple-element.448), channel_id=1, source_target_pairs={{24,0},{25,1},{26,2},{27,3},{28,4},{29,5},{30,6},{31,7}} | collective-permute-start | bytes 921608 | tf_op jit(solution)/shard_map/ppermute | solution.py:902
  425.6 7.8 %collective-permute-start.25 = (bf16[1,120,1600]{2,1,0:T(8,128)(2,1)S(1)}, bf16[1,120,1600]{2,1,0:T(8,128)(2,1)S(1)}, u32[]{:S(2)}, u32[]{:S(2)}) collective-permute-start(bf16[1,120,1600]{2,1,0:T(8,128)(2,1)S(1)} %dynamic-slice_bitcast_fusion.4), channel_id=1, source_target_pairs={{0,1},{1,0},{2,3},{3,2},{4,5},{5,4},{6,7},{7,6},{8,9},{9,8},{10,11... | collective-permute-start | bytes 1152008 | tf_op jit(solution)/shard_map/ppermute | solution.py:693
  (22 other events, 154.0 us)
Sparse Core Ops, SparseCore 0:
  215.5 61.4 reduce-scatter.5
  279.4 49.6 reduce-scatter.11
  331.5 49.1 reduce-scatter.7
  382.9 52.4 reduce-scatter.13
  437.7 25.5 reduce-scatter.9

commit v4 on v3

--- a/solution.py
+++ b/solution.py
@@ -592,7 +592,8 @@
     scratch.append(pltpu.SemaphoreType.DMA((len(shapes), 2, 2)))
     scratch.append(pltpu.SemaphoreType.DMA((1,)))
     blocks = [*tables, *edge_parts, *inbound]
-    tables = [pltpu.with_memory_space_constraint(array, pltpu.VMEM) for array in tables]
+    kept = len(tables) + (0 if sizes["backward"] else len(edge_parts))
+    blocks[:kept] = [pltpu.with_memory_space_constraint(array, pltpu.VMEM) for array in blocks[:kept]]
     first_alias = 1 + len(blocks) + len(weights) + len(reads)
     sizes = dict(
         sizes,
@@ -626,9 +627,7 @@
         name=name,
     )(
         lengths,
-        *tables,
-        *edge_parts,
-        *inbound,
+        *blocks,
         *[pltpu.with_memory_space_constraint(weight, pltpu.VMEM) for weight in weights],
         *[pltpu.with_memory_space_constraint(array, pltpu.HBM) for array in (*reads, *aliased)],
     )
@@ -662,6 +661,29 @@
     return input_parts, cotangent_parts
 
 
+def spread_ends(results, input_grads):
+    sections, section = lax.axis_size("pipe"), lax.axis_index("pipe")
+    last = sections - 1
+    columns = results.shape[1] // sections
+
+    def block(value, at):
+        return value[:, at * columns : (at + 1) * columns]
+
+    outputs = jnp.where(section == last, block(results, last), 0.0)
+    grads = jnp.where(section == 0, block(input_grads, 0), 0.0)
+    for target in range(last):
+        mirror = last - target
+        if mirror == target:
+            outputs += lax.ppermute(block(results, target), "pipe", [(last, target)])
+            grads += lax.ppermute(block(input_grads, target), "pipe", [(0, target)])
+            continue
+        sent = jnp.where(section == 0, block(input_grads, mirror), block(results, target))
+        got = lax.ppermute(sent, "pipe", [(last, target), (0, mirror)])
+        outputs = jnp.where(section == target, got, outputs)
+        grads = jnp.where(section == mirror, got, grads)
+    return outputs, grads
+
+
 def after(values, *tokens):
     return lax.optimization_barrier((values, tokens))[0]
 
@@ -670,40 +692,40 @@
     return with_layout_constraint(value, Layout(major_to_minor=(0, 1)))
 
 
-def odd_device():
-    return lax.axis_index("dp") % 2
-
-
-def pair_view(value):
-    devices = lax.axis_size("dp")
+def cube_view(value):
+    bits = lax.axis_size("dp").bit_length() - 1
     rows, columns = value.shape
-    return value.reshape(devices // 2, 2, rows // devices, columns)
-
-
-def neighbours_half(view):
-    return lax.dynamic_index_in_dim(view, 1 - odd_device(), 1, keepdims=False)
-
-
-def own_half(view):
-    return lax.dynamic_index_in_dim(view, odd_device(), 1, keepdims=False)
-
-
-def to_neighbour(part):
-    devices = lax.axis_size("dp")
-    return lax.ppermute(part, "dp", [(i, i ^ 1) for i in range(devices)])
-
-
-def line_scatter(part):
-    devices = lax.axis_size("dp")
-    lines = [list(range(first, devices, 2)) for first in range(2)]
-    line, rows, columns = part.shape
-    return lax.psum_scatter(
-        part.reshape(line * rows, columns),
-        "dp",
-        scatter_dimension=0,
-        tiled=True,
-        axis_index_groups=lines,
-    )
+    return value.reshape((2,) * bits + (rows >> bits, columns))
+
+
+class Piece:
+    def __init__(self, value, bits):
+        self.value, self.bits, self.got = value, list(bits), None
+
+    def send(self, *tokens):
+        devices = lax.axis_size("dp")
+        bit = self.bits.pop(0)
+        axis = devices.bit_length() - 2 - bit
+        mine = (lax.axis_index("dp") >> bit) & 1
+        sent = lax.dynamic_index_in_dim(self.value, 1 - mine, axis)
+        if tokens:
+            sent = after(sent, *tokens)
+        self.kept = (axis, mine)
+        self.got = lax.ppermute(sent, "dp", [(i, i ^ (1 << bit)) for i in range(devices)])
+        return sent
+
+    def take(self, *tokens):
+        axis, mine = self.kept
+        got = after(self.got, *tokens) if tokens else self.got
+        self.value = lax.dynamic_index_in_dim(self.value, mine, axis) + got
+        return self.value
+
+    def finish(self, *tokens):
+        self.take(*tokens)
+        while self.bits:
+            self.send()
+            self.take()
+        return self.value.reshape(self.value.shape[-2:])
 
 
 def per_device(
@@ -855,52 +877,70 @@
         right = right.reshape(2 * total_rows, right.shape[-1])
         return by_rows(dot_rows(left, right).astype(BF16))
 
-    heads_grads = product(normed_attn, heads_grad)
-    line = lax.axis_size("dp") // 2
-    own_heads = line_scatter(heads_grads.reshape(line, width // line, all_width))
-    gate_view = pair_view(product(*after((normed_mlp, gate_grad), heads_grads)))
-    gate_sent = neighbours_half(gate_view)
-    gate_got = to_neighbour(gate_sent)
-    up_view = pair_view(product(*after((normed_mlp, up_grad), gate_sent)))
-    up_sent = neighbours_half(up_view)
-    up_got = to_neighbour(up_sent)
-    down_view = pair_view(product(*after((inner, branch), up_sent)))
-    down_sent = neighbours_half(down_view)
-    down_got = to_neighbour(down_sent)
-    proj_view = pair_view(product(*after((mixed, attn_grad), down_sent)))
-    proj_sent = neighbours_half(proj_view)
-    proj_got = to_neighbour(proj_sent)
-
-    gate_part = own_half(gate_view) + after(gate_got, proj_sent)
-    grad_gate = line_scatter(gate_part)
-    up_part = own_half(up_view) + after(up_got, gate_part)
-    grad_up = line_scatter(after(up_part, own_heads))
-    down_part = own_half(down_view) + after(down_got, up_part)
-    grad_down = line_scatter(after(down_part, grad_gate))
-    proj_part = own_half(proj_view) + after(proj_got, down_part)
-    grad_proj = line_scatter(after(proj_part, grad_up)).astype(F32)
-    grad_gate, grad_up, grad_down = [
-        grad.astype(F32) for grad in (grad_gate, grad_up, grad_down)
+    bits = lax.axis_size("dp").bit_length() - 1
+    across_first, along_first = range(bits), range(1, bits)
+    attn = Piece(cube_view(product(normed_attn, heads_grad)), along_first)
+    token = attn.send()
+    gate = Piece(cube_view(product(*after((normed_mlp, gate_grad), token))), across_first)
+    token = gate.send()
+    gain_sums = jnp.swapaxes(jnp.sum(gains, axis=(0, 1, 3)), 0, 1).astype(BF16)
+    proj_product = product(*after((mixed, attn_grad), token))
+    proj = Piece(cube_view(jnp.concatenate([proj_product, gain_sums], axis=1)), along_first)
+    token = proj.send()
+    attn.take(token)
+    token = attn.send()
+    up = Piece(cube_view(product(*after((normed_mlp, up_grad), token))), across_first)
+    token = up.send()
+    gate.take(token)
+    token = gate.send()
+    down_view = cube_view(product(*after((inner, branch), token)))
+    part = down_view.shape[-2] * 3 // 5
+    down = [Piece(view, across_first) for view in (down_view[..., :part, :], down_view[..., part:, :])]
+    proj.take(down_view)
+    token = proj.send()
+    while attn.bits:
+        attn.take(token)
+        token = attn.send()
+    token = attn.take(token)
+    gate.take(token)
+    token = gate.send()
+    while proj.bits:
+        proj.take(token)
+        token = proj.send()
+    token = proj.take(token)
+    up.take(token)
+    token = up.send()
+    token = down[0].send(token)
+    token = down[1].send(token)
+    token = grad_gate = gate.finish(token)
+    attn.bits, proj.bits = [0], [0]
+    token = attn.send(token)
+    up.take(token)
+    token = up.send()
+    token = proj.send(token)
+    down[0].take(token)
+    token = down[0].send()
+    down[0].take(token)
+    token = down[0].send()
+    down[1].take(token)
+    token = down[1].send()
+    token = grad_up = up.finish(token)
+    token = grad_heads = attn.finish(token)
+    token = grad_proj = proj.finish(token)
+    token = down_end = down[0].finish(token)
+    down[1].take(token)
+    token = down[1].send()
+    layer_output, grad_input = spread_ends(*after((results, input_grads), token))
+    grad_down = jnp.concatenate([down_end, down[1].finish(layer_output, grad_input)], axis=0)
+    grad_down = grad_down.astype(F32)
+    grad_gate, grad_up, grad_heads, grad_proj = [
+        grad.astype(F32) for grad in (grad_gate, grad_up, grad_heads, grad_proj)
     ]
-
-    own_heads = own_heads.reshape(1, 2, width // (2 * line), all_width)
-    heads_got = to_neighbour(neighbours_half(own_heads))
-    grad_heads = (own_half(own_heads) + heads_got)[0].astype(F32)
     grad_query = grad_heads[:, :width]
     grad_key = grad_heads[:, width : width + kv_width]
     grad_value = grad_heads[:, width + kv_width :]
-    gain_sums = jnp.sum(gains, axis=(0, 1, 3))
-    grad_gain_attn = lax.psum_scatter(gain_sums[0], "dp", scatter_dimension=0, tiled=True)
-    grad_gain_mlp = lax.psum_scatter(gain_sums[1], "dp", scatter_dimension=0, tiled=True)
-
-    def spread(store, source):
-        own = store[:, source * columns : (source + 1) * columns]
-        arrived = jnp.where(section == source, own, 0.0)
-        for target in range(sections):
-            if target != source:
-                block = store[:, target * columns : (target + 1) * columns]
-                arrived = arrived + lax.ppermute(block, "pipe", [(source, target)])
-        return arrived
+    grad_gain_attn, grad_gain_mlp = grad_proj[:, width], grad_proj[:, width + 1]
+    grad_proj = grad_proj[:, :width]
 
     position = jnp.arange(total_rows)
     long_rows = position < rows
@@ -910,9 +950,7 @@
     for m in range(MICRO):
         bound = jnp.where(micro == m, group[m], bound)
     valid = (offsets < bound)[:, None]
-    results, input_grads = after((results, input_grads), up_part)
-    layer_output = jnp.where(valid, spread(results, sections - 1), 0.0)
-    grad_input = spread(input_grads, 0)
+    layer_output = jnp.where(valid, layer_output, 0.0)
     return (
         layer_output,
         grad_input,

time: 480 us -> 447 us (0.931)
  blocking collectives: 25.9 us -> 0 us
  waiting for transfers between devices: 188 us -> 169 us
  starting transfers between devices: 33.3 us -> 49.2 us
  between operations: 15.5 us -> 1.86 us
  Pallas kernels: 145 us -> 152 us
  local copies, waits for them, and re-layouts: 18 us -> 24.6 us
    unnamed x1 -> x0, blocking collectives: 25.9 us -> none
    reduce_scatter x5 -> x0, waiting for transfers between devices: 22.7 us -> none  [line_scatter(): lax.psum_scatter(part.reshape(line * rows, columns), 'dp', scatter_dimens...]
    ppermute x11 -> x21, starting transfers between devices: 12.8 us -> 29.1 us  [the longest x18 24.6 us: send(): lax.ppermute(sent, 'dp', [(i, i ^ 1 << bit) for i in range(devices)])]
    dynamic_slice x0 -> x18, local copies, waits for them, and re-layouts: none -> 10.3 us  [send(): sent = lax.dynamic_index_in_dim(self.value, 1 - mine, axis)]
    broadcast_in_dim x4 -> x0, other arithmetic: 6.36 us -> none  [the longest x1 2.29 us: per_device(): grad_down[None]]
    pallas_call x18, Pallas kernels: 135 us -> 141 us  [run_tick(): pl.pallas_call(functools.partial(kernel, sizes), out_shape=outs, grid_spe...]
    convert_element_type x1 -> x5, other arithmetic: 0.06 us -> 5.6 us  [the longest x4 4.4 us: per_device(): grad.astype(F32)]
    add x5 -> x12, other arithmetic: 11.8 us -> 7.15 us  [take(): self.value = lax.dynamic_index_in_dim(self.value, mine, axis) + got]
  transfers between devices with their start and end apart: 33 -> 38, of which waited for: 7 -> 16; matrix products, arithmetic and copies ran while one was open for 9% -> 12% of each run, Pallas kernels for 25% -> 27%
where the time goes in v4:
time: 447 us; the launch traced here: 438 us
  waiting for transfers between devices  169 us (38%)
  Pallas kernels  152 us (34%)
  starting transfers between devices  49.2 us (11%)
  local copies, waits for them, and re-layouts  24.6 us (6%)
  matrix products  21 us (5%)
  other arithmetic  20.7 us (5%)
    pallas_call x18, Pallas kernels, run_tick(): pl.pallas_call(functools.partial(kernel, sizes), out_shape=outs, grid_spe...  141 us
    ppermute x18, waiting for transfers between devices, send(): lax.ppermute(sent, 'dp', [(i, i ^ 1 << bit) for i in range(devices)])  134 us
    ppermute x14, waiting for transfers between devices, per_device(): sent[tick] = lax.ppermute(rounded, 'pipe', route)  33.8 us
    ppermute x18, starting transfers between devices, send(): lax.ppermute(sent, 'dp', [(i, i ^ 1 << bit) for i in range(devices)])  24.6 us
    dot_general x5, matrix products, dot_rows(): lax.dot_general(left, right, (((0,), (0,)), ((), ())), preferred_element_...  21 us
    ppermute x14, starting transfers between devices, per_device(): sent[tick] = lax.ppermute(rounded, 'pipe', route)  13.2 us
    dynamic_slice x18, local copies, waits for them, and re-layouts, send(): sent = lax.dynamic_index_in_dim(self.value, 1 - mine, axis)  10.3 us
  transfers between devices with their start and end apart: 38, of which 16 were waited for; matrix products, arithmetic and copies ran while one was open for 12% of the time, Pallas kernels for 27%

profile of v4, /device:TPU:0, one launch (start us, length us, event | category | flops | bytes accessed | tf_op | source)
XLA Modules:
  0.0 438.4 jit_solution(5392970494033153057)
XLA Ops:
  5.0 4.3 collective-permute-start.2
  9.4 7.1 %load_weights.1 = (bf16[1600,960]{1,0:T(8,128)(2,1)S(1)}, bf16[960,1600]{1,0:T(8,128)(2,1)S(1)}, bf16[960,960]{1,0:T(8,128)(2,1)S(1)}, bf16[960,2560]{1,0:T(8,12...) custom-call(bf16[320,960]{1,0:T(8,128)(2,1)} %bitcast.87, ...), custom_call_target="tpu_custom_call" | custom-call | tf_op jit(solution)/shard_map/load_weights/pallas_call | solution.py:529
  17.8 12.1 %layer_pair_forward.9 = (bf16[128,960]{1,0:T(8,128)(2,1)S(1)}, f32[320,960]{1,0:T(8,128)}, f32[2,320,960]{2,1,0:T(8,128)}, bf16[2,320,960]{2,1,0:T(8,128)(2,1)},...) custom-call(s32[1,4]{1,0:T(1,128)S(1)} %copy-done.1, ...), custom_call_target="tpu_custom_call" | custom-call | flops 5033164800 | bytes 19660800 | tf_op jit(solution)/shard_map/layer_pair_forward/pallas_call | solution.py:609
  31.2 12.8 %layer_pair_forward.10 = (bf16[128,960]{1,0:T(8,128)(2,1)S(1)}, f32[320,960]{1,0:T(8,128)}, f32[2,320,960]{2,1,0:T(8,128)}, bf16[2,320,960]{2,1,0:T(8,128)(2,1)}...) custom-call(s32[1,4]{1,0:T(1,128)S(1)} %copy-done.1, ...), custom_call_target="tpu_custom_call", output_to_operand_aliasing={{1}: (14, {}), {2}: (15, {}), {3}: (16, {}), {4}: (17, {}),... | custom-call | flops 5033164800 | bytes 19660800 | tf_op jit(solution)/shard_map/layer_pair_forward/pallas_call | solution.py:609
  45.3 11.8 %layer_pair_forward.11 = (bf16[128,960]{1,0:T(8,128)(2,1)S(1)}, f32[320,960]{1,0:T(8,128)}, f32[2,320,960]{2,1,0:T(8,128)}, bf16[2,320,960]{2,1,0:T(8,128)(2,1)}...) custom-call(s32[1,4]{1,0:T(1,128)S(1)} %copy-done.1, ...), custom_call_target="tpu_custom_call", output_to_operand_aliasing={{1}: (15, {}), {2}: (16, {}), {3}: (17, {}), {4}: (18, {}),... | custom-call | flops 5033164800 | bytes 19660800 | tf_op jit(solution)/shard_map/layer_pair_forward/pallas_call | solution.py:609
  58.4 9.0 %layer_pair_forward.12 = (bf16[128,960]{1,0:T(8,128)(2,1)S(1)}, f32[320,960]{1,0:T(8,128)}, f32[2,320,960]{2,1,0:T(8,128)}, bf16[2,320,960]{2,1,0:T(8,128)(2,1)}...) custom-call(s32[1,4]{1,0:T(1,128)S(1)} %copy-done.1, ...), custom_call_target="tpu_custom_call", output_to_operand_aliasing={{1}: (11, {}), {2}: (12, {}), {3}: (13, {}), {4}: (14, {}),... | custom-call | flops 5033164800 | bytes 19660800 | tf_op jit(solution)/shard_map/layer_pair_forward/pallas_call | solution.py:609
  68.2 3.4 turn_weights.3
  73.2 7.4 %layer_pair_forward.14 = (bf16[128,960]{1,0:T(8,128)(2,1)S(1)}, f32[320,960]{1,0:T(8,128)}, f32[2,320,960]{2,1,0:T(8,128)}, bf16[2,320,960]{2,1,0:T(8,128)(2,1)}...) custom-call(s32[1,4]{1,0:T(1,128)S(1)} %copy-done.1, ...), custom_call_target="tpu_custom_call", output_to_operand_aliasing={{1}: (11, {}), {2}: (12, {}), {3}: (13, {}), {4}: (14, {}),... | custom-call | flops 5033164800 | bytes 19660800 | tf_op jit(solution)/shard_map/layer_pair_forward/pallas_call | solution.py:609
  82.9 8.5 %layer_pair_forward.16 = (bf16[128,960]{1,0:T(8,128)(2,1)}, f32[320,960]{1,0:T(8,128)}, f32[2,320,960]{2,1,0:T(8,128)}, bf16[2,320,960]{2,1,0:T(8,128)(2,1)}, bf...) custom-call(s32[1,4]{1,0:T(1,128)S(1)} %copy-done.1, ...), custom_call_target="tpu_custom_call", output_to_operand_aliasing={{1}: (11, {}), {2}: (12, {}), {3}: (13, {}), {4}: (14, {}),... | custom-call | flops 5033164800 | bytes 19660800 | tf_op jit(solution)/shard_map/layer_pair_forward/pallas_call | solution.py:609
  95.8 9.1 %layer_pair_backward.10 = (bf16[128,960]{1,0:T(8,128)(2,1)S(1)}, f32[320,960]{1,0:T(8,128)}, bf16[2,320,960]{2,1,0:T(8,128)(2,1)}, bf16[2,320,2560]{2,1,0:T(8,12...) custom-call(s32[1,4]{1,0:T(1,128)S(1)} %copy-done.1, ...), custom_call_target="tpu_custom_call", output_to_operand_aliasing={{1}: (19, {}), {2}: (20, {}), {3}: (21, {}), {4}: (22, {}),... | custom-call | flops 5033164800 | bytes 19660800 | tf_op jit(solution)/shard_map/layer_pair_backward/pallas_call | solution.py:609
  108.2 8.1 %layer_pair_backward.12 = (bf16[128,960]{1,0:T(8,128)(2,1)S(1)}, f32[320,960]{1,0:T(8,128)}, bf16[2,320,960]{2,1,0:T(8,128)(2,1)}, bf16[2,320,2560]{2,1,0:T(8,12...) custom-call(s32[1,4]{1,0:T(1,128)S(1)} %copy-done.1, ...), custom_call_target="tpu_custom_call", output_to_operand_aliasing={{1}: (16, {}), {2}: (17, {}), {3}: (18, {}), {4}: (19, {}),... | custom-call | flops 5033164800 | bytes 19660800 | tf_op jit(solution)/shard_map/layer_pair_backward/pallas_call | solution.py:609
  119.3 7.9 %layer_pair_backward.14 = (bf16[128,960]{1,0:T(8,128)(2,1)S(1)}, f32[320,960]{1,0:T(8,128)}, bf16[2,320,960]{2,1,0:T(8,128)(2,1)}, bf16[2,320,2560]{2,1,0:T(8,12...) custom-call(s32[1,4]{1,0:T(1,128)S(1)} %copy-done.1, ...), custom_call_target="tpu_custom_call", output_to_operand_aliasing={{1}: (16, {}), {2}: (17, {}), {3}: (18, {}), {4}: (19, {}),... | custom-call | flops 5033164800 | bytes 19660800 | tf_op jit(solution)/shard_map/layer_pair_backward/pallas_call | solution.py:609
  128.5 33.7 %collective-permute-done.13.refs_4_ = bf16[128,960]{1,0:T(8,128)(2,1)S(1)} collective-permute-done((bf16[128,960]{1,0:T(8,128)(2,1)S(1)}, bf16[128,960]{1,0:T(8,128)(2,1)S(1)}, u32[]{:S(2)}, u32[]{:S(2)}) %collective-permute-start.13) | collective-permute-done | bytes 245792 | tf_op jit(solution)/shard_map/ppermute | solution.py:871
  162.2 14.7 %layer_pair_backward.15 = (bf16[128,960]{1,0:T(8,128)(2,1)S(1)}, f32[320,960]{1,0:T(8,128)}, bf16[2,320,960]{2,1,0:T(8,128)(2,1)}, bf16[2,320,2560]{2,1,0:T(8,12...) custom-call(s32[1,4]{1,0:T(1,128)S(1)} %copy-done.1, ...), custom_call_target="tpu_custom_call", output_to_operand_aliasing={{1}: (16, {}), {2}: (17, {}), {3}: (18, {}), {4}: (19, {}),... | custom-call | flops 5033164800 | bytes 19660800 | tf_op jit(solution)/shard_map/layer_pair_backward/pallas_call | solution.py:609
  178.2 15.9 %layer_pair_backward.16 = (bf16[128,960]{1,0:T(8,128)(2,1)}, f32[320,960]{1,0:T(8,128)}, bf16[2,320,960]{2,1,0:T(8,128)(2,1)}, bf16[2,320,2560]{2,1,0:T(8,128)(2...) custom-call(s32[1,4]{1,0:T(1,128)S(1)} %copy-done.1, ...), custom_call_target="tpu_custom_call", output_to_operand_aliasing={{1}: (16, {}), {2}: (17, {}), {3}: (18, {}), {4}: (19, {}),... | custom-call | flops 5033164800 | bytes 19660800 | tf_op jit(solution)/shard_map/layer_pair_backward/pallas_call | solution.py:609
  194.2 15.5 %layer_pair_backward.17 = (bf16[128,960]{1,0:T(8,128)(2,1)}, f32[320,960]{1,0:T(8,128)}, bf16[2,320,960]{2,1,0:T(8,128)(2,1)}, bf16[2,320,2560]{2,1,0:T(8,128)(2...) custom-call(s32[1,4]{1,0:T(1,128)S(1)} %copy-done.1, ...), custom_call_target="tpu_custom_call", output_to_operand_aliasing={{1}: (16, {}), {2}: (17, {}), {3}: (18, {}), {4}: (19, {}),... | custom-call | flops 5033164800 | bytes 19660800 | tf_op jit(solution)/shard_map/layer_pair_backward/pallas_call | solution.py:609
  209.7 4.6 %bitcast_convert_fusion.3 = bf16[960,1600]{1,0:T(8,128)(2,1)S(1)} fusion(bf16[2,320,960]{2,1,0:T(8,128)(2,1)S(1)} %copy-done.7, bf16[2,320,1600]{2,1,0:T(8,128)(2,1)} %get-tuple-element.411), kind=kOutput, calls=%fused_computation.3 | convolution fusion | flops 1967616000 | bytes 6348800 | tf_op jit(solution)/shard_map/dot_general | solution.py:38
  217.3 4.5 %bitcast_convert_fusion.2 = bf16[960,2560]{1,0:T(8,128)(2,1)S(1)} fusion(bf16[2,320,960]{2,1,0:T(8,128)(2,1)S(1)} %copy-done.9, bf16[2,320,2560]{2,1,0:T(8,128)(2,1)S(1)} %copy-done.3), kind=kOutput, calls=%fused_computation.2 | convolution fusion | flops 3148185600 | bytes 9420800 | tf_op jit(solution)/shard_map/dot_general | solution.py:38
  233.0 29.2 %collective-permute-done.18 = bf16[2,1,2,120,1600]{4,3,2,1,0:T(8,128)(2,1)S(1)} collective-permute-done((bf16[2,1,2,120,1600]{4,3,2,1,0:T(8,128)(2,1)}, bf16[2,1,2,120,1600]{4,3,2,1,0:T(8,128)(2,1)S(1)}, u32[]{:S(2)}, u32[]{:S(2)}) %collective-permute-start.18) | collective-permute-done | bytes 1536032 | tf_op jit(solution)/shard_map/ppermute | solution.py:714
  264.5 4.3 bitcast_convert_fusion.1
  270.6 11.1 %collective-permute-done.17 = bf16[2,2,1,120,2560]{4,3,2,1,0:T(8,128)(2,1)} collective-permute-done((bf16[2,2,1,120,2560]{4,3,2,1,0:T(8,128)(2,1)}, bf16[2,2,1,120,2560]{4,3,2,1,0:T(8,128)(2,1)}, u32[]{:S(2)}, u32[]{:S(2)}) %collective-permute-start.17) | collective-permute-done | bytes 2457632 | tf_op jit(solution)/shard_map/ppermute | solution.py:714
  285.3 4.5 %bitcast_convert_fusion = bf16[2560,960]{1,0:T(8,128)(2,1)S(1)} fusion(bf16[2,320,2560]{2,1,0:T(8,128)(2,1)S(1)} %copy-done.2, bf16[2,320,960]{2,1,0:T(8,128)(2,1)S(1)} %copy-done.10), kind=kOutput, calls=%fused_computation | convolution fusion | flops 3148185600 | bytes 9420800 | tf_op jit(solution)/shard_map/dot_general | solution.py:38
  289.9 5.5 %collective-permute-done.20 = bf16[2,1,2,120,962]{4,3,2,1,0:T(8,128)(2,1)S(1)} collective-permute-done((bf16[2,1,2,120,962]{4,3,2,1,0:T(8,128)(2,1)S(1)}, bf16[2,1,2,120,962]{4,3,2,1,0:T(8,128)(2,1)S(1)}, u32[]{:S(2)}, u32[]{:S(2)}) %collective-permute-start.20) | collective-permute-done | bytes 923552 | tf_op jit(solution)/shard_map/ppermute | solution.py:714
  297.5 22.8 %collective-permute-done.22 = bf16[2,1,1,120,2560]{4,3,2,1,0:T(8,128)(2,1)S(1)} collective-permute-done((bf16[2,1,1,120,2560]{4,3,2,1,0:T(8,128)(2,1)S(1)}, bf16[2,1,1,120,2560]{4,3,2,1,0:T(8,128)(2,1)S(1)}, u32[]{:S(2)}, u32[]{:S(2)}) %collective-permute-start.22) | collective-permute-done | bytes 1228832 | tf_op jit(solution)/shard_map/ppermute | solution.py:714
  322.4 5.4 %collective-permute-done.19 = bf16[2,2,1,120,2560]{4,3,2,1,0:T(8,128)(2,1)S(1)} collective-permute-done((bf16[2,2,1,120,2560]{4,3,2,1,0:T(8,128)(2,1)S(1)}, bf16[2,2,1,120,2560]{4,3,2,1,0:T(8,128)(2,1)S(1)}, u32[]{:S(2)}, u32[]{:S(2)}) %collective-permute-start.19) | collective-permute-done | bytes 2457632 | tf_op jit(solution)/shard_map/ppermute | solution.py:714
  349.6 9.4 %collective-permute-done.26 = bf16[2,1,1,120,2560]{4,3,2,1,0:T(8,128)(2,1)} collective-permute-done((bf16[2,1,1,120,2560]{4,3,2,1,0:T(8,128)(2,1)}, bf16[2,1,1,120,2560]{4,3,2,1,0:T(8,128)(2,1)}, u32[]{:S(2)}, u32[]{:S(2)}) %collective-permute-start.26) | collective-permute-done | bytes 1228832 | tf_op jit(solution)/shard_map/ppermute | solution.py:714
  361.7 12.2 %collective-permute-done.25 = bf16[2,2,1,192,960]{4,3,2,1,0:T(8,128)(2,1)S(1)} collective-permute-done((bf16[2,2,1,192,960]{4,3,2,1,0:T(8,128)(2,1)S(1)}, bf16[2,2,1,192,960]{4,3,2,1,0:T(8,128)(2,1)S(1)}, u32[]{:S(2)}, u32[]{:S(2)}) %collective-permute-start.25) | collective-permute-done | bytes 1474592 | tf_op jit(solution)/shard_map/ppermute | solution.py:714
  384.8 13.7 %collective-permute-done.33 = bf16[1,1,1,120,962]{4,3,2,1,0:T(8,128)(2,1)S(1)} collective-permute-done((bf16[1,1,1,120,962]{4,3,2,1,0:T(8,128)(2,1)S(1)}, bf16[1,1,1,120,962]{4,3,2,1,0:T(8,128)(2,1)S(1)}, u32[]{:S(2)}, u32[]{:S(2)}) %collective-permute-start.33) | collective-permute-done | bytes 230912 | tf_op jit(solution)/shard_map/ppermute | solution.py:714
  398.5 7.2 %collective-permute-done.27 = bf16[2,1,1,192,960]{4,3,2,1,0:T(8,128)(2,1)} collective-permute-done((bf16[2,1,1,192,960]{4,3,2,1,0:T(8,128)(2,1)}, bf16[2,1,1,192,960]{4,3,2,1,0:T(8,128)(2,1)}, u32[]{:S(2)}, u32[]{:S(2)}) %collective-permute-start.27) | collective-permute-done | bytes 737312 | tf_op jit(solution)/shard_map/ppermute | solution.py:714
  411.6 6.3 %collective-permute-done.28 = bf16[2,1,1,128,960]{3,4,2,1,0:T(8,128)(2,1)S(1)} collective-permute-done((bf16[2,1,1,128,960]{3,4,2,1,0:T(8,128)(2,1)S(1)}, bf16[2,1,1,128,960]{3,4,2,1,0:T(8,128)(2,1)S(1)}, u32[]{:S(2)}, u32[]{:S(2)}) %collective-permute-start.28) | collective-permute-done | bytes 491552 | tf_op jit(solution)/shard_map/ppermute | solution.py:714
  424.3 3.8 collective-permute-done.36
  430.6 6.2 %collective-permute-done.37 = bf16[1,1,1,128,960]{3,4,2,1,0:T(8,128)(2,1)S(1)} collective-permute-done((bf16[1,1,1,128,960]{3,4,2,1,0:T(8,128)(2,1)S(1)}, bf16[1,1,1,128,960]{3,4,2,1,0:T(8,128)(2,1)S(1)}, u32[]{:S(2)}, u32[]{:S(2)}) %collective-permute-start.37) | collective-permute-done | bytes 245792 | tf_op jit(solution)/shard_map/ppermute | solution.py:714
  (192 shorter events, 104.5 us)
Async XLA Ops:
  2.5 15.3 %collective-permute-start = (bf16[320,240]{1,0:T(8,128)(2,1)}, bf16[320,240]{1,0:T(8,128)(2,1)}, u32[]{:S(2)}, u32[]{:S(2)}) collective-permute-start(bf16[320,240]{1,0:T(8,128)(2,1)} %get-tuple-element.485), channel_id=1, source_target_pairs={{8,0},{16,24},{9,1},{17,25},{10,2},{18,26},{11,3},{19,27},{12,4},{... | collective-permute-start | bytes 460808 | tf_op jit(solution)/shard_map/ppermute | solution.py:659
  3.7 14.0 %collective-permute-start.1 = (bf16[320,240]{1,0:T(8,128)(2,1)}, bf16[320,240]{1,0:T(8,128)(2,1)}, u32[]{:S(2)}, u32[]{:S(2)}) collective-permute-start(bf16[320,240]{1,0:T(8,128)(2,1)} %get-tuple-element.484), channel_id=1, source_target_pairs={{16,0},{8,24},{17,1},{9,25},{18,2},{10,26},{19,3},{11,27},{20,4},{... | collective-permute-start | bytes 460808 | tf_op jit(solution)/shard_map/ppermute | solution.py:659
  5.0 12.7 %collective-permute-start.2 = (bf16[320,240]{1,0:T(8,128)(2,1)}, bf16[320,240]{1,0:T(8,128)(2,1)}, u32[]{:S(2)}, u32[]{:S(2)}) collective-permute-start(bf16[320,240]{1,0:T(8,128)(2,1)} %get-tuple-element.483), channel_id=1, source_target_pairs={{24,0},{0,24},{25,1},{1,25},{26,2},{2,26},{27,3},{3,27},{28,4},{4,... | collective-permute-start | bytes 460808 | tf_op jit(solution)/shard_map/ppermute | solution.py:659
  29.9 15.4 %collective-permute-start.3 = (bf16[128,960]{1,0:T(8,128)(2,1)S(1)}, bf16[128,960]{1,0:T(8,128)(2,1)S(1)}, u32[]{:S(2)}, u32[]{:S(2)}) collective-permute-start(bf16[128,960]{1,0:T(8,128)(2,1)S(1)} %get-tuple-element.238), channel_id=1, source_target_pairs={{0,8},{1,9},{2,10},{3,11},{4,12},{5,13},{6,14},{7,15}} | collective-permute-start | bytes 737288 | tf_op jit(solution)/shard_map/ppermute | solution.py:826
  44.0 14.4 %collective-permute-start.5 = (bf16[128,960]{1,0:T(8,128)(2,1)S(1)}, bf16[128,960]{1,0:T(8,128)(2,1)S(1)}, u32[]{:S(2)}, u32[]{:S(2)}) collective-permute-start(bf16[128,960]{1,0:T(8,128)(2,1)S(1)} %get-tuple-element.260), channel_id=1, source_target_pairs={{0,8},{1,9},{2,10},{3,11},{4,12},{5,13},{6,14},{7,15}} | collective-permute-start | bytes 737288 | tf_op jit(solution)/shard_map/ppermute | solution.py:826
  57.1 14.4 %collective-permute-start.4 = (bf16[128,960]{1,0:T(8,128)(2,1)S(1)}, bf16[128,960]{1,0:T(8,128)(2,1)S(1)}, u32[]{:S(2)}, u32[]{:S(2)}) collective-permute-start(bf16[128,960]{1,0:T(8,128)(2,1)S(1)} %get-tuple-element.259), channel_id=1, source_target_pairs={{0,8},{8,16},{1,9},{9,17},{2,10},{10,18},{3,11},{11,19},{4,12},{12... | collective-permute-start | bytes 737288 | tf_op jit(solution)/shard_map/ppermute | solution.py:826
  72.5 8.8 %collective-permute-start.6 = (bf16[128,960]{1,0:T(8,128)(2,1)S(1)}, bf16[128,960]{1,0:T(8,128)(2,1)S(1)}, u32[]{:S(2)}, u32[]{:S(2)}) collective-permute-start(bf16[128,960]{1,0:T(8,128)(2,1)S(1)} %get-tuple-element.281), channel_id=1, source_target_pairs={{8,16},{16,24},{9,17},{17,25},{10,18},{18,26},{11,19},{19,27},{12,... | collective-permute-start | bytes 737288 | tf_op jit(solution)/shard_map/ppermute | solution.py:826
  82.2 9.2 %collective-permute-start.8 = (bf16[128,960]{1,0:T(8,128)(2,1)S(1)}, bf16[128,960]{1,0:T(8,128)(2,1)S(1)}, u32[]{:S(2)}, u32[]{:S(2)}) collective-permute-start(bf16[128,960]{1,0:T(8,128)(2,1)S(1)} %get-tuple-element.303), channel_id=1, source_target_pairs={{16,24},{17,25},{18,26},{19,27},{20,28},{21,29},{22,30},{23,31}} | collective-permute-start | bytes 737288 | tf_op jit(solution)/shard_map/ppermute | solution.py:826
  95.1 10.4 %collective-permute-start.10 = (bf16[128,960]{1,0:T(8,128)(2,1)S(1)}, bf16[128,960]{1,0:T(8,128)(2,1)S(1)}, u32[]{:S(2)}, u32[]{:S(2)}) collective-permute-start(bf16[128,960]{1,0:T(8,128)(2,1)S(1)} %get-tuple-element.342), channel_id=1, source_target_pairs={{24,16},{25,17},{26,18},{27,19},{28,20},{29,21},{30,22},{31,23}} | collective-permute-start | bytes 737288 | tf_op jit(solution)/shard_map/ppermute | solution.py:871
  107.5 9.5 %collective-permute-start.11 = (bf16[128,960]{1,0:T(8,128)(2,1)S(1)}, bf16[128,960]{1,0:T(8,128)(2,1)S(1)}, u32[]{:S(2)}, u32[]{:S(2)}) collective-permute-start(bf16[128,960]{1,0:T(8,128)(2,1)S(1)} %get-tuple-element.357), channel_id=1, source_target_pairs={{16,8},{24,16},{17,9},{25,17},{18,10},{26,18},{19,11},{27,19},{20,... | collective-permute-start | bytes 737288 | tf_op jit(solution)/shard_map/ppermute | solution.py:871
  117.9 44.2 %collective-permute-start.13 = (bf16[128,960]{1,0:T(8,128)(2,1)S(1)}, bf16[128,960]{1,0:T(8,128)(2,1)S(1)}, u32[]{:S(2)}, u32[]{:S(2)}) collective-permute-start(bf16[128,960]{1,0:T(8,128)(2,1)S(1)} %get-tuple-element.373), channel_id=1, source_target_pairs={{8,0},{16,8},{9,1},{17,9},{10,2},{18,10},{11,3},{19,11},{12,4},{20... | collective-permute-start | bytes 737288 | tf_op jit(solution)/shard_map/ppermute | solution.py:871
  127.2 51.0 %collective-permute-start.16 = (bf16[128,960]{1,0:T(8,128)(2,1)S(1)}, bf16[128,960]{1,0:T(8,128)(2,1)S(1)}, u32[]{:S(2)}, u32[]{:S(2)}) collective-permute-start(bf16[128,960]{1,0:T(8,128)(2,1)S(1)} %get-tuple-element.390), channel_id=1, source_target_pairs={{8,0},{9,1},{10,2},{11,3},{12,4},{13,5},{14,6},{15,7}} | collective-permute-start | bytes 737288 | tf_op jit(solution)/shard_map/ppermute | solution.py:871
  176.9 17.3 %collective-permute-start.15 = (bf16[128,960]{1,0:T(8,128)(2,1)S(1)}, bf16[128,960]{1,0:T(8,128)(2,1)S(1)}, u32[]{:S(2)}, u32[]{:S(2)}) collective-permute-start(bf16[128,960]{1,0:T(8,128)(2,1)S(1)} %get-tuple-element.389), channel_id=1, source_target_pairs={{8,0},{9,1},{10,2},{11,3},{12,4},{13,5},{14,6},{15,7}} | collective-permute-start | bytes 737288 | tf_op jit(solution)/shard_map/ppermute | solution.py:871
  215.6 46.6 %collective-permute-start.18 = (bf16[2,1,2,120,1600]{4,3,2,1,0:T(8,128)(2,1)}, bf16[2,1,2,120,1600]{4,3,2,1,0:T(8,128)(2,1)S(1)}, u32[]{:S(2)}, u32[]{:S(2)}) collective-permute-start(bf16[2,1,2,120,1600]{4,3,2,1,0:T(8,128)(2,1)} %constant_dynamic-slice_fusion.18), channel_id=1, source_target_pairs={{0,2},{1,3},{2,0},{3,1},{4,6},{5,7},{6,4},{7,5},{8,10},{9,11},{10,... | collective-permute-start | bytes 4608008 | tf_op jit(solution)/shard_map/ppermute | solution.py:714
  225.1 56.6 %collective-permute-start.17 = (bf16[2,2,1,120,2560]{4,3,2,1,0:T(8,128)(2,1)}, bf16[2,2,1,120,2560]{4,3,2,1,0:T(8,128)(2,1)}, u32[]{:S(2)}, u32[]{:S(2)}) collective-permute-start(bf16[2,2,1,120,2560]{4,3,2,1,0:T(8,128)(2,1)} %constant_dynamic-slice_fusion.17), channel_id=1, source_target_pairs={{0,1},{1,0},{2,3},{3,2},{4,5},{5,4},{6,7},{7,6},{8,9},{9,8},{10,11... | collective-permute-start | bytes 7372808 | tf_op jit(solution)/shard_map/ppermute | solution.py:714
  232.0 63.4 %collective-permute-start.20 = (bf16[2,1,2,120,962]{4,3,2,1,0:T(8,128)(2,1)S(1)}, bf16[2,1,2,120,962]{4,3,2,1,0:T(8,128)(2,1)S(1)}, u32[]{:S(2)}, u32[]{:S(2)}) collective-permute-start(bf16[2,1,2,120,962]{4,3,2,1,0:T(8,128)(2,1)S(1)} %constant_dynamic-slice_fusion.16), channel_id=1, source_target_pairs={{0,2},{1,3},{2,0},{3,1},{4,6},{5,7},{6,4},{7,5},{8,10},{9,11},{10,... | collective-permute-start | bytes 2770568 | tf_op jit(solution)/shard_map/ppermute | solution.py:714
  262.6 34.9 %collective-permute-start.23 = (bf16[1,1,2,120,1600]{4,3,2,1,0:T(8,128)(2,1)S(1)}, bf16[1,1,2,120,1600]{4,3,2,1,0:T(8,128)(2,1)S(1)}, u32[]{:S(2)}, u32[]{:S(2)}) collective-permute-start(bf16[1,1,2,120,1600]{4,3,2,1,0:T(8,128)(2,1)S(1)} %constant_dynamic-slice_fusion.15), channel_id=1, source_target_pairs={{0,4},{1,5},{2,6},{3,7},{4,0},{5,1},{6,2},{7,3},{8,12},{9,13},{10,... | collective-permute-start | bytes 2304008 | tf_op jit(solution)/shard_map/ppermute | solution.py:714
  269.0 58.8 %collective-permute-start.19 = (bf16[2,2,1,120,2560]{4,3,2,1,0:T(8,128)(2,1)S(1)}, bf16[2,2,1,120,2560]{4,3,2,1,0:T(8,128)(2,1)S(1)}, u32[]{:S(2)}, u32[]{:S(2)}) collective-permute-start(bf16[2,2,1,120,2560]{4,3,2,1,0:T(8,128)(2,1)S(1)} %constant_dynamic-slice_fusion.14), channel_id=1, source_target_pairs={{0,1},{1,0},{2,3},{3,2},{4,5},{5,4},{6,7},{7,6},{8,9},{9,8},{10,11... | collective-permute-start | bytes 7372808 | tf_op jit(solution)/shard_map/ppermute | solution.py:714
  284.0 36.4 %collective-permute-start.22 = (bf16[2,1,1,120,2560]{4,3,2,1,0:T(8,128)(2,1)S(1)}, bf16[2,1,1,120,2560]{4,3,2,1,0:T(8,128)(2,1)S(1)}, u32[]{:S(2)}, u32[]{:S(2)}) collective-permute-start(bf16[2,1,1,120,2560]{4,3,2,1,0:T(8,128)(2,1)S(1)} %constant_dynamic-slice_fusion.13), channel_id=1, source_target_pairs={{0,2},{1,3},{2,0},{3,1},{4,6},{5,7},{6,4},{7,5},{8,10},{9,11},{10,... | collective-permute-start | bytes 3686408 | tf_op jit(solution)/shard_map/ppermute | solution.py:714
  295.5 26.0 %collective-permute-start.21 = (bf16[1,1,2,120,962]{4,3,2,1,0:T(8,128)(2,1)S(1)}, bf16[1,1,2,120,962]{4,3,2,1,0:T(8,128)(2,1)S(1)}, u32[]{:S(2)}, u32[]{:S(2)}) collective-permute-start(bf16[1,1,2,120,962]{4,3,2,1,0:T(8,128)(2,1)S(1)} %constant_dynamic-slice_fusion.9), channel_id=1, source_target_pairs={{0,4},{1,5},{2,6},{3,7},{4,0},{5,1},{6,2},{7,3},{8,12},{9,13},{10,... | collective-permute-start | bytes 1385288 | tf_op jit(solution)/shard_map/ppermute | solution.py:714
  329.3 29.7 %collective-permute-start.26 = (bf16[2,1,1,120,2560]{4,3,2,1,0:T(8,128)(2,1)}, bf16[2,1,1,120,2560]{4,3,2,1,0:T(8,128)(2,1)}, u32[]{:S(2)}, u32[]{:S(2)}) collective-permute-start(bf16[2,1,1,120,2560]{4,3,2,1,0:T(8,128)(2,1)} %constant_dynamic-slice_fusion.7), channel_id=1, source_target_pairs={{0,2},{1,3},{2,0},{3,1},{4,6},{5,7},{6,4},{7,5},{8,10},{9,11},{10,... | collective-permute-start | bytes 3686408 | tf_op jit(solution)/shard_map/ppermute | solution.py:714
  332.0 12.4 %collective-permute-start.32 = (bf16[1,1,1,120,1600]{4,3,2,1,0:T(8,128)(2,1)}, bf16[1,1,1,120,1600]{4,3,2,1,0:T(8,128)(2,1)S(1)}, u32[]{:S(2)}, u32[]{:S(2)}) collective-permute-start(bf16[1,1,1,120,1600]{4,3,2,1,0:T(8,128)(2,1)} %constant_dynamic-slice_fusion.5), channel_id=1, source_target_pairs={{0,1},{1,0},{2,3},{3,2},{4,5},{5,4},{6,7},{7,6},{8,9},{9,8},{10,11... | collective-permute-start | bytes 1152008 | tf_op jit(solution)/shard_map/ppermute | solution.py:714
  344.4 29.5 %collective-permute-start.25 = (bf16[2,2,1,192,960]{4,3,2,1,0:T(8,128)(2,1)S(1)}, bf16[2,2,1,192,960]{4,3,2,1,0:T(8,128)(2,1)S(1)}, u32[]{:S(2)}, u32[]{:S(2)}) collective-permute-start(bf16[2,2,1,192,960]{4,3,2,1,0:T(8,128)(2,1)S(1)} %constant_dynamic-slice_fusion.10), channel_id=1, source_target_pairs={{0,1},{1,0},{2,3},{3,2},{4,5},{5,4},{6,7},{7,6},{8,9},{9,8},{10,11... | collective-permute-start | bytes 4423688 | tf_op jit(solution)/shard_map/ppermute | solution.py:714
  347.0 31.6 %collective-permute-start.34 = (bf16[1,1,1,120,2560]{4,3,2,1,0:T(8,128)(2,1)}, bf16[1,1,1,120,2560]{4,3,2,1,0:T(8,128)(2,1)}, u32[]{:S(2)}, u32[]{:S(2)}) collective-permute-start(bf16[1,1,1,120,2560]{4,3,2,1,0:T(8,128)(2,1)} %constant_dynamic-slice_fusion.8), channel_id=1, source_target_pairs={{0,4},{1,5},{2,6},{3,7},{4,0},{5,1},{6,2},{7,3},{8,12},{9,13},{10,... | collective-permute-start | bytes 1843208 | tf_op jit(solution)/shard_map/ppermute | solution.py:714
  376.3 29.4 %collective-permute-start.27 = (bf16[2,1,1,192,960]{4,3,2,1,0:T(8,128)(2,1)}, bf16[2,1,1,192,960]{4,3,2,1,0:T(8,128)(2,1)}, u32[]{:S(2)}, u32[]{:S(2)}) collective-permute-start(bf16[2,1,1,192,960]{4,3,2,1,0:T(8,128)(2,1)} %constant_dynamic-slice_fusion.3), channel_id=1, source_target_pairs={{0,2},{1,3},{2,0},{3,1},{4,6},{5,7},{6,4},{7,5},{8,10},{9,11},{10,... | collective-permute-start | bytes 2211848 | tf_op jit(solution)/shard_map/ppermute | solution.py:714
  378.0 29.0 %collective-permute-start.24 = (bf16[2,2,1,128,960]{3,4,2,1,0:T(8,128)(2,1)}, bf16[2,2,1,128,960]{3,4,2,1,0:T(8,128)(2,1)S(1)}, u32[]{:S(2)}, u32[]{:S(2)}) collective-permute-start(bf16[2,2,1,128,960]{3,4,2,1,0:T(8,128)(2,1)} %copy.175), channel_id=1, source_target_pairs={{0,1},{1,0},{2,3},{3,2},{4,5},{5,4},{6,7},{7,6},{8,9},{9,8},{10,11... | collective-permute-start | bytes 2949128 | tf_op jit(solution)/shard_map/ppermute | solution.py:714
  378.6 20.0 %collective-permute-start.33 = (bf16[1,1,1,120,962]{4,3,2,1,0:T(8,128)(2,1)S(1)}, bf16[1,1,1,120,962]{4,3,2,1,0:T(8,128)(2,1)S(1)}, u32[]{:S(2)}, u32[]{:S(2)}) collective-permute-start(bf16[1,1,1,120,962]{4,3,2,1,0:T(8,128)(2,1)S(1)} %constant_dynamic-slice_fusion.6), channel_id=1, source_target_pairs={{0,1},{1,0},{2,3},{3,2},{4,5},{5,4},{6,7},{7,6},{8,9},{9,8},{10,11... | collective-permute-start | bytes 692648 | tf_op jit(solution)/shard_map/ppermute | solution.py:714
  382.2 29.4 %collective-permute-start.35 = (bf16[1,1,1,120,2560]{4,3,2,1,0:T(8,128)(2,1)S(1)}, bf16[1,1,1,120,2560]{4,3,2,1,0:T(8,128)(2,1)S(1)}, u32[]{:S(2)}, u32[]{:S(2)}) collective-permute-start(bf16[1,1,1,120,2560]{4,3,2,1,0:T(8,128)(2,1)S(1)} %copy-done.30), channel_id=1, source_target_pairs={{0,4},{1,5},{2,6},{3,7},{4,0},{5,1},{6,2},{7,3},{8,12},{9,13},{10,... | collective-permute-start | bytes 1843208 | tf_op jit(solution)/shard_map/ppermute | solution.py:714
  407.4 10.6 %collective-permute-start.28 = (bf16[2,1,1,128,960]{3,4,2,1,0:T(8,128)(2,1)S(1)}, bf16[2,1,1,128,960]{3,4,2,1,0:T(8,128)(2,1)S(1)}, u32[]{:S(2)}, u32[]{:S(2)}) collective-permute-start(bf16[2,1,1,128,960]{3,4,2,1,0:T(8,128)(2,1)S(1)} %constant_dynamic-slice_fusion.1), channel_id=1, source_target_pairs={{0,2},{1,3},{2,0},{3,1},{4,6},{5,7},{6,4},{7,5},{8,10},{9,11},{10,... | collective-permute-start | bytes 1474568 | tf_op jit(solution)/shard_map/ppermute | solution.py:714
  409.9 18.2 %collective-permute-start.36 = (bf16[1,1,1,192,960]{4,3,2,1,0:T(8,128)(2,1)S(1)}, bf16[1,1,1,192,960]{4,3,2,1,0:T(8,128)(2,1)S(1)}, u32[]{:S(2)}, u32[]{:S(2)}) collective-permute-start(bf16[1,1,1,192,960]{4,3,2,1,0:T(8,128)(2,1)S(1)} %constant_dynamic-slice_fusion.2), channel_id=1, source_target_pairs={{0,4},{1,5},{2,6},{3,7},{4,0},{5,1},{6,2},{7,3},{8,12},{9,13},{10,... | collective-permute-start | bytes 1105928 | tf_op jit(solution)/shard_map/ppermute | solution.py:714
  418.6 9.6 %collective-permute-start.29 = (f32[320,240]{1,0:T(8,128)S(1)}, f32[320,240]{1,0:T(8,128)S(1)}, u32[]{:S(2)}, u32[]{:S(2)}) collective-permute-start(f32[320,240]{1,0:T(8,128)S(1)} %get-tuple-element.477), channel_id=1, source_target_pairs={{24,16},{0,8},{25,17},{1,9},{26,18},{2,10},{27,19},{3,11},{28,20},... | collective-permute-start | bytes 921608 | tf_op jit(solution)/shard_map/ppermute | solution.py:681
  428.1 8.6 %collective-permute-start.37 = (bf16[1,1,1,128,960]{3,4,2,1,0:T(8,128)(2,1)S(1)}, bf16[1,1,1,128,960]{3,4,2,1,0:T(8,128)(2,1)S(1)}, u32[]{:S(2)}, u32[]{:S(2)}) collective-permute-start(bf16[1,1,1,128,960]{3,4,2,1,0:T(8,128)(2,1)S(1)} %constant_dynamic-slice_fusion), channel_id=1, source_target_pairs={{0,4},{1,5},{2,6},{3,7},{4,0},{5,1},{6,2},{7,3},{8,12},{9,13},{10,... | collective-permute-start | bytes 737288 | tf_op jit(solution)/shard_map/ppermute | solution.py:714
  (39 other events, 387.5 us)

commit v5 on v4

--- a/solution.py
+++ b/solution.py
@@ -21,6 +21,12 @@
 epsilon = 1e-05
 rope_base = 10000.0
 masked_score = -1e30
+
+ORDER = (
+    *("H>", "G>", "P>", "H", "U>", "G", "D", "P", "H.", "G", "P.", "U", "d>", "e>", "G."),
+    *("H>", "U", "P>", "d", "d", "e", "U.", "H.", "P.", "S", "d.", "e", "e."),
+)
+DOWN_PART = 13
 
 def round_up(value, multiple):
     return -(-value // multiple) * multiple
@@ -156,12 +162,6 @@
     for rows, slots in found.items():
         mine = functools.reduce(jnp.logical_or, [tick.slot == slot for slot in slots])
         when(tick.active & mine, functools.partial(run, rows))
-
-
-def final_at(rows_s, array, slot, rows):
-    chunk = rows_s.shape[0]
-    at = pl.ds(pl.multiple_of(slot * chunk, chunk), rows)
-    return rows_s.at[pl.ds(0, rows)], array.at[at]
 
 
 def forward_kernel(sizes, lengths, *refs):
@@ -192,7 +192,7 @@
         slopes_b,
         inner_b,
     ) = buffers
-    store_sems, final_sem = refs
+    (store_sems,) = refs
     chunk, width = hidden_s.shape
     heads = width // HEAD_DIM
     all_width = w_heads.shape[1]
@@ -287,16 +287,20 @@
         heads_s[:, heads_s.shape[1] - LANES :] = jnp.zeros((chunk, LANES), F32)
         lax.fori_loop(0, 2, functools.partial(apply, rows), 0)
         out_round[:rows] = hidden_s[:rows].astype(BF16)
-        source, target = final_at(hidden_s, out_full, slot, rows)
-        final = pltpu.make_async_copy(source, target, final_sem.at[0])
-        when(tick.final, final.start)
+
+        @pl.when(tick.final)
+        def _():
+            row = lax.broadcasted_iota(jnp.int32, (rows, 1), 0)
+            valid = row < tick.bound(row, chunk // 2)
+            at = pl.ds(pl.multiple_of(slot * chunk, chunk), rows)
+            out_full[at] = jnp.where(valid, hidden_s[:rows], 0.0).astype(BF16)
+
         for app in (0, 1):
             for buffer in buffers[:-2]:
                 store(buffer, app, rows).wait()
             for part in range(ff // step):
                 store(inner_b, app, rows, part).wait()
                 store(slopes_b, app, rows, part).wait()
-        when(tick.final, final.wait)
 
     run_active(tick, sizes, run)
 
@@ -322,7 +326,7 @@
     hidden_k, heads_k, probs_k, middle_k, slopes_k = kept
     buffers = take(sizes["stores"])
     branch_b, gate_b, up_b, attn_b, heads_b, gains_b = buffers
-    read_sems, store_sems, final_sem = refs
+    read_sems, store_sems = refs
     chunk, width = grad_s.shape
     heads = width // HEAD_DIM
     all_width = w_heads.shape[0]
@@ -453,13 +457,15 @@
         mixed_s[:, mixed_s.shape[1] - LANES :] = jnp.zeros((chunk, LANES), F32)
         lax.fori_loop(0, 2, functools.partial(apply, rows), 0)
         out_round[:rows] = grad_s[:rows].astype(BF16)
-        source, target = final_at(grad_s, out_full, slot, rows)
-        final = pltpu.make_async_copy(source, target, final_sem.at[0])
-        when(tick.final, final.start)
+
+        @pl.when(tick.final)
+        def _():
+            at = pl.ds(pl.multiple_of(slot * chunk, chunk), rows)
+            out_full[at] = grad_s[:rows].astype(BF16)
+
         for buffer in buffers:
             store(buffer, 0, rows).wait()
             store(buffer, 1, rows).wait()
-        when(tick.final, final.wait)
 
     run_active(tick, sizes, run)
 
@@ -535,7 +541,7 @@
             pltpu.VMEM(query.shape, BF16),
             pltpu.SemaphoreType.DMA((len(sources),)),
         ],
-        compiler_params=pltpu.CompilerParams(vmem_limit_bytes=12 * 2**20),
+        compiler_params=pltpu.CompilerParams(vmem_limit_bytes=8 * 2**20),
         name="load_weights",
     )(*[pltpu.with_memory_space_constraint(array, pltpu.HBM) for array in sources])
 
@@ -548,7 +554,7 @@
         in_specs=[in_vmem() for _ in (*weights, *turned)],
         out_specs=[in_vmem() for _ in weights],
         input_output_aliases={count + i: i for i in range(len(turned))},
-        compiler_params=pltpu.CompilerParams(vmem_limit_bytes=12 * 2**20),
+        compiler_params=pltpu.CompilerParams(vmem_limit_bytes=8 * 2**20),
         name="turn_weights",
     )(*[pltpu.with_memory_space_constraint(weight, pltpu.VMEM) for weight in (*weights, *turned)])
 
@@ -582,15 +588,12 @@
     rows, width = sizes["rows"], sizes["width"]
     aliased = [] if state is None else list(state)
     inbound = [] if inbound is None else [inbound]
-    outs = [jax.ShapeDtypeStruct((rows, width), BF16)] + [
-        pltpu.HBM(shape.shape, shape.dtype)
-        for shape in (jax.ShapeDtypeStruct((sizes["total_rows"], width), F32), *shapes)
-    ]
+    outs = [jax.ShapeDtypeStruct((rows, width), BF16), pltpu.VMEM((sizes["total_rows"], width), BF16)]
+    outs += [pltpu.HBM(shape.shape, shape.dtype) for shape in shapes]
     scratch = scratch + buffers_for(reads, rows) + buffers_for(shapes, rows)
     if reads:
         scratch.append(pltpu.SemaphoreType.DMA((len(reads), 2)))
     scratch.append(pltpu.SemaphoreType.DMA((len(shapes), 2, 2)))
-    scratch.append(pltpu.SemaphoreType.DMA((1,)))
     blocks = [*tables, *edge_parts, *inbound]
     kept = len(tables) + (0 if sizes["backward"] else len(edge_parts))
     blocks[:kept] = [pltpu.with_memory_space_constraint(array, pltpu.VMEM) for array in blocks[:kept]]
@@ -613,13 +616,15 @@
             num_scalar_prefetch=1,
             grid=(1,),
             in_specs=[in_vmem() for _ in (*blocks, *weights)]
-            + [in_hbm() for _ in (*reads, *aliased)],
-            out_specs=[in_vmem()] + [in_hbm() for _ in outs[1:]],
+            + [in_hbm() for _ in reads]
+            + [in_vmem() for _ in aliased[:1]]
+            + [in_hbm() for _ in aliased[1:]],
+            out_specs=[in_vmem(), in_vmem()] + [in_hbm() for _ in shapes],
             scratch_shapes=scratch,
         ),
         input_output_aliases={first_alias + i: 1 + i for i in range(len(aliased))},
         compiler_params=pltpu.CompilerParams(
-            dimension_semantics=("arbitrary",), vmem_limit_bytes=18 * 2**20
+            dimension_semantics=("arbitrary",), vmem_limit_bytes=61 * 2**18
         ),
         cost_estimate=pl.CostEstimate(
             flops=flops, bytes_accessed=flops // (2 * rows), transcendentals=0
@@ -629,7 +634,9 @@
         lengths,
         *blocks,
         *[pltpu.with_memory_space_constraint(weight, pltpu.VMEM) for weight in weights],
-        *[pltpu.with_memory_space_constraint(array, pltpu.HBM) for array in (*reads, *aliased)],
+        *[pltpu.with_memory_space_constraint(array, pltpu.HBM) for array in reads],
+        *[pltpu.with_memory_space_constraint(array, pltpu.VMEM) for array in aliased[:1]],
+        *[pltpu.with_memory_space_constraint(array, pltpu.HBM) for array in aliased[1:]],
     )
 
 
@@ -669,19 +676,20 @@
     def block(value, at):
         return value[:, at * columns : (at + 1) * columns]
 
-    outputs = jnp.where(section == last, block(results, last), 0.0)
-    grads = jnp.where(section == 0, block(input_grads, 0), 0.0)
+    outputs, grads = block(results, last), block(input_grads, 0)
     for target in range(last):
         mirror = last - target
         if mirror == target:
-            outputs += lax.ppermute(block(results, target), "pipe", [(last, target)])
-            grads += lax.ppermute(block(input_grads, target), "pipe", [(0, target)])
+            got = lax.ppermute(block(results, target), "pipe", [(last, target)])
+            outputs = jnp.where(section == target, got, outputs)
+            got = lax.ppermute(block(input_grads, target), "pipe", [(0, target)])
+            grads = jnp.where(section == target, got, grads)
             continue
         sent = jnp.where(section == 0, block(input_grads, mirror), block(results, target))
         got = lax.ppermute(sent, "pipe", [(last, target), (0, mirror)])
         outputs = jnp.where(section == target, got, outputs)
         grads = jnp.where(section == mirror, got, grads)
-    return outputs, grads
+    return outputs.astype(F32), grads.astype(F32)
 
 
 def after(values, *tokens):
@@ -719,13 +727,6 @@
         got = after(self.got, *tokens) if tokens else self.got
         self.value = lax.dynamic_index_in_dim(self.value, mine, axis) + got
         return self.value
-
-    def finish(self, *tokens):
-        self.take(*tokens)
-        while self.bits:
-            self.send()
-            self.take()
-        return self.value.reshape(self.value.shape[-2:])
 
 
 def per_device(
@@ -878,61 +879,55 @@
         return by_rows(dot_rows(left, right).astype(BF16))
 
     bits = lax.axis_size("dp").bit_length() - 1
-    across_first, along_first = range(bits), range(1, bits)
-    attn = Piece(cube_view(product(normed_attn, heads_grad)), along_first)
-    token = attn.send()
-    gate = Piece(cube_view(product(*after((normed_mlp, gate_grad), token))), across_first)
-    token = gate.send()
+    across_first, along_first = range(bits), [*range(1, bits), 0]
     gain_sums = jnp.swapaxes(jnp.sum(gains, axis=(0, 1, 3)), 0, 1).astype(BF16)
-    proj_product = product(*after((mixed, attn_grad), token))
-    proj = Piece(cube_view(jnp.concatenate([proj_product, gain_sums], axis=1)), along_first)
-    token = proj.send()
-    attn.take(token)
-    token = attn.send()
-    up = Piece(cube_view(product(*after((normed_mlp, up_grad), token))), across_first)
-    token = up.send()
-    gate.take(token)
-    token = gate.send()
-    down_view = cube_view(product(*after((inner, branch), token)))
-    part = down_view.shape[-2] * 3 // 5
-    down = [Piece(view, across_first) for view in (down_view[..., :part, :], down_view[..., part:, :])]
-    proj.take(down_view)
-    token = proj.send()
-    while attn.bits:
-        attn.take(token)
-        token = attn.send()
-    token = attn.take(token)
-    gate.take(token)
-    token = gate.send()
-    while proj.bits:
-        proj.take(token)
-        token = proj.send()
-    token = proj.take(token)
-    up.take(token)
-    token = up.send()
-    token = down[0].send(token)
-    token = down[1].send(token)
-    token = grad_gate = gate.finish(token)
-    attn.bits, proj.bits = [0], [0]
-    token = attn.send(token)
-    up.take(token)
-    token = up.send()
-    token = proj.send(token)
-    down[0].take(token)
-    token = down[0].send()
-    down[0].take(token)
-    token = down[0].send()
-    down[1].take(token)
-    token = down[1].send()
-    token = grad_up = up.finish(token)
-    token = grad_heads = attn.finish(token)
-    token = grad_proj = proj.finish(token)
-    token = down_end = down[0].finish(token)
-    down[1].take(token)
-    token = down[1].send()
-    layer_output, grad_input = spread_ends(*after((results, input_grads), token))
-    grad_down = jnp.concatenate([down_end, down[1].finish(layer_output, grad_input)], axis=0)
-    grad_down = grad_down.astype(F32)
+
+    def make(name, token):
+        terms = dict(
+            G=(normed_mlp, gate_grad),
+            U=(normed_mlp, up_grad),
+            H=(normed_attn, heads_grad),
+            P=(mixed, attn_grad),
+            D=(inner, branch),
+        )[name]
+        value = product(*(terms if token is None else after(terms, token)))
+        if name == "P":
+            value = jnp.concatenate([value, gain_sums], axis=1)
+        view = cube_view(value)
+        if name != "D":
+            return {name: Piece(view, along_first if name in "HP" else across_first)}
+        part = view.shape[-2] * DOWN_PART // 20 // 16 * 16
+        return {
+            "d": Piece(view[..., :part, :], across_first),
+            "e": Piece(view[..., part:, :], across_first),
+        }
+
+    pieces, token, outputs = {}, None, None
+    for step in ORDER:
+        name, mark = step[0], step[1:]
+        if name == "S":
+            outputs = spread_ends(*after((results, input_grads), token))
+            continue
+        if name not in pieces:
+            pieces.update(make(name, token))
+            if name == "D":
+                token = pieces["e"].value
+                continue
+        piece = pieces[name]
+        if mark != ">":
+            token = piece.take(token)
+        if mark == ".":
+            spare = 0 if name in "HP" and 0 in piece.bits else len(piece.bits)
+            spare = len(piece.bits) - 1 if name in "HP" and 0 in piece.bits else spare
+            for _ in range(spare):
+                piece.send()
+                token = piece.take()
+        else:
+            token = piece.send(*(() if token is None else (token,)))
+    layer_output, grad_input = outputs
+    ends = {name: piece.value.reshape(piece.value.shape[-2:]) for name, piece in pieces.items()}
+    grad_down = jnp.concatenate([ends["d"], ends["e"]], axis=0).astype(F32)
+    grad_gate, grad_up, grad_heads, grad_proj = [ends[name] for name in "GUHP"]
     grad_gate, grad_up, grad_heads, grad_proj = [
         grad.astype(F32) for grad in (grad_gate, grad_up, grad_heads, grad_proj)
     ]
@@ -942,15 +937,6 @@
     grad_gain_attn, grad_gain_mlp = grad_proj[:, width], grad_proj[:, width + 1]
     grad_proj = grad_proj[:, :width]
 
-    position = jnp.arange(total_rows)
-    long_rows = position < rows
-    offsets = jnp.where(long_rows, position, position % segment)
-    micro = jnp.where(long_rows, 0, position // segment - 1)
-    bound = jnp.zeros_like(position)
-    for m in range(MICRO):
-        bound = jnp.where(micro == m, group[m], bound)
-    valid = (offsets < bound)[:, None]
-    layer_output = jnp.where(valid, layer_output, 0.0)
     return (
         layer_output,
         grad_input,

time: 447 us -> 432 us (0.966)
  waiting for transfers between devices: 169 us -> 161 us
  Pallas kernels: 152 us -> 145 us
  local copies, waits for them, and re-layouts: 24.6 us -> 19 us
  starting transfers between devices: 49.2 us -> 54.7 us
    ppermute x18, waiting for transfers between devices: 134 us -> 127 us  [send(): lax.ppermute(sent, 'dp', [(i, i ^ 1 << bit) for i in range(devices)])]
    pallas_call x18, Pallas kernels: 141 us -> 135 us  [run_tick(): pl.pallas_call(functools.partial(kernel, sizes), out_shape=outs, grid_spe...]
    add x12 -> x13, other arithmetic: 7.15 us -> 11 us  [take(): self.value = lax.dynamic_index_in_dim(self.value, mine, axis) + got]
  transfers between devices with their start and end apart: 38 -> 38, of which waited for: 16 -> 15; matrix products, arithmetic and copies ran while one was open for 12% -> 11% of each run, Pallas kernels for 27% -> 27%
where the time goes in v5:
time: 432 us; the launch traced here: 424 us
  waiting for transfers between devices  161 us (37%)
  Pallas kernels  145 us (34%)
  starting transfers between devices  54.7 us (13%)
  matrix products  21.3 us (5%)
  other arithmetic  20.7 us (5%)
  local copies, waits for them, and re-layouts  19 us (4%)
    pallas_call x18, Pallas kernels, run_tick(): pl.pallas_call(functools.partial(kernel, sizes), out_shape=outs, grid_spe...  135 us
    ppermute x18, waiting for transfers between devices, send(): lax.ppermute(sent, 'dp', [(i, i ^ 1 << bit) for i in range(devices)])  127 us
    ppermute x14, waiting for transfers between devices, per_device(): sent[tick] = lax.ppermute(rounded, 'pipe', route)  34.6 us
    ppermute x18, starting transfers between devices, send(): lax.ppermute(sent, 'dp', [(i, i ^ 1 << bit) for i in range(devices)])  28.5 us
    dot_general x5, matrix products, dot_rows(): lax.dot_general(left, right, (((0,), (0,)), ((), ())), preferred_element_...  21.3 us
    ppermute x14, starting transfers between devices, per_device(): sent[tick] = lax.ppermute(rounded, 'pipe', route)  13.2 us
    add x13, other arithmetic, take(): self.value = lax.dynamic_index_in_dim(self.value, mine, axis) + got  11 us
    dynamic_slice x18, local copies, waits for them, and re-layouts, send(): sent = lax.dynamic_index_in_dim(self.value, 1 - mine, axis)  10.1 us
  transfers between devices with their start and end apart: 38, of which 15 were waited for; matrix products, arithmetic and copies ran while one was open for 11% of the time, Pallas kernels for 27%

profile of v5, /device:TPU:0, one launch (start us, length us, event | category | flops | bytes accessed | tf_op | source)
XLA Modules:
  0.0 424.2 jit_solution(5234554647253424830)
XLA Ops:
  4.3 4.3 %collective-permute-start.2 = (bf16[320,240]{1,0:T(8,128)(2,1)S(1)}, bf16[320,240]{1,0:T(8,128)(2,1)S(1)}, u32[]{:S(2)}, u32[]{:S(2)}) collective-permute-start(bf16[320,240]{1,0:T(8,128)(2,1)S(1)} %get-tuple-element.516), channel_id=1, source_target_pairs={{24,0},{0,24},{25,1},{1,25},{26,2},{2,26},{27,3},{3,27},{28,4},{4,... | collective-permute-start | bytes 460808 | tf_op jit(solution)/shard_map/ppermute | solution.py:666
  8.6 7.0 %load_weights.1 = (bf16[1600,960]{1,0:T(8,128)(2,1)S(1)}, bf16[960,1600]{1,0:T(8,128)(2,1)S(1)}, bf16[960,960]{1,0:T(8,128)(2,1)S(1)}, bf16[960,2560]{1,0:T(8,12...) custom-call(bf16[320,960]{1,0:T(8,128)(2,1)} %bitcast.83, ...), custom_call_target="tpu_custom_call" | custom-call | tf_op jit(solution)/shard_map/load_weights/pallas_call | solution.py:535
  16.3 11.3 %layer_pair_forward.9 = (bf16[128,960]{1,0:T(8,128)(2,1)S(1)}, bf16[320,960]{1,0:T(8,128)(2,1)S(1)}, f32[2,320,960]{2,1,0:T(8,128)}, bf16[2,320,960]{2,1,0:T(8,1...) custom-call(s32[1,4]{1,0:T(1,128)S(1)} %copy-done.3, ...), custom_call_target="tpu_custom_call" | custom-call | flops 5033164800 | bytes 19660800 | tf_op jit(solution)/shard_map/layer_pair_forward/pallas_call | solution.py:612
  28.9 11.6 %layer_pair_forward.10 = (bf16[128,960]{1,0:T(8,128)(2,1)S(1)}, bf16[320,960]{1,0:T(8,128)(2,1)S(1)}, f32[2,320,960]{2,1,0:T(8,128)}, bf16[2,320,960]{2,1,0:T(8,...) custom-call(s32[1,4]{1,0:T(1,128)S(1)} %copy-done.3, ...), custom_call_target="tpu_custom_call", output_to_operand_aliasing={{1}: (14, {}), {2}: (15, {}), {3}: (16, {}), {4}: (17, {}),... | custom-call | flops 5033164800 | bytes 19660800 | tf_op jit(solution)/shard_map/layer_pair_forward/pallas_call | solution.py:612
  41.9 10.9 %layer_pair_forward.11 = (bf16[128,960]{1,0:T(8,128)(2,1)S(1)}, bf16[320,960]{1,0:T(8,128)(2,1)S(1)}, f32[2,320,960]{2,1,0:T(8,128)}, bf16[2,320,960]{2,1,0:T(8,...) custom-call(s32[1,4]{1,0:T(1,128)S(1)} %copy-done.3, ...), custom_call_target="tpu_custom_call", output_to_operand_aliasing={{1}: (15, {}), {2}: (16, {}), {3}: (17, {}), {4}: (18, {}),... | custom-call | flops 5033164800 | bytes 19660800 | tf_op jit(solution)/shard_map/layer_pair_forward/pallas_call | solution.py:612
  54.1 9.1 %layer_pair_forward.12 = (bf16[128,960]{1,0:T(8,128)(2,1)S(1)}, bf16[320,960]{1,0:T(8,128)(2,1)S(1)}, f32[2,320,960]{2,1,0:T(8,128)}, bf16[2,320,960]{2,1,0:T(8,...) custom-call(s32[1,4]{1,0:T(1,128)S(1)} %copy-done.3, ...), custom_call_target="tpu_custom_call", output_to_operand_aliasing={{1}: (11, {}), {2}: (12, {}), {3}: (13, {}), {4}: (14, {}),... | custom-call | flops 5033164800 | bytes 19660800 | tf_op jit(solution)/shard_map/layer_pair_forward/pallas_call | solution.py:612
  63.9 3.4 turn_weights.3
  68.9 7.4 %layer_pair_forward.14 = (bf16[128,960]{1,0:T(8,128)(2,1)S(1)}, bf16[320,960]{1,0:T(8,128)(2,1)S(1)}, f32[2,320,960]{2,1,0:T(8,128)}, bf16[2,320,960]{2,1,0:T(8,...) custom-call(s32[1,4]{1,0:T(1,128)S(1)} %copy-done.3, ...), custom_call_target="tpu_custom_call", output_to_operand_aliasing={{1}: (11, {}), {2}: (12, {}), {3}: (13, {}), {4}: (14, {}),... | custom-call | flops 5033164800 | bytes 19660800 | tf_op jit(solution)/shard_map/layer_pair_forward/pallas_call | solution.py:612
  78.6 8.6 %layer_pair_forward.16 = (bf16[128,960]{1,0:T(8,128)(2,1)}, bf16[320,960]{1,0:T(8,128)(2,1)S(1)}, f32[2,320,960]{2,1,0:T(8,128)}, bf16[2,320,960]{2,1,0:T(8,128)...) custom-call(s32[1,4]{1,0:T(1,128)S(1)} %copy-done.3, ...), custom_call_target="tpu_custom_call", output_to_operand_aliasing={{1}: (11, {}), {2}: (12, {}), {3}: (13, {}), {4}: (14, {}),... | custom-call | flops 5033164800 | bytes 19660800 | tf_op jit(solution)/shard_map/layer_pair_forward/pallas_call | solution.py:612
  90.5 8.3 %layer_pair_backward.10 = (bf16[128,960]{1,0:T(8,128)(2,1)S(1)}, bf16[320,960]{1,0:T(8,128)(2,1)S(1)}, bf16[2,320,960]{2,1,0:T(8,128)(2,1)}, bf16[2,320,2560]{2,...) custom-call(s32[1,4]{1,0:T(1,128)S(1)} %copy-done.3, ...), custom_call_target="tpu_custom_call", output_to_operand_aliasing={{1}: (19, {}), {2}: (20, {}), {3}: (21, {}), {4}: (22, {}),... | custom-call | flops 5033164800 | bytes 19660800 | tf_op jit(solution)/shard_map/layer_pair_backward/pallas_call | solution.py:612
  101.1 8.5 %layer_pair_backward.12 = (bf16[128,960]{1,0:T(8,128)(2,1)S(1)}, bf16[320,960]{1,0:T(8,128)(2,1)S(1)}, bf16[2,320,960]{2,1,0:T(8,128)(2,1)}, bf16[2,320,2560]{2,...) custom-call(s32[1,4]{1,0:T(1,128)S(1)} %copy-done.3, ...), custom_call_target="tpu_custom_call", output_to_operand_aliasing={{1}: (16, {}), {2}: (17, {}), {3}: (18, {}), {4}: (19, {}),... | custom-call | flops 5033164800 | bytes 19660800 | tf_op jit(solution)/shard_map/layer_pair_backward/pallas_call | solution.py:612
  112.5 8.0 %layer_pair_backward.14 = (bf16[128,960]{1,0:T(8,128)(2,1)S(1)}, bf16[320,960]{1,0:T(8,128)(2,1)S(1)}, bf16[2,320,960]{2,1,0:T(8,128)(2,1)}, bf16[2,320,2560]{2,...) custom-call(s32[1,4]{1,0:T(1,128)S(1)} %copy-done.3, ...), custom_call_target="tpu_custom_call", output_to_operand_aliasing={{1}: (16, {}), {2}: (17, {}), {3}: (18, {}), {4}: (19, {}),... | custom-call | flops 5033164800 | bytes 19660800 | tf_op jit(solution)/shard_map/layer_pair_backward/pallas_call | solution.py:612
  121.8 33.7 %collective-permute-done.13.refs_4_ = bf16[128,960]{1,0:T(8,128)(2,1)S(1)} collective-permute-done((bf16[128,960]{1,0:T(8,128)(2,1)S(1)}, bf16[128,960]{1,0:T(8,128)(2,1)S(1)}, u32[]{:S(2)}, u32[]{:S(2)}) %collective-permute-start.13) | collective-permute-done | bytes 245792 | tf_op jit(solution)/shard_map/ppermute | solution.py:872
  155.5 14.4 %layer_pair_backward.15 = (bf16[128,960]{1,0:T(8,128)(2,1)S(1)}, bf16[320,960]{1,0:T(8,128)(2,1)S(1)}, bf16[2,320,960]{2,1,0:T(8,128)(2,1)}, bf16[2,320,2560]{2,...) custom-call(s32[1,4]{1,0:T(1,128)S(1)} %copy-done.3, ...), custom_call_target="tpu_custom_call", output_to_operand_aliasing={{1}: (16, {}), {2}: (17, {}), {3}: (18, {}), {4}: (19, {}),... | custom-call | flops 5033164800 | bytes 19660800 | tf_op jit(solution)/shard_map/layer_pair_backward/pallas_call | solution.py:612
  171.5 15.3 %layer_pair_backward.16 = (bf16[128,960]{1,0:T(8,128)(2,1)}, bf16[320,960]{1,0:T(8,128)(2,1)S(1)}, bf16[2,320,960]{2,1,0:T(8,128)(2,1)}, bf16[2,320,2560]{2,1,0:...) custom-call(s32[1,4]{1,0:T(1,128)S(1)} %copy-done.3, ...), custom_call_target="tpu_custom_call", output_to_operand_aliasing={{1}: (16, {}), {2}: (17, {}), {3}: (18, {}), {4}: (19, {}),... | custom-call | flops 5033164800 | bytes 19660800 | tf_op jit(solution)/shard_map/layer_pair_backward/pallas_call | solution.py:612
  187.4 15.3 %layer_pair_backward.17 = (bf16[128,960]{1,0:T(8,128)(2,1)}, bf16[320,960]{1,0:T(8,128)(2,1)S(1)}, bf16[2,320,960]{2,1,0:T(8,128)(2,1)}, bf16[2,320,2560]{2,1,0:...) custom-call(s32[1,4]{1,0:T(1,128)S(1)} %copy-done.3, ...), custom_call_target="tpu_custom_call", output_to_operand_aliasing={{1}: (16, {}), {2}: (17, {}), {3}: (18, {}), {4}: (19, {}),... | custom-call | flops 5033164800 | bytes 19660800 | tf_op jit(solution)/shard_map/layer_pair_backward/pallas_call | solution.py:612
  202.7 4.6 %bitcast_convert_fusion.3 = bf16[960,1600]{1,0:T(8,128)(2,1)S(1)} fusion(bf16[2,320,960]{2,1,0:T(8,128)(2,1)S(1)} %copy-done.7, bf16[2,320,1600]{2,1,0:T(8,128)(2,1)} %get-tuple-element.427), kind=kOutput, calls=%fused_computation.3 | convolution fusion | flops 1967616000 | bytes 6348800 | tf_op jit(solution)/shard_map/dot_general | solution.py:44
  210.3 4.5 %bitcast_convert_fusion.2 = bf16[960,2560]{1,0:T(8,128)(2,1)S(1)} fusion(bf16[2,320,960]{2,1,0:T(8,128)(2,1)S(1)} %copy-done.9, bf16[2,320,2560]{2,1,0:T(8,128)(2,1)S(1)} %copy-done.5), kind=kOutput, calls=%fused_computation.2 | convolution fusion | flops 3148185600 | bytes 9420800 | tf_op jit(solution)/shard_map/dot_general | solution.py:44
  219.6 3.1 bitcast_convert_fusion.4
  226.0 29.5 %collective-permute-done.19 = bf16[2,1,2,120,1600]{4,3,2,1,0:T(8,128)(2,1)} collective-permute-done((bf16[2,1,2,120,1600]{4,3,2,1,0:T(8,128)(2,1)}, bf16[2,1,2,120,1600]{4,3,2,1,0:T(8,128)(2,1)}, u32[]{:S(2)}, u32[]{:S(2)}) %collective-permute-start.19) | collective-permute-done | bytes 1536032 | tf_op jit(solution)/shard_map/ppermute | solution.py:722
  258.9 4.3 %bitcast_convert_fusion.1 = bf16[960,2560]{1,0:T(8,128)(2,1)S(1)} fusion(bf16[2,320,960]{2,1,0:T(8,128)(2,1)S(1)} %copy-done.9, bf16[2,320,2560]{2,1,0:T(8,128)(2,1)S(1)} %copy-done.6), kind=kOutput, calls=%fused_computation.1 | convolution fusion | flops 3148185600 | bytes 9420800 | tf_op jit(solution)/shard_map/dot_general | solution.py:44
  265.0 9.8 %collective-permute-done.18 = bf16[2,2,1,120,2560]{4,3,2,1,0:T(8,128)(2,1)} collective-permute-done((bf16[2,2,1,120,2560]{4,3,2,1,0:T(8,128)(2,1)}, bf16[2,2,1,120,2560]{4,3,2,1,0:T(8,128)(2,1)}, u32[]{:S(2)}, u32[]{:S(2)}) %collective-permute-start.18) | collective-permute-done | bytes 2457632 | tf_op jit(solution)/shard_map/ppermute | solution.py:722
  278.4 4.8 %bitcast_convert_fusion = bf16[2560,960]{1,0:T(8,128)(2,1)S(1)} fusion(bf16[2,320,2560]{2,1,0:T(8,128)(2,1)S(1)} %copy-done.4, bf16[2,320,960]{2,1,0:T(8,128)(2,1)S(1)} %copy-done.10), kind=kOutput, calls=%fused_computation | convolution fusion | flops 3148185600 | bytes 9420800 | tf_op jit(solution)/shard_map/dot_general | solution.py:44
  285.9 3.7 collective-permute-start.20
  289.8 24.2 %collective-permute-done.21 = bf16[2,1,1,120,2560]{4,3,2,1,0:T(8,128)(2,1)S(1)} collective-permute-done((bf16[2,1,1,120,2560]{4,3,2,1,0:T(8,128)(2,1)S(1)}, bf16[2,1,1,120,2560]{4,3,2,1,0:T(8,128)(2,1)S(1)}, u32[]{:S(2)}, u32[]{:S(2)}) %collective-permute-start.21) | collective-permute-done | bytes 1228832 | tf_op jit(solution)/shard_map/ppermute | solution.py:722
  316.1 4.8 %collective-permute-done.23 = bf16[2,2,1,120,2560]{4,3,2,1,0:T(8,128)(2,1)S(1)} collective-permute-done((bf16[2,2,1,120,2560]{4,3,2,1,0:T(8,128)(2,1)S(1)}, bf16[2,2,1,120,2560]{4,3,2,1,0:T(8,128)(2,1)S(1)}, u32[]{:S(2)}, u32[]{:S(2)}) %collective-permute-start.23) | collective-permute-done | bytes 2457632 | tf_op jit(solution)/shard_map/ppermute | solution.py:722
  326.6 15.4 %collective-permute-done.25 = bf16[1,1,1,120,2560]{4,3,2,1,0:T(8,128)(2,1)S(1)} collective-permute-done((bf16[1,1,1,120,2560]{4,3,2,1,0:T(8,128)(2,1)S(1)}, bf16[1,1,1,120,2560]{4,3,2,1,0:T(8,128)(2,1)S(1)}, u32[]{:S(2)}, u32[]{:S(2)}) %collective-permute-start.25) | collective-permute-done | bytes 614432 | tf_op jit(solution)/shard_map/ppermute | solution.py:722
  343.1 10.0 %collective-permute-done.24 = bf16[2,1,1,120,2560]{4,3,2,1,0:T(8,128)(2,1)S(1)} collective-permute-done((bf16[2,1,1,120,2560]{4,3,2,1,0:T(8,128)(2,1)S(1)}, bf16[2,1,1,120,2560]{4,3,2,1,0:T(8,128)(2,1)S(1)}, u32[]{:S(2)}, u32[]{:S(2)}) %collective-permute-start.24) | collective-permute-done | bytes 1228832 | tf_op jit(solution)/shard_map/ppermute | solution.py:722
  363.7 2.5 collective-permute-start.28
  366.3 22.2 %collective-permute-done.31 = bf16[2,1,1,208,960]{4,3,2,1,0:T(8,128)(2,1)} collective-permute-done((bf16[2,1,1,208,960]{4,3,2,1,0:T(8,128)(2,1)}, bf16[2,1,1,208,960]{4,3,2,1,0:T(8,128)(2,1)}, u32[]{:S(2)}, u32[]{:S(2)}) %collective-permute-start.31) | collective-permute-done | bytes 798752 | tf_op jit(solution)/shard_map/ppermute | solution.py:722
  394.1 2.5 collective-permute-start.36
  414.5 8.3 %collective-permute-done.37 = bf16[1,1,1,112,960]{4,3,2,1,0:T(8,128)(2,1)S(1)} collective-permute-done((bf16[1,1,1,112,960]{4,3,2,1,0:T(8,128)(2,1)S(1)}, bf16[1,1,1,112,960]{4,3,2,1,0:T(8,128)(2,1)S(1)}, u32[]{:S(2)}, u32[]{:S(2)}) %collective-permute-start.37) | collective-permute-done | bytes 215072 | tf_op jit(solution)/shard_map/ppermute | solution.py:722
  (179 shorter events, 91.3 us)
Async XLA Ops:
  1.7 14.0 %collective-permute-start = (bf16[320,240]{1,0:T(8,128)(2,1)S(1)}, bf16[320,240]{1,0:T(8,128)(2,1)S(1)}, u32[]{:S(2)}, u32[]{:S(2)}) collective-permute-start(bf16[320,240]{1,0:T(8,128)(2,1)S(1)} %get-tuple-element.518), channel_id=1, source_target_pairs={{8,0},{16,24},{9,1},{17,25},{10,2},{18,26},{11,3},{19,27},{12,4},{... | collective-permute-start | bytes 460808 | tf_op jit(solution)/shard_map/ppermute | solution.py:666
  3.0 12.7 %collective-permute-start.1 = (bf16[320,240]{1,0:T(8,128)(2,1)S(1)}, bf16[320,240]{1,0:T(8,128)(2,1)S(1)}, u32[]{:S(2)}, u32[]{:S(2)}) collective-permute-start(bf16[320,240]{1,0:T(8,128)(2,1)S(1)} %get-tuple-element.517), channel_id=1, source_target_pairs={{16,0},{8,24},{17,1},{9,25},{18,2},{10,26},{19,3},{11,27},{20,4},{... | collective-permute-start | bytes 460808 | tf_op jit(solution)/shard_map/ppermute | solution.py:666
  4.3 11.4 %collective-permute-start.2 = (bf16[320,240]{1,0:T(8,128)(2,1)S(1)}, bf16[320,240]{1,0:T(8,128)(2,1)S(1)}, u32[]{:S(2)}, u32[]{:S(2)}) collective-permute-start(bf16[320,240]{1,0:T(8,128)(2,1)S(1)} %get-tuple-element.516), channel_id=1, source_target_pairs={{24,0},{0,24},{25,1},{1,25},{26,2},{2,26},{27,3},{3,27},{28,4},{4,... | collective-permute-start | bytes 460808 | tf_op jit(solution)/shard_map/ppermute | solution.py:666
  27.6 14.3 %collective-permute-start.3 = (bf16[128,960]{1,0:T(8,128)(2,1)S(1)}, bf16[128,960]{1,0:T(8,128)(2,1)S(1)}, u32[]{:S(2)}, u32[]{:S(2)}) collective-permute-start(bf16[128,960]{1,0:T(8,128)(2,1)S(1)} %get-tuple-element.254), channel_id=1, source_target_pairs={{0,8},{1,9},{2,10},{3,11},{4,12},{5,13},{6,14},{7,15}} | collective-permute-start | bytes 737288 | tf_op jit(solution)/shard_map/ppermute | solution.py:827
  40.6 13.5 %collective-permute-start.5 = (bf16[128,960]{1,0:T(8,128)(2,1)S(1)}, bf16[128,960]{1,0:T(8,128)(2,1)S(1)}, u32[]{:S(2)}, u32[]{:S(2)}) collective-permute-start(bf16[128,960]{1,0:T(8,128)(2,1)S(1)} %get-tuple-element.276), channel_id=1, source_target_pairs={{0,8},{1,9},{2,10},{3,11},{4,12},{5,13},{6,14},{7,15}} | collective-permute-start | bytes 737288 | tf_op jit(solution)/shard_map/ppermute | solution.py:827
  52.8 14.5 %collective-permute-start.4 = (bf16[128,960]{1,0:T(8,128)(2,1)S(1)}, bf16[128,960]{1,0:T(8,128)(2,1)S(1)}, u32[]{:S(2)}, u32[]{:S(2)}) collective-permute-start(bf16[128,960]{1,0:T(8,128)(2,1)S(1)} %get-tuple-element.275), channel_id=1, source_target_pairs={{0,8},{8,16},{1,9},{9,17},{2,10},{10,18},{3,11},{11,19},{4,12},{12... | collective-permute-start | bytes 737288 | tf_op jit(solution)/shard_map/ppermute | solution.py:827
  89.8 9.7 %collective-permute-start.10 = (bf16[128,960]{1,0:T(8,128)(2,1)S(1)}, bf16[128,960]{1,0:T(8,128)(2,1)S(1)}, u32[]{:S(2)}, u32[]{:S(2)}) collective-permute-start(bf16[128,960]{1,0:T(8,128)(2,1)S(1)} %get-tuple-element.358), channel_id=1, source_target_pairs={{24,16},{25,17},{26,18},{27,19},{28,20},{29,21},{30,22},{31,23}} | collective-permute-start | bytes 737288 | tf_op jit(solution)/shard_map/ppermute | solution.py:872
  100.4 9.9 %collective-permute-start.11 = (bf16[128,960]{1,0:T(8,128)(2,1)S(1)}, bf16[128,960]{1,0:T(8,128)(2,1)S(1)}, u32[]{:S(2)}, u32[]{:S(2)}) collective-permute-start(bf16[128,960]{1,0:T(8,128)(2,1)S(1)} %get-tuple-element.373), channel_id=1, source_target_pairs={{16,8},{24,16},{17,9},{25,17},{18,10},{26,18},{19,11},{27,19},{20,... | collective-permute-start | bytes 737288 | tf_op jit(solution)/shard_map/ppermute | solution.py:872
  111.2 44.3 %collective-permute-start.13 = (bf16[128,960]{1,0:T(8,128)(2,1)S(1)}, bf16[128,960]{1,0:T(8,128)(2,1)S(1)}, u32[]{:S(2)}, u32[]{:S(2)}) collective-permute-start(bf16[128,960]{1,0:T(8,128)(2,1)S(1)} %get-tuple-element.389), channel_id=1, source_target_pairs={{8,0},{16,8},{9,1},{17,9},{10,2},{18,10},{11,3},{19,11},{12,4},{20... | collective-permute-start | bytes 737288 | tf_op jit(solution)/shard_map/ppermute | solution.py:872
  120.5 51.0 %collective-permute-start.16 = (bf16[128,960]{1,0:T(8,128)(2,1)S(1)}, bf16[128,960]{1,0:T(8,128)(2,1)S(1)}, u32[]{:S(2)}, u32[]{:S(2)}) collective-permute-start(bf16[128,960]{1,0:T(8,128)(2,1)S(1)} %get-tuple-element.406), channel_id=1, source_target_pairs={{8,0},{9,1},{10,2},{11,3},{12,4},{13,5},{14,6},{15,7}} | collective-permute-start | bytes 737288 | tf_op jit(solution)/shard_map/ppermute | solution.py:872
  169.9 17.5 %collective-permute-start.15 = (bf16[128,960]{1,0:T(8,128)(2,1)S(1)}, bf16[128,960]{1,0:T(8,128)(2,1)S(1)}, u32[]{:S(2)}, u32[]{:S(2)}) collective-permute-start(bf16[128,960]{1,0:T(8,128)(2,1)S(1)} %get-tuple-element.405), channel_id=1, source_target_pairs={{8,0},{9,1},{10,2},{11,3},{12,4},{13,5},{14,6},{15,7}} | collective-permute-start | bytes 737288 | tf_op jit(solution)/shard_map/ppermute | solution.py:872
  208.7 46.7 %collective-permute-start.19 = (bf16[2,1,2,120,1600]{4,3,2,1,0:T(8,128)(2,1)}, bf16[2,1,2,120,1600]{4,3,2,1,0:T(8,128)(2,1)}, u32[]{:S(2)}, u32[]{:S(2)}) collective-permute-start(bf16[2,1,2,120,1600]{4,3,2,1,0:T(8,128)(2,1)} %constant_dynamic-slice_fusion.17), channel_id=1, source_target_pairs={{0,2},{1,3},{2,0},{3,1},{4,6},{5,7},{6,4},{7,5},{8,10},{9,11},{10,... | collective-permute-start | bytes 4608008 | tf_op jit(solution)/shard_map/ppermute | solution.py:722
  218.1 56.6 %collective-permute-start.18 = (bf16[2,2,1,120,2560]{4,3,2,1,0:T(8,128)(2,1)}, bf16[2,2,1,120,2560]{4,3,2,1,0:T(8,128)(2,1)}, u32[]{:S(2)}, u32[]{:S(2)}) collective-permute-start(bf16[2,2,1,120,2560]{4,3,2,1,0:T(8,128)(2,1)} %constant_dynamic-slice_fusion.16), channel_id=1, source_target_pairs={{0,1},{1,0},{2,3},{3,2},{4,5},{5,4},{6,7},{7,6},{8,9},{9,8},{10,11... | collective-permute-start | bytes 7372808 | tf_op jit(solution)/shard_map/ppermute | solution.py:722
  225.0 60.8 %collective-permute-start.17 = (bf16[2,1,2,120,962]{4,3,2,1,0:T(8,128)(2,1)S(1)}, bf16[2,1,2,120,962]{4,3,2,1,0:T(8,128)(2,1)S(1)}, u32[]{:S(2)}, u32[]{:S(2)}) collective-permute-start(bf16[2,1,2,120,962]{4,3,2,1,0:T(8,128)(2,1)S(1)} %constant_dynamic-slice_fusion.15), channel_id=1, source_target_pairs={{0,2},{1,3},{2,0},{3,1},{4,6},{5,7},{6,4},{7,5},{8,10},{9,11},{10,... | collective-permute-start | bytes 2770568 | tf_op jit(solution)/shard_map/ppermute | solution.py:722
  257.2 32.4 %collective-permute-start.22 = (bf16[1,1,2,120,1600]{4,3,2,1,0:T(8,128)(2,1)S(1)}, bf16[1,1,2,120,1600]{4,3,2,1,0:T(8,128)(2,1)S(1)}, u32[]{:S(2)}, u32[]{:S(2)}) collective-permute-start(bf16[1,1,2,120,1600]{4,3,2,1,0:T(8,128)(2,1)S(1)} %constant_dynamic-slice_fusion.14), channel_id=1, source_target_pairs={{0,4},{1,5},{2,6},{3,7},{4,0},{5,1},{6,2},{7,3},{8,12},{9,13},{10,... | collective-permute-start | bytes 2304008 | tf_op jit(solution)/shard_map/ppermute | solution.py:722
  263.4 57.4 %collective-permute-start.23 = (bf16[2,2,1,120,2560]{4,3,2,1,0:T(8,128)(2,1)S(1)}, bf16[2,2,1,120,2560]{4,3,2,1,0:T(8,128)(2,1)S(1)}, u32[]{:S(2)}, u32[]{:S(2)}) collective-permute-start(bf16[2,2,1,120,2560]{4,3,2,1,0:T(8,128)(2,1)S(1)} %constant_dynamic-slice_fusion.13), channel_id=1, source_target_pairs={{0,1},{1,0},{2,3},{3,2},{4,5},{5,4},{6,7},{7,6},{8,9},{9,8},{10,11... | collective-permute-start | bytes 7372808 | tf_op jit(solution)/shard_map/ppermute | solution.py:722
  277.0 36.9 %collective-permute-start.21 = (bf16[2,1,1,120,2560]{4,3,2,1,0:T(8,128)(2,1)S(1)}, bf16[2,1,1,120,2560]{4,3,2,1,0:T(8,128)(2,1)S(1)}, u32[]{:S(2)}, u32[]{:S(2)}) collective-permute-start(bf16[2,1,1,120,2560]{4,3,2,1,0:T(8,128)(2,1)S(1)} %constant_dynamic-slice_fusion.12), channel_id=1, source_target_pairs={{0,2},{1,3},{2,0},{3,1},{4,6},{5,7},{6,4},{7,5},{8,10},{9,11},{10,... | collective-permute-start | bytes 3686408 | tf_op jit(solution)/shard_map/ppermute | solution.py:722
  285.9 30.1 %collective-permute-start.20 = (bf16[1,1,2,120,962]{4,3,2,1,0:T(8,128)(2,1)S(1)}, bf16[1,1,2,120,962]{4,3,2,1,0:T(8,128)(2,1)S(1)}, u32[]{:S(2)}, u32[]{:S(2)}) collective-permute-start(bf16[1,1,2,120,962]{4,3,2,1,0:T(8,128)(2,1)S(1)} %constant_dynamic-slice_fusion.11), channel_id=1, source_target_pairs={{0,4},{1,5},{2,6},{3,7},{4,0},{5,1},{6,2},{7,3},{8,12},{9,13},{10,... | collective-permute-start | bytes 1385288 | tf_op jit(solution)/shard_map/ppermute | solution.py:722
  314.2 27.8 %collective-permute-start.25 = (bf16[1,1,1,120,2560]{4,3,2,1,0:T(8,128)(2,1)S(1)}, bf16[1,1,1,120,2560]{4,3,2,1,0:T(8,128)(2,1)S(1)}, u32[]{:S(2)}, u32[]{:S(2)}) collective-permute-start(bf16[1,1,1,120,2560]{4,3,2,1,0:T(8,128)(2,1)S(1)} %constant_dynamic-slice_fusion.10), channel_id=1, source_target_pairs={{0,4},{1,5},{2,6},{3,7},{4,0},{5,1},{6,2},{7,3},{8,12},{9,13},{10,... | collective-permute-start | bytes 1843208 | tf_op jit(solution)/shard_map/ppermute | solution.py:722
  321.2 31.9 %collective-permute-start.24 = (bf16[2,1,1,120,2560]{4,3,2,1,0:T(8,128)(2,1)S(1)}, bf16[2,1,1,120,2560]{4,3,2,1,0:T(8,128)(2,1)S(1)}, u32[]{:S(2)}, u32[]{:S(2)}) collective-permute-start(bf16[2,1,1,120,2560]{4,3,2,1,0:T(8,128)(2,1)S(1)} %constant_dynamic-slice_fusion.8), channel_id=1, source_target_pairs={{0,2},{1,3},{2,0},{3,1},{4,6},{5,7},{6,4},{7,5},{8,10},{9,11},{10,... | collective-permute-start | bytes 3686408 | tf_op jit(solution)/shard_map/ppermute | solution.py:722
  325.1 30.1 %collective-permute-start.30 = (bf16[2,2,1,208,960]{4,3,2,1,0:T(8,128)(2,1)S(1)}, bf16[2,2,1,208,960]{4,3,2,1,0:T(8,128)(2,1)S(1)}, u32[]{:S(2)}, u32[]{:S(2)}) collective-permute-start(bf16[2,2,1,208,960]{4,3,2,1,0:T(8,128)(2,1)S(1)} %constant_dynamic-slice_fusion.5), channel_id=1, source_target_pairs={{0,1},{1,0},{2,3},{3,2},{4,5},{5,4},{6,7},{7,6},{8,9},{9,8},{10,11... | collective-permute-start | bytes 4792328 | tf_op jit(solution)/shard_map/ppermute | solution.py:722
  358.8 29.7 %collective-permute-start.31 = (bf16[2,1,1,208,960]{4,3,2,1,0:T(8,128)(2,1)}, bf16[2,1,1,208,960]{4,3,2,1,0:T(8,128)(2,1)}, u32[]{:S(2)}, u32[]{:S(2)}) collective-permute-start(bf16[2,1,1,208,960]{4,3,2,1,0:T(8,128)(2,1)} %constant_dynamic-slice_fusion.3), channel_id=1, source_target_pairs={{0,2},{1,3},{2,0},{3,1},{4,6},{5,7},{6,4},{7,5},{8,10},{9,11},{10,... | collective-permute-start | bytes 2396168 | tf_op jit(solution)/shard_map/ppermute | solution.py:722
  360.2 31.8 %collective-permute-start.29 = (bf16[2,2,1,112,960]{4,3,2,1,0:T(8,128)(2,1)}, bf16[2,2,1,112,960]{4,3,2,1,0:T(8,128)(2,1)}, u32[]{:S(2)}, u32[]{:S(2)}) collective-permute-start(bf16[2,2,1,112,960]{4,3,2,1,0:T(8,128)(2,1)} %constant_dynamic-slice_fusion.6), channel_id=1, source_target_pairs={{0,1},{1,0},{2,3},{3,2},{4,5},{5,4},{6,7},{7,6},{8,9},{9,8},{10,11... | collective-permute-start | bytes 2580488 | tf_op jit(solution)/shard_map/ppermute | solution.py:722
  361.7 36.0 %collective-permute-start.27 = (bf16[1,1,1,120,1600]{4,3,2,1,0:T(8,128)(2,1)S(1)}, bf16[1,1,1,120,1600]{4,3,2,1,0:T(8,128)(2,1)S(1)}, u32[]{:S(2)}, u32[]{:S(2)}) collective-permute-start(bf16[1,1,1,120,1600]{4,3,2,1,0:T(8,128)(2,1)S(1)} %constant_dynamic-slice_fusion.7), channel_id=1, source_target_pairs={{0,1},{1,0},{2,3},{3,2},{4,5},{5,4},{6,7},{7,6},{8,9},{9,8},{10,11... | collective-permute-start | bytes 1152008 | tf_op jit(solution)/shard_map/ppermute | solution.py:722
  362.3 35.6 %collective-permute-start.26 = (bf16[1,1,1,120,962]{4,3,2,1,0:T(8,128)(2,1)}, bf16[1,1,1,120,962]{4,3,2,1,0:T(8,128)(2,1)S(1)}, u32[]{:S(2)}, u32[]{:S(2)}) collective-permute-start(bf16[1,1,1,120,962]{4,3,2,1,0:T(8,128)(2,1)} %constant_dynamic-slice_fusion.9), channel_id=1, source_target_pairs={{0,1},{1,0},{2,3},{3,2},{4,5},{5,4},{6,7},{7,6},{8,9},{9,8},{10,11... | collective-permute-start | bytes 692648 | tf_op jit(solution)/shard_map/ppermute | solution.py:722
  363.7 32.9 %collective-permute-start.28 = (bf16[1,1,1,120,2560]{4,3,2,1,0:T(8,128)(2,1)}, bf16[1,1,1,120,2560]{4,3,2,1,0:T(8,128)(2,1)S(1)}, u32[]{:S(2)}, u32[]{:S(2)}) collective-permute-start(bf16[1,1,1,120,2560]{4,3,2,1,0:T(8,128)(2,1)} %constant_dynamic-slice_fusion.4), channel_id=1, source_target_pairs={{0,4},{1,5},{2,6},{3,7},{4,0},{5,1},{6,2},{7,3},{8,12},{9,13},{10,... | collective-permute-start | bytes 1843208 | tf_op jit(solution)/shard_map/ppermute | solution.py:722
  390.8 18.9 %collective-permute-start.35 = (bf16[1,1,1,208,960]{4,3,2,1,0:T(8,128)(2,1)}, bf16[1,1,1,208,960]{4,3,2,1,0:T(8,128)(2,1)}, u32[]{:S(2)}, u32[]{:S(2)}) collective-permute-start(bf16[1,1,1,208,960]{4,3,2,1,0:T(8,128)(2,1)} %constant_dynamic-slice_fusion.2), channel_id=1, source_target_pairs={{0,4},{1,5},{2,6},{3,7},{4,0},{5,1},{6,2},{7,3},{8,12},{9,13},{10,... | collective-permute-start | bytes 1198088 | tf_op jit(solution)/shard_map/ppermute | solution.py:722
  394.1 17.1 %collective-permute-start.36 = (bf16[2,1,1,112,960]{4,3,2,1,0:T(8,128)(2,1)}, bf16[2,1,1,112,960]{4,3,2,1,0:T(8,128)(2,1)}, u32[]{:S(2)}, u32[]{:S(2)}) collective-permute-start(bf16[2,1,1,112,960]{4,3,2,1,0:T(8,128)(2,1)} %constant_dynamic-slice_fusion.1), channel_id=1, source_target_pairs={{0,2},{1,3},{2,0},{3,1},{4,6},{5,7},{6,4},{7,5},{8,10},{9,11},{10,... | collective-permute-start | bytes 1290248 | tf_op jit(solution)/shard_map/ppermute | solution.py:722
  399.0 13.4 %collective-permute-start.32 = (bf16[320,240]{1,0:T(8,128)(2,1)}, bf16[320,240]{1,0:T(8,128)(2,1)}, u32[]{:S(2)}, u32[]{:S(2)}) collective-permute-start(bf16[320,240]{1,0:T(8,128)(2,1)} %get-tuple-element.511), channel_id=1, source_target_pairs={{24,16},{0,8},{25,17},{1,9},{26,18},{2,10},{27,19},{3,11},{28,20},... | collective-permute-start | bytes 460808 | tf_op jit(solution)/shard_map/ppermute | solution.py:689
  401.1 11.3 %collective-permute-start.33 = (bf16[320,240]{1,0:T(8,128)(2,1)}, bf16[320,240]{1,0:T(8,128)(2,1)}, u32[]{:S(2)}, u32[]{:S(2)}) collective-permute-start(bf16[320,240]{1,0:T(8,128)(2,1)} %get-tuple-element.510), channel_id=1, source_target_pairs={{24,8},{0,16},{25,9},{1,17},{26,10},{2,18},{27,11},{3,19},{28,12},... | collective-permute-start | bytes 460808 | tf_op jit(solution)/shard_map/ppermute | solution.py:689
  403.0 9.4 %collective-permute-start.34 = (bf16[320,240]{1,0:T(8,128)(2,1)}, bf16[320,240]{1,0:T(8,128)(2,1)}, u32[]{:S(2)}, u32[]{:S(2)}) collective-permute-start(bf16[320,240]{1,0:T(8,128)(2,1)} %get-tuple-element.509), channel_id=1, source_target_pairs={{24,0},{0,24},{25,1},{1,25},{26,2},{2,26},{27,3},{3,27},{28,4},{4,... | collective-permute-start | bytes 460808 | tf_op jit(solution)/shard_map/ppermute | solution.py:689
  412.3 10.4 %collective-permute-start.37 = (bf16[1,1,1,112,960]{4,3,2,1,0:T(8,128)(2,1)S(1)}, bf16[1,1,1,112,960]{4,3,2,1,0:T(8,128)(2,1)S(1)}, u32[]{:S(2)}, u32[]{:S(2)}) collective-permute-start(bf16[1,1,1,112,960]{4,3,2,1,0:T(8,128)(2,1)S(1)} %constant_dynamic-slice_fusion), channel_id=1, source_target_pairs={{0,4},{1,5},{2,6},{3,7},{4,0},{5,1},{6,2},{7,3},{8,12},{9,13},{10,... | collective-permute-start | bytes 645128 | tf_op jit(solution)/shard_map/ppermute | solution.py:722
  (35 other events, 280.2 us)

commit v6 on v5

--- a/solution.py
+++ b/solution.py
@@ -412,9 +412,13 @@
             score_grad = (weighted - probs_wide * shared).astype(BF16)
             pulled = dot(score_grad, keys[kv])
             query_grads += [pulled[i * rows : (i + 1) * rows] for i in range(share)]
-            pulled = dot_rows(score_grad, grouped)[:rows]
+            both = dot_rows(
+                jnp.concatenate([score_grad, probs], axis=1),
+                jnp.concatenate([grouped, mixed], axis=1),
+            )
+            pulled = both[:rows, :LANES]
             key_grads.append(pulled + pltpu.roll(pulled, HEAD_DIM, 1))
-            pulled = dot_rows(probs, mixed)[:rows]
+            pulled = both[chunk : chunk + rows, LANES:]
             value_grads.append(pulled + pltpu.roll(pulled, HEAD_DIM, 1))
 
         parts = query_grads + key_grads + value_grads

time: 432 us -> 432 us (level)
  transfers between devices with their start and end apart: 38 -> 38, of which waited for: 15 -> 14; matrix products, arithmetic and copies ran while one was open for 11% -> 11% of each run, Pallas kernels for 27% -> 27%
where the time goes in v6:
time: 432 us; the launch traced here: 424 us
  waiting for transfers between devices  161 us (37%)
  Pallas kernels  144 us (33%)
  starting transfers between devices  55.1 us (13%)
  matrix products  21.3 us (5%)
  other arithmetic  20.7 us (5%)
  local copies, waits for them, and re-layouts  19 us (4%)
    pallas_call x18, Pallas kernels, run_tick(): pl.pallas_call(functools.partial(kernel, sizes), out_shape=outs, grid_spe...  134 us
    ppermute x18, waiting for transfers between devices, send(): lax.ppermute(sent, 'dp', [(i, i ^ 1 << bit) for i in range(devices)])  127 us
    ppermute x14, waiting for transfers between devices, per_device(): sent[tick] = lax.ppermute(rounded, 'pipe', route)  34 us
    ppermute x18, starting transfers between devices, send(): lax.ppermute(sent, 'dp', [(i, i ^ 1 << bit) for i in range(devices)])  28.9 us
    dot_general x5, matrix products, dot_rows(): lax.dot_general(left, right, (((0,), (0,)), ((), ())), preferred_element_...  21.3 us
    ppermute x14, starting transfers between devices, per_device(): sent[tick] = lax.ppermute(rounded, 'pipe', route)  13.2 us
    add x13, other arithmetic, take(): self.value = lax.dynamic_index_in_dim(self.value, mine, axis) + got  11 us
    dynamic_slice x18, local copies, waits for them, and re-layouts, send(): sent = lax.dynamic_index_in_dim(self.value, 1 - mine, axis)  10.1 us
  transfers between devices with their start and end apart: 38, of which 14 were waited for; matrix products, arithmetic and copies ran while one was open for 11% of the time, Pallas kernels for 27%

profile of v6, /device:TPU:0, one launch (start us, length us, event | category | flops | bytes accessed | tf_op | source)
XLA Modules:
  0.0 423.8 jit_solution(17969704483808052437)
XLA Ops:
  4.3 4.3 %collective-permute-start.2 = (bf16[320,240]{1,0:T(8,128)(2,1)S(1)}, bf16[320,240]{1,0:T(8,128)(2,1)S(1)}, u32[]{:S(2)}, u32[]{:S(2)}) collective-permute-start(bf16[320,240]{1,0:T(8,128)(2,1)S(1)} %get-tuple-element.516), channel_id=1, source_target_pairs={{24,0},{0,24},{25,1},{1,25},{26,2},{2,26},{27,3},{3,27},{28,4},{4,... | collective-permute-start | bytes 460808 | tf_op jit(solution)/shard_map/ppermute | solution.py:670
  8.6 7.0 %load_weights.1 = (bf16[1600,960]{1,0:T(8,128)(2,1)S(1)}, bf16[960,1600]{1,0:T(8,128)(2,1)S(1)}, bf16[960,960]{1,0:T(8,128)(2,1)S(1)}, bf16[960,2560]{1,0:T(8,12...) custom-call(bf16[320,960]{1,0:T(8,128)(2,1)} %bitcast.83, ...), custom_call_target="tpu_custom_call" | custom-call | tf_op jit(solution)/shard_map/load_weights/pallas_call | solution.py:539
  16.3 11.3 %layer_pair_forward.9 = (bf16[128,960]{1,0:T(8,128)(2,1)S(1)}, bf16[320,960]{1,0:T(8,128)(2,1)S(1)}, f32[2,320,960]{2,1,0:T(8,128)}, bf16[2,320,960]{2,1,0:T(8,1...) custom-call(s32[1,4]{1,0:T(1,128)S(1)} %copy-done.3, ...), custom_call_target="tpu_custom_call" | custom-call | flops 5033164800 | bytes 19660800 | tf_op jit(solution)/shard_map/layer_pair_forward/pallas_call | solution.py:616
  28.9 11.6 %layer_pair_forward.10 = (bf16[128,960]{1,0:T(8,128)(2,1)S(1)}, bf16[320,960]{1,0:T(8,128)(2,1)S(1)}, f32[2,320,960]{2,1,0:T(8,128)}, bf16[2,320,960]{2,1,0:T(8,...) custom-call(s32[1,4]{1,0:T(1,128)S(1)} %copy-done.3, ...), custom_call_target="tpu_custom_call", output_to_operand_aliasing={{1}: (14, {}), {2}: (15, {}), {3}: (16, {}), {4}: (17, {}),... | custom-call | flops 5033164800 | bytes 19660800 | tf_op jit(solution)/shard_map/layer_pair_forward/pallas_call | solution.py:616
  41.9 10.9 %layer_pair_forward.11 = (bf16[128,960]{1,0:T(8,128)(2,1)S(1)}, bf16[320,960]{1,0:T(8,128)(2,1)S(1)}, f32[2,320,960]{2,1,0:T(8,128)}, bf16[2,320,960]{2,1,0:T(8,...) custom-call(s32[1,4]{1,0:T(1,128)S(1)} %copy-done.3, ...), custom_call_target="tpu_custom_call", output_to_operand_aliasing={{1}: (15, {}), {2}: (16, {}), {3}: (17, {}), {4}: (18, {}),... | custom-call | flops 5033164800 | bytes 19660800 | tf_op jit(solution)/shard_map/layer_pair_forward/pallas_call | solution.py:616
  54.1 9.1 %layer_pair_forward.12 = (bf16[128,960]{1,0:T(8,128)(2,1)S(1)}, bf16[320,960]{1,0:T(8,128)(2,1)S(1)}, f32[2,320,960]{2,1,0:T(8,128)}, bf16[2,320,960]{2,1,0:T(8,...) custom-call(s32[1,4]{1,0:T(1,128)S(1)} %copy-done.3, ...), custom_call_target="tpu_custom_call", output_to_operand_aliasing={{1}: (11, {}), {2}: (12, {}), {3}: (13, {}), {4}: (14, {}),... | custom-call | flops 5033164800 | bytes 19660800 | tf_op jit(solution)/shard_map/layer_pair_forward/pallas_call | solution.py:616
  63.9 3.4 turn_weights.3
  68.9 7.4 %layer_pair_forward.14 = (bf16[128,960]{1,0:T(8,128)(2,1)S(1)}, bf16[320,960]{1,0:T(8,128)(2,1)S(1)}, f32[2,320,960]{2,1,0:T(8,128)}, bf16[2,320,960]{2,1,0:T(8,...) custom-call(s32[1,4]{1,0:T(1,128)S(1)} %copy-done.3, ...), custom_call_target="tpu_custom_call", output_to_operand_aliasing={{1}: (11, {}), {2}: (12, {}), {3}: (13, {}), {4}: (14, {}),... | custom-call | flops 5033164800 | bytes 19660800 | tf_op jit(solution)/shard_map/layer_pair_forward/pallas_call | solution.py:616
  78.6 8.6 %layer_pair_forward.16 = (bf16[128,960]{1,0:T(8,128)(2,1)}, bf16[320,960]{1,0:T(8,128)(2,1)S(1)}, f32[2,320,960]{2,1,0:T(8,128)}, bf16[2,320,960]{2,1,0:T(8,128)...) custom-call(s32[1,4]{1,0:T(1,128)S(1)} %copy-done.3, ...), custom_call_target="tpu_custom_call", output_to_operand_aliasing={{1}: (11, {}), {2}: (12, {}), {3}: (13, {}), {4}: (14, {}),... | custom-call | flops 5033164800 | bytes 19660800 | tf_op jit(solution)/shard_map/layer_pair_forward/pallas_call | solution.py:616
  90.5 8.3 %layer_pair_backward.10 = (bf16[128,960]{1,0:T(8,128)(2,1)S(1)}, bf16[320,960]{1,0:T(8,128)(2,1)S(1)}, bf16[2,320,960]{2,1,0:T(8,128)(2,1)}, bf16[2,320,2560]{2,...) custom-call(s32[1,4]{1,0:T(1,128)S(1)} %copy-done.3, ...), custom_call_target="tpu_custom_call", output_to_operand_aliasing={{1}: (19, {}), {2}: (20, {}), {3}: (21, {}), {4}: (22, {}),... | custom-call | flops 5033164800 | bytes 19660800 | tf_op jit(solution)/shard_map/layer_pair_backward/pallas_call | solution.py:616
  101.1 8.5 %layer_pair_backward.12 = (bf16[128,960]{1,0:T(8,128)(2,1)S(1)}, bf16[320,960]{1,0:T(8,128)(2,1)S(1)}, bf16[2,320,960]{2,1,0:T(8,128)(2,1)}, bf16[2,320,2560]{2,...) custom-call(s32[1,4]{1,0:T(1,128)S(1)} %copy-done.3, ...), custom_call_target="tpu_custom_call", output_to_operand_aliasing={{1}: (16, {}), {2}: (17, {}), {3}: (18, {}), {4}: (19, {}),... | custom-call | flops 5033164800 | bytes 19660800 | tf_op jit(solution)/shard_map/layer_pair_backward/pallas_call | solution.py:616
  112.5 7.9 %layer_pair_backward.14 = (bf16[128,960]{1,0:T(8,128)(2,1)S(1)}, bf16[320,960]{1,0:T(8,128)(2,1)S(1)}, bf16[2,320,960]{2,1,0:T(8,128)(2,1)}, bf16[2,320,2560]{2,...) custom-call(s32[1,4]{1,0:T(1,128)S(1)} %copy-done.3, ...), custom_call_target="tpu_custom_call", output_to_operand_aliasing={{1}: (16, {}), {2}: (17, {}), {3}: (18, {}), {4}: (19, {}),... | custom-call | flops 5033164800 | bytes 19660800 | tf_op jit(solution)/shard_map/layer_pair_backward/pallas_call | solution.py:616
  121.7 33.6 %collective-permute-done.13.refs_4_ = bf16[128,960]{1,0:T(8,128)(2,1)S(1)} collective-permute-done((bf16[128,960]{1,0:T(8,128)(2,1)S(1)}, bf16[128,960]{1,0:T(8,128)(2,1)S(1)}, u32[]{:S(2)}, u32[]{:S(2)}) %collective-permute-start.13) | collective-permute-done | bytes 245792 | tf_op jit(solution)/shard_map/ppermute | solution.py:876
  155.4 14.3 %layer_pair_backward.15 = (bf16[128,960]{1,0:T(8,128)(2,1)S(1)}, bf16[320,960]{1,0:T(8,128)(2,1)S(1)}, bf16[2,320,960]{2,1,0:T(8,128)(2,1)}, bf16[2,320,2560]{2,...) custom-call(s32[1,4]{1,0:T(1,128)S(1)} %copy-done.3, ...), custom_call_target="tpu_custom_call", output_to_operand_aliasing={{1}: (16, {}), {2}: (17, {}), {3}: (18, {}), {4}: (19, {}),... | custom-call | flops 5033164800 | bytes 19660800 | tf_op jit(solution)/shard_map/layer_pair_backward/pallas_call | solution.py:616
  171.2 15.3 %layer_pair_backward.16 = (bf16[128,960]{1,0:T(8,128)(2,1)}, bf16[320,960]{1,0:T(8,128)(2,1)S(1)}, bf16[2,320,960]{2,1,0:T(8,128)(2,1)}, bf16[2,320,2560]{2,1,0:...) custom-call(s32[1,4]{1,0:T(1,128)S(1)} %copy-done.3, ...), custom_call_target="tpu_custom_call", output_to_operand_aliasing={{1}: (16, {}), {2}: (17, {}), {3}: (18, {}), {4}: (19, {}),... | custom-call | flops 5033164800 | bytes 19660800 | tf_op jit(solution)/shard_map/layer_pair_backward/pallas_call | solution.py:616
  186.6 14.7 %layer_pair_backward.17 = (bf16[128,960]{1,0:T(8,128)(2,1)}, bf16[320,960]{1,0:T(8,128)(2,1)S(1)}, bf16[2,320,960]{2,1,0:T(8,128)(2,1)}, bf16[2,320,2560]{2,1,0:...) custom-call(s32[1,4]{1,0:T(1,128)S(1)} %copy-done.3, ...), custom_call_target="tpu_custom_call", output_to_operand_aliasing={{1}: (16, {}), {2}: (17, {}), {3}: (18, {}), {4}: (19, {}),... | custom-call | flops 5033164800 | bytes 19660800 | tf_op jit(solution)/shard_map/layer_pair_backward/pallas_call | solution.py:616
  201.4 4.6 %bitcast_convert_fusion.3 = bf16[960,1600]{1,0:T(8,128)(2,1)S(1)} fusion(bf16[2,320,960]{2,1,0:T(8,128)(2,1)S(1)} %copy-done.7, bf16[2,320,1600]{2,1,0:T(8,128)(2,1)} %get-tuple-element.427), kind=kOutput, calls=%fused_computation.3 | convolution fusion | flops 1967616000 | bytes 6348800 | tf_op jit(solution)/shard_map/dot_general | solution.py:44
  208.9 4.5 %bitcast_convert_fusion.2 = bf16[960,2560]{1,0:T(8,128)(2,1)S(1)} fusion(bf16[2,320,960]{2,1,0:T(8,128)(2,1)S(1)} %copy-done.9, bf16[2,320,2560]{2,1,0:T(8,128)(2,1)S(1)} %copy-done.5), kind=kOutput, calls=%fused_computation.2 | convolution fusion | flops 3148185600 | bytes 9420800 | tf_op jit(solution)/shard_map/dot_general | solution.py:44
  218.2 3.1 bitcast_convert_fusion.4
  224.6 29.5 %collective-permute-done.19 = bf16[2,1,2,120,1600]{4,3,2,1,0:T(8,128)(2,1)} collective-permute-done((bf16[2,1,2,120,1600]{4,3,2,1,0:T(8,128)(2,1)}, bf16[2,1,2,120,1600]{4,3,2,1,0:T(8,128)(2,1)}, u32[]{:S(2)}, u32[]{:S(2)}) %collective-permute-start.19) | collective-permute-done | bytes 1536032 | tf_op jit(solution)/shard_map/ppermute | solution.py:726
  257.5 4.3 %bitcast_convert_fusion.1 = bf16[960,2560]{1,0:T(8,128)(2,1)S(1)} fusion(bf16[2,320,960]{2,1,0:T(8,128)(2,1)S(1)} %copy-done.9, bf16[2,320,2560]{2,1,0:T(8,128)(2,1)S(1)} %copy-done.6), kind=kOutput, calls=%fused_computation.1 | convolution fusion | flops 3148185600 | bytes 9420800 | tf_op jit(solution)/shard_map/dot_general | solution.py:44
  263.6 9.8 %collective-permute-done.18 = bf16[2,2,1,120,2560]{4,3,2,1,0:T(8,128)(2,1)} collective-permute-done((bf16[2,2,1,120,2560]{4,3,2,1,0:T(8,128)(2,1)}, bf16[2,2,1,120,2560]{4,3,2,1,0:T(8,128)(2,1)}, u32[]{:S(2)}, u32[]{:S(2)}) %collective-permute-start.18) | collective-permute-done | bytes 2457632 | tf_op jit(solution)/shard_map/ppermute | solution.py:726
  277.0 4.8 %bitcast_convert_fusion = bf16[2560,960]{1,0:T(8,128)(2,1)S(1)} fusion(bf16[2,320,2560]{2,1,0:T(8,128)(2,1)S(1)} %copy-done.4, bf16[2,320,960]{2,1,0:T(8,128)(2,1)S(1)} %copy-done.10), kind=kOutput, calls=%fused_computation | convolution fusion | flops 3148185600 | bytes 9420800 | tf_op jit(solution)/shard_map/dot_general | solution.py:44
  284.6 4.2 collective-permute-start.20
  288.9 23.9 %collective-permute-done.21 = bf16[2,1,1,120,2560]{4,3,2,1,0:T(8,128)(2,1)S(1)} collective-permute-done((bf16[2,1,1,120,2560]{4,3,2,1,0:T(8,128)(2,1)S(1)}, bf16[2,1,1,120,2560]{4,3,2,1,0:T(8,128)(2,1)S(1)}, u32[]{:S(2)}, u32[]{:S(2)}) %collective-permute-start.21) | collective-permute-done | bytes 1228832 | tf_op jit(solution)/shard_map/ppermute | solution.py:726
  314.9 4.8 %collective-permute-done.23 = bf16[2,2,1,120,2560]{4,3,2,1,0:T(8,128)(2,1)S(1)} collective-permute-done((bf16[2,2,1,120,2560]{4,3,2,1,0:T(8,128)(2,1)S(1)}, bf16[2,2,1,120,2560]{4,3,2,1,0:T(8,128)(2,1)S(1)}, u32[]{:S(2)}, u32[]{:S(2)}) %collective-permute-start.23) | collective-permute-done | bytes 2457632 | tf_op jit(solution)/shard_map/ppermute | solution.py:726
  325.3 15.9 %collective-permute-done.25 = bf16[1,1,1,120,2560]{4,3,2,1,0:T(8,128)(2,1)S(1)} collective-permute-done((bf16[1,1,1,120,2560]{4,3,2,1,0:T(8,128)(2,1)S(1)}, bf16[1,1,1,120,2560]{4,3,2,1,0:T(8,128)(2,1)S(1)}, u32[]{:S(2)}, u32[]{:S(2)}) %collective-permute-start.25) | collective-permute-done | bytes 614432 | tf_op jit(solution)/shard_map/ppermute | solution.py:726
  342.3 10.1 %collective-permute-done.24 = bf16[2,1,1,120,2560]{4,3,2,1,0:T(8,128)(2,1)S(1)} collective-permute-done((bf16[2,1,1,120,2560]{4,3,2,1,0:T(8,128)(2,1)S(1)}, bf16[2,1,1,120,2560]{4,3,2,1,0:T(8,128)(2,1)S(1)}, u32[]{:S(2)}, u32[]{:S(2)}) %collective-permute-start.24) | collective-permute-done | bytes 1228832 | tf_op jit(solution)/shard_map/ppermute | solution.py:726
  362.9 2.7 collective-permute-start.28
  365.7 22.4 %collective-permute-done.31 = bf16[2,1,1,208,960]{4,3,2,1,0:T(8,128)(2,1)} collective-permute-done((bf16[2,1,1,208,960]{4,3,2,1,0:T(8,128)(2,1)}, bf16[2,1,1,208,960]{4,3,2,1,0:T(8,128)(2,1)}, u32[]{:S(2)}, u32[]{:S(2)}) %collective-permute-start.31) | collective-permute-done | bytes 798752 | tf_op jit(solution)/shard_map/ppermute | solution.py:726
  393.7 2.5 collective-permute-start.36
  414.1 8.3 %collective-permute-done.37 = bf16[1,1,1,112,960]{4,3,2,1,0:T(8,128)(2,1)S(1)} collective-permute-done((bf16[1,1,1,112,960]{4,3,2,1,0:T(8,128)(2,1)S(1)}, bf16[1,1,1,112,960]{4,3,2,1,0:T(8,128)(2,1)S(1)}, u32[]{:S(2)}, u32[]{:S(2)}) %collective-permute-start.37) | collective-permute-done | bytes 215072 | tf_op jit(solution)/shard_map/ppermute | solution.py:726
  (179 shorter events, 90.4 us)
Async XLA Ops:
  1.7 14.0 %collective-permute-start = (bf16[320,240]{1,0:T(8,128)(2,1)S(1)}, bf16[320,240]{1,0:T(8,128)(2,1)S(1)}, u32[]{:S(2)}, u32[]{:S(2)}) collective-permute-start(bf16[320,240]{1,0:T(8,128)(2,1)S(1)} %get-tuple-element.518), channel_id=1, source_target_pairs={{8,0},{16,24},{9,1},{17,25},{10,2},{18,26},{11,3},{19,27},{12,4},{... | collective-permute-start | bytes 460808 | tf_op jit(solution)/shard_map/ppermute | solution.py:670
  3.0 12.7 %collective-permute-start.1 = (bf16[320,240]{1,0:T(8,128)(2,1)S(1)}, bf16[320,240]{1,0:T(8,128)(2,1)S(1)}, u32[]{:S(2)}, u32[]{:S(2)}) collective-permute-start(bf16[320,240]{1,0:T(8,128)(2,1)S(1)} %get-tuple-element.517), channel_id=1, source_target_pairs={{16,0},{8,24},{17,1},{9,25},{18,2},{10,26},{19,3},{11,27},{20,4},{... | collective-permute-start | bytes 460808 | tf_op jit(solution)/shard_map/ppermute | solution.py:670
  4.3 11.4 %collective-permute-start.2 = (bf16[320,240]{1,0:T(8,128)(2,1)S(1)}, bf16[320,240]{1,0:T(8,128)(2,1)S(1)}, u32[]{:S(2)}, u32[]{:S(2)}) collective-permute-start(bf16[320,240]{1,0:T(8,128)(2,1)S(1)} %get-tuple-element.516), channel_id=1, source_target_pairs={{24,0},{0,24},{25,1},{1,25},{26,2},{2,26},{27,3},{3,27},{28,4},{4,... | collective-permute-start | bytes 460808 | tf_op jit(solution)/shard_map/ppermute | solution.py:670
  27.6 14.3 %collective-permute-start.3 = (bf16[128,960]{1,0:T(8,128)(2,1)S(1)}, bf16[128,960]{1,0:T(8,128)(2,1)S(1)}, u32[]{:S(2)}, u32[]{:S(2)}) collective-permute-start(bf16[128,960]{1,0:T(8,128)(2,1)S(1)} %get-tuple-element.254), channel_id=1, source_target_pairs={{0,8},{1,9},{2,10},{3,11},{4,12},{5,13},{6,14},{7,15}} | collective-permute-start | bytes 737288 | tf_op jit(solution)/shard_map/ppermute | solution.py:831
  40.6 13.5 %collective-permute-start.5 = (bf16[128,960]{1,0:T(8,128)(2,1)S(1)}, bf16[128,960]{1,0:T(8,128)(2,1)S(1)}, u32[]{:S(2)}, u32[]{:S(2)}) collective-permute-start(bf16[128,960]{1,0:T(8,128)(2,1)S(1)} %get-tuple-element.276), channel_id=1, source_target_pairs={{0,8},{1,9},{2,10},{3,11},{4,12},{5,13},{6,14},{7,15}} | collective-permute-start | bytes 737288 | tf_op jit(solution)/shard_map/ppermute | solution.py:831
  52.8 14.5 %collective-permute-start.4 = (bf16[128,960]{1,0:T(8,128)(2,1)S(1)}, bf16[128,960]{1,0:T(8,128)(2,1)S(1)}, u32[]{:S(2)}, u32[]{:S(2)}) collective-permute-start(bf16[128,960]{1,0:T(8,128)(2,1)S(1)} %get-tuple-element.275), channel_id=1, source_target_pairs={{0,8},{8,16},{1,9},{9,17},{2,10},{10,18},{3,11},{11,19},{4,12},{12... | collective-permute-start | bytes 737288 | tf_op jit(solution)/shard_map/ppermute | solution.py:831
  89.8 9.6 %collective-permute-start.10 = (bf16[128,960]{1,0:T(8,128)(2,1)S(1)}, bf16[128,960]{1,0:T(8,128)(2,1)S(1)}, u32[]{:S(2)}, u32[]{:S(2)}) collective-permute-start(bf16[128,960]{1,0:T(8,128)(2,1)S(1)} %get-tuple-element.358), channel_id=1, source_target_pairs={{24,16},{25,17},{26,18},{27,19},{28,20},{29,21},{30,22},{31,23}} | collective-permute-start | bytes 737288 | tf_op jit(solution)/shard_map/ppermute | solution.py:876
  100.4 9.9 %collective-permute-start.11 = (bf16[128,960]{1,0:T(8,128)(2,1)S(1)}, bf16[128,960]{1,0:T(8,128)(2,1)S(1)}, u32[]{:S(2)}, u32[]{:S(2)}) collective-permute-start(bf16[128,960]{1,0:T(8,128)(2,1)S(1)} %get-tuple-element.373), channel_id=1, source_target_pairs={{16,8},{24,16},{17,9},{25,17},{18,10},{26,18},{19,11},{27,19},{20,... | collective-permute-start | bytes 737288 | tf_op jit(solution)/shard_map/ppermute | solution.py:876
  111.2 44.2 %collective-permute-start.13 = (bf16[128,960]{1,0:T(8,128)(2,1)S(1)}, bf16[128,960]{1,0:T(8,128)(2,1)S(1)}, u32[]{:S(2)}, u32[]{:S(2)}) collective-permute-start(bf16[128,960]{1,0:T(8,128)(2,1)S(1)} %get-tuple-element.389), channel_id=1, source_target_pairs={{8,0},{16,8},{9,1},{17,9},{10,2},{18,10},{11,3},{19,11},{12,4},{20... | collective-permute-start | bytes 737288 | tf_op jit(solution)/shard_map/ppermute | solution.py:876
  120.4 50.8 %collective-permute-start.16 = (bf16[128,960]{1,0:T(8,128)(2,1)S(1)}, bf16[128,960]{1,0:T(8,128)(2,1)S(1)}, u32[]{:S(2)}, u32[]{:S(2)}) collective-permute-start(bf16[128,960]{1,0:T(8,128)(2,1)S(1)} %get-tuple-element.406), channel_id=1, source_target_pairs={{8,0},{9,1},{10,2},{11,3},{12,4},{13,5},{14,6},{15,7}} | collective-permute-start | bytes 737288 | tf_op jit(solution)/shard_map/ppermute | solution.py:876
  169.7 16.9 %collective-permute-start.15 = (bf16[128,960]{1,0:T(8,128)(2,1)S(1)}, bf16[128,960]{1,0:T(8,128)(2,1)S(1)}, u32[]{:S(2)}, u32[]{:S(2)}) collective-permute-start(bf16[128,960]{1,0:T(8,128)(2,1)S(1)} %get-tuple-element.405), channel_id=1, source_target_pairs={{8,0},{9,1},{10,2},{11,3},{12,4},{13,5},{14,6},{15,7}} | collective-permute-start | bytes 737288 | tf_op jit(solution)/shard_map/ppermute | solution.py:876
  207.3 46.7 %collective-permute-start.19 = (bf16[2,1,2,120,1600]{4,3,2,1,0:T(8,128)(2,1)}, bf16[2,1,2,120,1600]{4,3,2,1,0:T(8,128)(2,1)}, u32[]{:S(2)}, u32[]{:S(2)}) collective-permute-start(bf16[2,1,2,120,1600]{4,3,2,1,0:T(8,128)(2,1)} %constant_dynamic-slice_fusion.17), channel_id=1, source_target_pairs={{0,2},{1,3},{2,0},{3,1},{4,6},{5,7},{6,4},{7,5},{8,10},{9,11},{10,... | collective-permute-start | bytes 4608008 | tf_op jit(solution)/shard_map/ppermute | solution.py:726
  216.7 56.6 %collective-permute-start.18 = (bf16[2,2,1,120,2560]{4,3,2,1,0:T(8,128)(2,1)}, bf16[2,2,1,120,2560]{4,3,2,1,0:T(8,128)(2,1)}, u32[]{:S(2)}, u32[]{:S(2)}) collective-permute-start(bf16[2,2,1,120,2560]{4,3,2,1,0:T(8,128)(2,1)} %constant_dynamic-slice_fusion.16), channel_id=1, source_target_pairs={{0,1},{1,0},{2,3},{3,2},{4,5},{5,4},{6,7},{7,6},{8,9},{9,8},{10,11... | collective-permute-start | bytes 7372808 | tf_op jit(solution)/shard_map/ppermute | solution.py:726
  223.6 60.8 %collective-permute-start.17 = (bf16[2,1,2,120,962]{4,3,2,1,0:T(8,128)(2,1)S(1)}, bf16[2,1,2,120,962]{4,3,2,1,0:T(8,128)(2,1)S(1)}, u32[]{:S(2)}, u32[]{:S(2)}) collective-permute-start(bf16[2,1,2,120,962]{4,3,2,1,0:T(8,128)(2,1)S(1)} %constant_dynamic-slice_fusion.15), channel_id=1, source_target_pairs={{0,2},{1,3},{2,0},{3,1},{4,6},{5,7},{6,4},{7,5},{8,10},{9,11},{10,... | collective-permute-start | bytes 2770568 | tf_op jit(solution)/shard_map/ppermute | solution.py:726
  255.8 33.0 %collective-permute-start.22 = (bf16[1,1,2,120,1600]{4,3,2,1,0:T(8,128)(2,1)S(1)}, bf16[1,1,2,120,1600]{4,3,2,1,0:T(8,128)(2,1)S(1)}, u32[]{:S(2)}, u32[]{:S(2)}) collective-permute-start(bf16[1,1,2,120,1600]{4,3,2,1,0:T(8,128)(2,1)S(1)} %constant_dynamic-slice_fusion.14), channel_id=1, source_target_pairs={{0,4},{1,5},{2,6},{3,7},{4,0},{5,1},{6,2},{7,3},{8,12},{9,13},{10,... | collective-permute-start | bytes 2304008 | tf_op jit(solution)/shard_map/ppermute | solution.py:726
  262.0 57.6 %collective-permute-start.23 = (bf16[2,2,1,120,2560]{4,3,2,1,0:T(8,128)(2,1)S(1)}, bf16[2,2,1,120,2560]{4,3,2,1,0:T(8,128)(2,1)S(1)}, u32[]{:S(2)}, u32[]{:S(2)}) collective-permute-start(bf16[2,2,1,120,2560]{4,3,2,1,0:T(8,128)(2,1)S(1)} %constant_dynamic-slice_fusion.13), channel_id=1, source_target_pairs={{0,1},{1,0},{2,3},{3,2},{4,5},{5,4},{6,7},{7,6},{8,9},{9,8},{10,11... | collective-permute-start | bytes 7372808 | tf_op jit(solution)/shard_map/ppermute | solution.py:726
  275.7 37.2 %collective-permute-start.21 = (bf16[2,1,1,120,2560]{4,3,2,1,0:T(8,128)(2,1)S(1)}, bf16[2,1,1,120,2560]{4,3,2,1,0:T(8,128)(2,1)S(1)}, u32[]{:S(2)}, u32[]{:S(2)}) collective-permute-start(bf16[2,1,1,120,2560]{4,3,2,1,0:T(8,128)(2,1)S(1)} %constant_dynamic-slice_fusion.12), channel_id=1, source_target_pairs={{0,2},{1,3},{2,0},{3,1},{4,6},{5,7},{6,4},{7,5},{8,10},{9,11},{10,... | collective-permute-start | bytes 3686408 | tf_op jit(solution)/shard_map/ppermute | solution.py:726
  284.6 30.2 %collective-permute-start.20 = (bf16[1,1,2,120,962]{4,3,2,1,0:T(8,128)(2,1)S(1)}, bf16[1,1,2,120,962]{4,3,2,1,0:T(8,128)(2,1)S(1)}, u32[]{:S(2)}, u32[]{:S(2)}) collective-permute-start(bf16[1,1,2,120,962]{4,3,2,1,0:T(8,128)(2,1)S(1)} %constant_dynamic-slice_fusion.11), channel_id=1, source_target_pairs={{0,4},{1,5},{2,6},{3,7},{4,0},{5,1},{6,2},{7,3},{8,12},{9,13},{10,... | collective-permute-start | bytes 1385288 | tf_op jit(solution)/shard_map/ppermute | solution.py:726
  313.1 28.1 %collective-permute-start.25 = (bf16[1,1,1,120,2560]{4,3,2,1,0:T(8,128)(2,1)S(1)}, bf16[1,1,1,120,2560]{4,3,2,1,0:T(8,128)(2,1)S(1)}, u32[]{:S(2)}, u32[]{:S(2)}) collective-permute-start(bf16[1,1,1,120,2560]{4,3,2,1,0:T(8,128)(2,1)S(1)} %constant_dynamic-slice_fusion.10), channel_id=1, source_target_pairs={{0,4},{1,5},{2,6},{3,7},{4,0},{5,1},{6,2},{7,3},{8,12},{9,13},{10,... | collective-permute-start | bytes 1843208 | tf_op jit(solution)/shard_map/ppermute | solution.py:726
  320.0 32.4 %collective-permute-start.24 = (bf16[2,1,1,120,2560]{4,3,2,1,0:T(8,128)(2,1)S(1)}, bf16[2,1,1,120,2560]{4,3,2,1,0:T(8,128)(2,1)S(1)}, u32[]{:S(2)}, u32[]{:S(2)}) collective-permute-start(bf16[2,1,1,120,2560]{4,3,2,1,0:T(8,128)(2,1)S(1)} %constant_dynamic-slice_fusion.8), channel_id=1, source_target_pairs={{0,2},{1,3},{2,0},{3,1},{4,6},{5,7},{6,4},{7,5},{8,10},{9,11},{10,... | collective-permute-start | bytes 3686408 | tf_op jit(solution)/shard_map/ppermute | solution.py:726
  323.8 30.7 %collective-permute-start.30 = (bf16[2,2,1,208,960]{4,3,2,1,0:T(8,128)(2,1)S(1)}, bf16[2,2,1,208,960]{4,3,2,1,0:T(8,128)(2,1)S(1)}, u32[]{:S(2)}, u32[]{:S(2)}) collective-permute-start(bf16[2,2,1,208,960]{4,3,2,1,0:T(8,128)(2,1)S(1)} %constant_dynamic-slice_fusion.5), channel_id=1, source_target_pairs={{0,1},{1,0},{2,3},{3,2},{4,5},{5,4},{6,7},{7,6},{8,9},{9,8},{10,11... | collective-permute-start | bytes 4792328 | tf_op jit(solution)/shard_map/ppermute | solution.py:726
  358.0 30.1 %collective-permute-start.31 = (bf16[2,1,1,208,960]{4,3,2,1,0:T(8,128)(2,1)}, bf16[2,1,1,208,960]{4,3,2,1,0:T(8,128)(2,1)}, u32[]{:S(2)}, u32[]{:S(2)}) collective-permute-start(bf16[2,1,1,208,960]{4,3,2,1,0:T(8,128)(2,1)} %constant_dynamic-slice_fusion.3), channel_id=1, source_target_pairs={{0,2},{1,3},{2,0},{3,1},{4,6},{5,7},{6,4},{7,5},{8,10},{9,11},{10,... | collective-permute-start | bytes 2396168 | tf_op jit(solution)/shard_map/ppermute | solution.py:726
  359.4 32.2 %collective-permute-start.29 = (bf16[2,2,1,112,960]{4,3,2,1,0:T(8,128)(2,1)}, bf16[2,2,1,112,960]{4,3,2,1,0:T(8,128)(2,1)}, u32[]{:S(2)}, u32[]{:S(2)}) collective-permute-start(bf16[2,2,1,112,960]{4,3,2,1,0:T(8,128)(2,1)} %constant_dynamic-slice_fusion.6), channel_id=1, source_target_pairs={{0,1},{1,0},{2,3},{3,2},{4,5},{5,4},{6,7},{7,6},{8,9},{9,8},{10,11... | collective-permute-start | bytes 2580488 | tf_op jit(solution)/shard_map/ppermute | solution.py:726
  360.9 36.4 %collective-permute-start.27 = (bf16[1,1,1,120,1600]{4,3,2,1,0:T(8,128)(2,1)S(1)}, bf16[1,1,1,120,1600]{4,3,2,1,0:T(8,128)(2,1)S(1)}, u32[]{:S(2)}, u32[]{:S(2)}) collective-permute-start(bf16[1,1,1,120,1600]{4,3,2,1,0:T(8,128)(2,1)S(1)} %constant_dynamic-slice_fusion.7), channel_id=1, source_target_pairs={{0,1},{1,0},{2,3},{3,2},{4,5},{5,4},{6,7},{7,6},{8,9},{9,8},{10,11... | collective-permute-start | bytes 1152008 | tf_op jit(solution)/shard_map/ppermute | solution.py:726
  361.4 36.0 %collective-permute-start.26 = (bf16[1,1,1,120,962]{4,3,2,1,0:T(8,128)(2,1)}, bf16[1,1,1,120,962]{4,3,2,1,0:T(8,128)(2,1)S(1)}, u32[]{:S(2)}, u32[]{:S(2)}) collective-permute-start(bf16[1,1,1,120,962]{4,3,2,1,0:T(8,128)(2,1)} %constant_dynamic-slice_fusion.9), channel_id=1, source_target_pairs={{0,1},{1,0},{2,3},{3,2},{4,5},{5,4},{6,7},{7,6},{8,9},{9,8},{10,11... | collective-permute-start | bytes 692648 | tf_op jit(solution)/shard_map/ppermute | solution.py:726
  362.9 33.3 %collective-permute-start.28 = (bf16[1,1,1,120,2560]{4,3,2,1,0:T(8,128)(2,1)}, bf16[1,1,1,120,2560]{4,3,2,1,0:T(8,128)(2,1)S(1)}, u32[]{:S(2)}, u32[]{:S(2)}) collective-permute-start(bf16[1,1,1,120,2560]{4,3,2,1,0:T(8,128)(2,1)} %constant_dynamic-slice_fusion.4), channel_id=1, source_target_pairs={{0,4},{1,5},{2,6},{3,7},{4,0},{5,1},{6,2},{7,3},{8,12},{9,13},{10,... | collective-permute-start | bytes 1843208 | tf_op jit(solution)/shard_map/ppermute | solution.py:726
  390.4 18.9 %collective-permute-start.35 = (bf16[1,1,1,208,960]{4,3,2,1,0:T(8,128)(2,1)}, bf16[1,1,1,208,960]{4,3,2,1,0:T(8,128)(2,1)}, u32[]{:S(2)}, u32[]{:S(2)}) collective-permute-start(bf16[1,1,1,208,960]{4,3,2,1,0:T(8,128)(2,1)} %constant_dynamic-slice_fusion.2), channel_id=1, source_target_pairs={{0,4},{1,5},{2,6},{3,7},{4,0},{5,1},{6,2},{7,3},{8,12},{9,13},{10,... | collective-permute-start | bytes 1198088 | tf_op jit(solution)/shard_map/ppermute | solution.py:726
  393.7 17.1 %collective-permute-start.36 = (bf16[2,1,1,112,960]{4,3,2,1,0:T(8,128)(2,1)}, bf16[2,1,1,112,960]{4,3,2,1,0:T(8,128)(2,1)}, u32[]{:S(2)}, u32[]{:S(2)}) collective-permute-start(bf16[2,1,1,112,960]{4,3,2,1,0:T(8,128)(2,1)} %constant_dynamic-slice_fusion.1), channel_id=1, source_target_pairs={{0,2},{1,3},{2,0},{3,1},{4,6},{5,7},{6,4},{7,5},{8,10},{9,11},{10,... | collective-permute-start | bytes 1290248 | tf_op jit(solution)/shard_map/ppermute | solution.py:726
  398.6 13.4 %collective-permute-start.32 = (bf16[320,240]{1,0:T(8,128)(2,1)}, bf16[320,240]{1,0:T(8,128)(2,1)}, u32[]{:S(2)}, u32[]{:S(2)}) collective-permute-start(bf16[320,240]{1,0:T(8,128)(2,1)} %get-tuple-element.511), channel_id=1, source_target_pairs={{24,16},{0,8},{25,17},{1,9},{26,18},{2,10},{27,19},{3,11},{28,20},... | collective-permute-start | bytes 460808 | tf_op jit(solution)/shard_map/ppermute | solution.py:693
  400.7 11.3 %collective-permute-start.33 = (bf16[320,240]{1,0:T(8,128)(2,1)}, bf16[320,240]{1,0:T(8,128)(2,1)}, u32[]{:S(2)}, u32[]{:S(2)}) collective-permute-start(bf16[320,240]{1,0:T(8,128)(2,1)} %get-tuple-element.510), channel_id=1, source_target_pairs={{24,8},{0,16},{25,9},{1,17},{26,10},{2,18},{27,11},{3,19},{28,12},... | collective-permute-start | bytes 460808 | tf_op jit(solution)/shard_map/ppermute | solution.py:693
  402.6 9.4 %collective-permute-start.34 = (bf16[320,240]{1,0:T(8,128)(2,1)}, bf16[320,240]{1,0:T(8,128)(2,1)}, u32[]{:S(2)}, u32[]{:S(2)}) collective-permute-start(bf16[320,240]{1,0:T(8,128)(2,1)} %get-tuple-element.509), channel_id=1, source_target_pairs={{24,0},{0,24},{25,1},{1,25},{26,2},{2,26},{27,3},{3,27},{28,4},{4,... | collective-permute-start | bytes 460808 | tf_op jit(solution)/shard_map/ppermute | solution.py:693
  411.9 10.4 %collective-permute-start.37 = (bf16[1,1,1,112,960]{4,3,2,1,0:T(8,128)(2,1)S(1)}, bf16[1,1,1,112,960]{4,3,2,1,0:T(8,128)(2,1)S(1)}, u32[]{:S(2)}, u32[]{:S(2)}) collective-permute-start(bf16[1,1,1,112,960]{4,3,2,1,0:T(8,128)(2,1)S(1)} %constant_dynamic-slice_fusion), channel_id=1, source_target_pairs={{0,4},{1,5},{2,6},{3,7},{4,0},{5,1},{6,2},{7,3},{8,12},{9,13},{10,... | collective-permute-start | bytes 645128 | tf_op jit(solution)/shard_map/ppermute | solution.py:726
  (35 other events, 278.9 us)
